TPU v7x, 32 devices: a whole 2x2x4 slice. The times are simulated.
32 devices in a mesh: row: 4 (over y, x), col: 8 (over z, core).
Axes of the slice: x: 2, y: 2, z: 4, core: 2. Of those that a mesh axis runs over, the one named last changes fastest.
Arguments:
- returns: bfloat16 [8192, 256], P(('col', 'row')), may hold values from -6 to 6
- start_day: int32 [8192], P(('col', 'row')), may hold values from 0 to 127
- shrink_code: int32 [1], replicated, may hold values from 64 to 191
- weights: bfloat16 [8192, 512], P(('col', 'row')), may hold values from -1.5 to 1.5
Outputs:
- exposures: float32 [8192, 512], P(('col', 'row'))
All inputs are finite; a program needn't handle non-finite values.
Results may differ from a plain program's by a relative error of at most 0.0041.
Values may be sent and summed in bfloat16 or wider, within the bound.
No kernel may reach another device: no remote copies, remote signals or barrier semaphores. Data moves between devices by JAX's collectives and lax.ppermute only.
A program may use at most 128 MiB of HBM per device.

v0:
```python
import jax
import jax.numpy as jnp
from jax import lax
from jax.sharding import PartitionSpec as P

DENOM = 256


def square_bf(values):
    wide = values.astype(jnp.float32)
    return (wide * wide).astype(jnp.bfloat16)


def per_device(returns, start_day, shrink_code, weights):
    own_rows = returns.shape[0]
    num_days = returns.shape[1]
    days = jnp.arange(num_days, dtype=jnp.int32)
    listed = days[None, :] >= start_day[:, None]
    masked = jnp.where(listed, returns, jnp.zeros_like(returns))
    observed = (masked != 0).astype(jnp.bfloat16)
    squared = square_bf(masked)
    counts = jnp.sum(observed.astype(jnp.float32), axis=1)
    sigma = jnp.sqrt(
        jnp.sum(squared.astype(jnp.float32), axis=1) / jnp.maximum(counts, 1.0) + 1e-06
    )
    scaled = (sigma[:, None] * weights.astype(jnp.float32)).astype(jnp.bfloat16)
    delta = shrink_code[0].astype(jnp.float32) / DENOM
    col_y, col_v = (
        lax.all_gather(masked, "row", axis=0, tiled=True),
        lax.all_gather(scaled, "row", axis=0, tiled=True),
    )
    col_obs = (col_y != 0).astype(jnp.bfloat16)
    col_sq = square_bf(col_y)
    row_y = lax.all_gather(masked, "col", axis=0, tiled=True)
    ncol = lax.axis_size("col")
    my_row = lax.axis_index("row")
    my_col = lax.axis_index("col")
    width = col_y.shape[0]
    port_cols = col_v.shape[1]
    col_pos = jnp.arange(width, dtype=jnp.int32)
    local_pos = jnp.arange(own_rows, dtype=jnp.int32)
    diag_ident = (col_pos[None, :] == my_row * own_rows + local_pos[:, None]).astype(jnp.float32)

    def shrink(rows_y, cols_y, cols_obs, cols_sq, ident):
        rows_o = (rows_y != 0).astype(jnp.bfloat16)
        rows_s = square_bf(rows_y)
        cross = jnp.dot(rows_y, cols_y.T, preferred_element_type=jnp.float32)
        left = jnp.dot(rows_s, cols_obs.T, preferred_element_type=jnp.float32)
        right = jnp.dot(rows_o, cols_sq.T, preferred_element_type=jnp.float32)
        corr = cross / jnp.sqrt(left * right + 1e-06)
        return ((1.0 - delta) * corr + delta * ident).astype(jnp.bfloat16)

    def piece_rows(piece):
        return lax.dynamic_slice_in_dim(row_y, piece * own_rows, own_rows, 0)

    def row_term(piece):
        ident = diag_ident * (piece == my_col).astype(jnp.float32)
        shrunk = shrink(piece_rows(piece), col_y, col_obs, col_sq, ident)
        return jnp.dot(shrunk, col_v, preferred_element_type=jnp.float32)

    terms = lax.map(row_term, jnp.arange(ncol, dtype=jnp.int32)).reshape(ncol * own_rows, port_cols)
    row_part = lax.psum_scatter(terms, "col", scatter_dimension=0, tiled=True)
    return sigma[:, None] * row_part


def solution(mesh):
    in_specs = (P(("col", "row"), None), P(("col", "row")), P(), P(("col", "row"), None))
    out_specs = P(("col", "row"), None)
    return jax.shard_map(
        per_device, mesh=mesh, in_specs=in_specs, out_specs=out_specs, check_vma=False
    )
```

profile of v0, /device:TPU:0, one launch (start us, length us, event | category | flops | bytes accessed | tf_op | source)
XLA Modules:
  0.0 180.6 jit_solution(2459196868090963265)
XLA Ops:
  6.5 0.0 all-gather.5.cloned.1.call-start
  6.5 1.7 convert_reduce_fusion
  8.2 1.8 multiply_convert_fusion.4
  10.0 0.0 all-gather.5.cloned.1.call-update
  10.0 0.0 all-gather.3.cloned.1.call-start
  10.1 0.7 all-gather.3.cloned.1.call-update
  10.8 0.0 reduce-scatter.2.cloned.1.call-start
  11.5 12.9 %all_gather.10 = bf16[1024,256]{1,0:T(8,128)(2,1)S(1)} all-gather(bf16[256,256]{1,0:T(8,128)(2,1)} %get-tuple-element.165), channel_id=1, replica_groups=mesh['row'=4,'col'=8] {'row'}, dimensions={0}, use_global_device_ids=true | all-gather | bytes 655360 | tf_op jit(solution)/shard_map/all_gather | solution.py:29
  24.4 0.9 compare_convert_fusion
  25.4 0.1 multiply_convert_fusion.3
  25.5 14.6 %all-gather.5.cloned.1.call-done = bf16[1024,512]{1,0:T(8,128)(2,1)} async-done(((bf16[256,512]{1,0:T(8,128)(2,1)}), bf16[1024,512]{1,0:T(8,128)(2,1)}) %all-gather.5.cloned.1.call-update) | async-done | bytes 1048592 | tf_op jit(solution)/shard_map/all_gather | solution.py:30
  40.1 23.7 %all-gather.3.cloned.1.call-done = bf16[2048,256]{1,0:T(8,128)(2,1)} async-done(((bf16[256,256]{1,0:T(8,128)(2,1)}), bf16[2048,256]{1,0:T(8,128)(2,1)}) %all-gather.3.cloned.1.call-update) | async-done | bytes 1048592 | tf_op jit(solution)/shard_map/all_gather | solution.py:34
  63.8 58.5 %while.12 = (s32[]{:T(128)}, f32[8,256,512]{2,1,0:T(8,128)}, f32[]{:T(128)}, s32[8]{0:T(128)S(1)}, bf16[2048,256]{1,0:T(8,128)(2,1)}, /*index=5*/bf16[1024,256]{...) while((s32[]{:T(128)}, f32[8,256,512]{2,1,0:T(8,128)}, ...), condition=%wide.region_3.4_spmd.clone, body=%wide.region_2.3_spmd.clone.sunk | while | flops 673841152 | bytes 7736045 | solution.py:61
  63.8 0.6 dynamic_slice.29
  65.1 1.2 fusion.51
  66.3 1.2 fusion.52
  68.2 2.9 %fusion.53 = f32[8,256,512]{2,1,0:T(8,128)} fusion(f32[8,256,512]{2,1,0:T(8,128)} %get-tuple-element.256, s32[]{:T(128)} %get-tuple-element.255, bf16[1024,512]{1,0:T(8,128)(2,1)} %get-tuple-element.281, f32[256,1024]{1,0:T(8,128)S(1)} %fusion.51, f32[256,1024]{1,0:T(8,128)S(1)} %fusion.52, bf16[1024,256]{1,0:T(8,128)(2,1)} %get-tuple-element.277, ...), kind=kOutput, calls=%fused_computation.9.clone.1 | convolution fusion | flops 405209088 | bytes 4327944 | tf_op jit(solution)/shard_map/while/body/eval_jaxpr/dot_general | solution.py:59
  71.1 0.6 dynamic_slice.29
  72.4 1.2 fusion.51
  73.6 1.2 fusion.52
  75.5 2.9 %fusion.53 = f32[8,256,512]{2,1,0:T(8,128)} fusion(f32[8,256,512]{2,1,0:T(8,128)} %get-tuple-element.256, s32[]{:T(128)} %get-tuple-element.255, bf16[1024,512]{1,0:T(8,128)(2,1)} %get-tuple-element.281, f32[256,1024]{1,0:T(8,128)S(1)} %fusion.51, f32[256,1024]{1,0:T(8,128)S(1)} %fusion.52, bf16[1024,256]{1,0:T(8,128)(2,1)} %get-tuple-element.277, ...), kind=kOutput, calls=%fused_computation.9.clone.1 | convolution fusion | flops 405209088 | bytes 4327944 | tf_op jit(solution)/shard_map/while/body/eval_jaxpr/dot_general | solution.py:59
  78.4 0.6 dynamic_slice.29
  79.7 1.2 fusion.51
  80.9 1.2 fusion.52
  82.8 2.9 %fusion.53 = f32[8,256,512]{2,1,0:T(8,128)} fusion(f32[8,256,512]{2,1,0:T(8,128)} %get-tuple-element.256, s32[]{:T(128)} %get-tuple-element.255, bf16[1024,512]{1,0:T(8,128)(2,1)} %get-tuple-element.281, f32[256,1024]{1,0:T(8,128)S(1)} %fusion.51, f32[256,1024]{1,0:T(8,128)S(1)} %fusion.52, bf16[1024,256]{1,0:T(8,128)(2,1)} %get-tuple-element.277, ...), kind=kOutput, calls=%fused_computation.9.clone.1 | convolution fusion | flops 405209088 | bytes 4327944 | tf_op jit(solution)/shard_map/while/body/eval_jaxpr/dot_general | solution.py:59
  85.8 0.6 dynamic_slice.29
  87.0 1.2 fusion.51
  88.2 1.2 fusion.52
  90.1 2.9 %fusion.53 = f32[8,256,512]{2,1,0:T(8,128)} fusion(f32[8,256,512]{2,1,0:T(8,128)} %get-tuple-element.256, s32[]{:T(128)} %get-tuple-element.255, bf16[1024,512]{1,0:T(8,128)(2,1)} %get-tuple-element.281, f32[256,1024]{1,0:T(8,128)S(1)} %fusion.51, f32[256,1024]{1,0:T(8,128)S(1)} %fusion.52, bf16[1024,256]{1,0:T(8,128)(2,1)} %get-tuple-element.277, ...), kind=kOutput, calls=%fused_computation.9.clone.1 | convolution fusion | flops 405209088 | bytes 4327944 | tf_op jit(solution)/shard_map/while/body/eval_jaxpr/dot_general | solution.py:59
  93.1 0.6 dynamic_slice.29
  94.3 1.2 fusion.51
  95.6 1.2 fusion.52
  97.5 2.9 %fusion.53 = f32[8,256,512]{2,1,0:T(8,128)} fusion(f32[8,256,512]{2,1,0:T(8,128)} %get-tuple-element.256, s32[]{:T(128)} %get-tuple-element.255, bf16[1024,512]{1,0:T(8,128)(2,1)} %get-tuple-element.281, f32[256,1024]{1,0:T(8,128)S(1)} %fusion.51, f32[256,1024]{1,0:T(8,128)S(1)} %fusion.52, bf16[1024,256]{1,0:T(8,128)(2,1)} %get-tuple-element.277, ...), kind=kOutput, calls=%fused_computation.9.clone.1 | convolution fusion | flops 405209088 | bytes 4327944 | tf_op jit(solution)/shard_map/while/body/eval_jaxpr/dot_general | solution.py:59
  100.4 0.6 dynamic_slice.29
  101.6 1.2 fusion.51
  102.9 1.2 fusion.52
  104.8 2.9 %fusion.53 = f32[8,256,512]{2,1,0:T(8,128)} fusion(f32[8,256,512]{2,1,0:T(8,128)} %get-tuple-element.256, s32[]{:T(128)} %get-tuple-element.255, bf16[1024,512]{1,0:T(8,128)(2,1)} %get-tuple-element.281, f32[256,1024]{1,0:T(8,128)S(1)} %fusion.51, f32[256,1024]{1,0:T(8,128)S(1)} %fusion.52, bf16[1024,256]{1,0:T(8,128)(2,1)} %get-tuple-element.277, ...), kind=kOutput, calls=%fused_computation.9.clone.1 | convolution fusion | flops 405209088 | bytes 4327944 | tf_op jit(solution)/shard_map/while/body/eval_jaxpr/dot_general | solution.py:59
  107.7 0.6 dynamic_slice.29
  108.9 1.2 fusion.51
  110.2 1.2 fusion.52
  112.1 2.9 %fusion.53 = f32[8,256,512]{2,1,0:T(8,128)} fusion(f32[8,256,512]{2,1,0:T(8,128)} %get-tuple-element.256, s32[]{:T(128)} %get-tuple-element.255, bf16[1024,512]{1,0:T(8,128)(2,1)} %get-tuple-element.281, f32[256,1024]{1,0:T(8,128)S(1)} %fusion.51, f32[256,1024]{1,0:T(8,128)S(1)} %fusion.52, bf16[1024,256]{1,0:T(8,128)(2,1)} %get-tuple-element.277, ...), kind=kOutput, calls=%fused_computation.9.clone.1 | convolution fusion | flops 405209088 | bytes 4327944 | tf_op jit(solution)/shard_map/while/body/eval_jaxpr/dot_general | solution.py:59
  115.0 0.6 dynamic_slice.29
  116.3 1.2 fusion.51
  117.5 1.2 fusion.52
  119.4 2.9 %fusion.53 = f32[8,256,512]{2,1,0:T(8,128)} fusion(f32[8,256,512]{2,1,0:T(8,128)} %get-tuple-element.256, s32[]{:T(128)} %get-tuple-element.255, bf16[1024,512]{1,0:T(8,128)(2,1)} %get-tuple-element.281, f32[256,1024]{1,0:T(8,128)S(1)} %fusion.51, f32[256,1024]{1,0:T(8,128)S(1)} %fusion.52, bf16[1024,256]{1,0:T(8,128)(2,1)} %get-tuple-element.277, ...), kind=kOutput, calls=%fused_computation.9.clone.1 | convolution fusion | flops 405209088 | bytes 4327944 | tf_op jit(solution)/shard_map/while/body/eval_jaxpr/dot_general | solution.py:59
  122.3 0.0 reduce-scatter.2.cloned.1.call-update
  122.3 49.8 %reduce-scatter.2.cloned.1.call-done = f32[256,512]{1,0:T(8,128)} async-done(((f32[2048,512]{1,0:T(8,128)}), f32[256,512]{1,0:T(8,128)}) %reduce-scatter.2.cloned.1.call-update) | async-done | bytes 524304 | tf_op jit(solution)/shard_map/reduce_scatter | solution.py:62
  172.1 1.9 %broadcast_multiply_fusion = f32[256,512]{1,0:T(8,128)} fusion(f32[256,512]{1,0:T(8,128)} %reduce-scatter.2.cloned.1.call-done, f32[256]{0:T(256)S(1)} %add_sqrt_fusion), kind=kLoop, calls=%fused_computation.35 | loop fusion | flops 131072 | bytes 1049600 | tf_op jit(solution)/shard_map/mul | solution.py:63
  (4 shorter events, 0.0 us)
Async XLA Ops:
  6.5 33.5 %all-gather.5.cloned.1.call-start = ((), (), s32[]{:S(2)}) async-start(), calls=%async_computation.2 | async-start | bytes 1310720 | tf_op jit(solution)/shard_map/all_gather | solution.py:30
  10.0 53.8 %all-gather.3.cloned.1.call-start = ((), (), s32[]{:S(2)}) async-start(), calls=%async_computation.1 | async-start | bytes 1179648 | tf_op jit(solution)/shard_map/all_gather | solution.py:34
  10.8 161.3 %reduce-scatter.2.cloned.1.call-start = ((), (), s32[]{:S(2)}) async-start(), calls=%async_computation.3 | async-start | bytes 4718592 | tf_op jit(solution)/shard_map/reduce_scatter | solution.py:62
Sparse Core Ops, SparseCore 0:
  10.2 29.8 all-gather.4
  41.7 22.0 all-gather.2
  122.5 49.6 reduce-scatter.1
where the time goes:
time: 181 us
  waiting for transfers between devices  88.9 us (49%)
  matrix products  43.3 us (24%)
  between operations  13.8 us (8%)
  blocking collectives  12.9 us (7%)
  loops' own time  10.4 us (6%)
  other arithmetic  6.43 us (4%)
  local copies, waits for them, and re-layouts  4.87 us (3%)
    reduce_scatter x1, waiting for transfers between devices, per_device(): row_part = lax.psum_scatter(terms, 'col', scatter_dimension=0, tiled=True)  49.8 us
    all_gather x1, waiting for transfers between devices, per_device(): row_y = lax.all_gather(masked, 'col', axis=0, tiled=True)  23.7 us
    dot_general x8, matrix products, row_term(): return jnp.dot(shrunk, col_v, preferred_element_type=jnp.float32)  23.4 us
    all_gather x1, waiting for transfers between devices, per_device(): lax.all_gather(scaled, 'row', axis=0, tiled=True)  14.6 us
    all_gather x1, blocking collectives, per_device(): lax.all_gather(masked, 'row', axis=0, tiled=True)  12.9 us
    another operation x1, loops' own time, per_device(): lax.map(row_term, jnp.arange(ncol, dtype=jnp.int32))  10.4 us
    dot_general x8, matrix products, shrink(): right = jnp.dot(rows_o, cols_sq.T, preferred_element_type=jnp.float32)  9.99 us
    dot_general x8, matrix products, shrink(): cross = jnp.dot(rows_y, cols_y.T, preferred_element_type=jnp.float32)  9.9 us
  transfers between devices with their start and end apart: 3, of which 3 were waited for; matrix products, arithmetic and copies ran while one was open for 1% of the time, Pallas kernels for 0%

commit v1 on v0

v1 whole, which is shorter than its diff:
```python
import functools

import jax
import jax.numpy as jnp
from jax import lax
from jax.experimental import pallas as pl
from jax.experimental.pallas import tpu as pltpu
from jax.sharding import PartitionSpec as P

DENOM = 256
VMEM = pltpu.VMEM


def vspec():
    return pl.BlockSpec(memory_space=VMEM)


def prep_kernel(start_ref, ret_ref, w_ref, masked_ref, both_ref, sigma_ref):
    rows, days = ret_ref.shape
    start = jnp.broadcast_to(start_ref[...].astype(jnp.float32), (days, rows)).T
    day = lax.broadcasted_iota(jnp.int32, (rows, days), 1).astype(jnp.float32)
    y = jnp.where(day >= start, ret_ref[...].astype(jnp.float32), 0.0)
    masked_ref[...] = y.astype(jnp.bfloat16)
    both_ref[:, :days] = y.astype(jnp.bfloat16)
    sq = (y * y).astype(jnp.bfloat16).astype(jnp.float32)
    obs = jnp.where(y != 0.0, 1.0, 0.0)
    total = jnp.sum(sq, axis=1, keepdims=True)
    count = jnp.sum(obs, axis=1, keepdims=True)
    sigma = jnp.sqrt(total / jnp.maximum(count, 1.0) + 1e-06)
    sigma_ref[...] = jnp.broadcast_to(sigma, sigma_ref.shape)
    both_ref[:, days:] = (sigma * w_ref[...].astype(jnp.float32)).astype(jnp.bfloat16)


def nt(a, b):
    return lax.dot_general(a, b, (((1,), (1,)), ((), ())), preferred_element_type=jnp.float32)


def parts_of(y):
    wide = y.astype(jnp.float32)
    obs = jnp.where(wide != 0.0, 1.0, 0.0).astype(jnp.bfloat16)
    return y, obs, (wide * wide).astype(jnp.bfloat16)


def corr_kernel(nrows, has_diag, code_ref, *refs):
    row_refs, col_refs, out_ref = refs[:nrows], refs[nrows:-1], refs[-1]
    own, days = row_refs[0].shape
    delta = code_ref[0].astype(jnp.float32) / DENOM
    keep = 1.0 - delta
    cols = [parts_of(c[:, :days]) for c in col_refs]
    for i, r in enumerate(row_refs):
        ry, ro, rs = parts_of(r[...])
        for j, (cy, co, cs) in enumerate(cols):
            cross, left, right = nt(ry, cy), nt(rs, co), nt(ro, cs)
            shrunk = keep * (cross * lax.rsqrt(left * right + 1e-06))
            if has_diag and i == 0 and j == 0:
                a = lax.broadcasted_iota(jnp.int32, shrunk.shape, 0)
                b = lax.broadcasted_iota(jnp.int32, shrunk.shape, 1)
                shrunk = shrunk + jnp.where(a == b, delta, 0.0)
            out_ref[i * own:(i + 1) * own, j * own:(j + 1) * own] = shrunk.astype(jnp.bfloat16)


def apply_kernel(nchunk, ncore, days, *refs):
    s_refs, v_refs, out_ref = refs[:nchunk], refs[nchunk:-1], refs[-1]
    acc = None
    for k in range(nchunk):
        own = v_refs[0].shape[0]
        for j in range(ncore):
            term = jnp.dot(
                s_refs[k][:, j * own:(j + 1) * own],
                v_refs[k * ncore + j][:, days:],
                preferred_element_type=jnp.float32,
            )
            acc = term if acc is None else acc + term
    out_ref[...] = acc.astype(out_ref.dtype)


def final_kernel(sigma_ref, own_ref, *refs):
    out_ref = refs[-1]
    total = own_ref[...]
    for r in refs[:-1]:
        total = total + r[...].astype(jnp.float32)
    out_ref[...] = sigma_ref[:, :1] * total


def call(kernel, args, outs, specs=None, grid=()):
    return pl.pallas_call(
        kernel,
        grid=grid,
        out_shape=outs,
        in_specs=specs or [vspec() for _ in args],
        out_specs=jax.tree.map(lambda _: vspec(), outs),
        compiler_params=pltpu.CompilerParams(vmem_limit_bytes=48 * 1024 * 1024),
    )(*args)


def per_device(nrow, ncol, returns, start_day, shrink_code, weights):
    own, days = returns.shape
    ports = weights.shape[1]
    far_y, far_z = nrow // 2, ncol // 4

    def send(value, y=0, x=0, zh=0, zl=0, core=0):
        pairs = []
        for r in range(nrow):
            for c in range(ncol):
                rr = (r // 2 + y) % far_y * 2 + (r % 2 + x) % 2
                cc = (c // 4 + zh) % far_z * 4 + (c // 2 % 2 + zl) % 2 * 2 + (c % 2 + core) % 2
                pairs.append((r * ncol + c, rr * ncol + cc))
        return lax.ppermute(value, ("row", "col"), pairs)

    masked, both, sigma = call(
        prep_kernel,
        (start_day.reshape(1, own), returns, weights),
        (
            jax.ShapeDtypeStruct((own, days), jnp.bfloat16),
            jax.ShapeDtypeStruct((own, days + ports), jnp.bfloat16),
            jax.ShapeDtypeStruct((own, 128), jnp.float32),
        ),
    )
    square = [(x, zl) for x in range(2) for zl in range(2)]
    chips = {(0, 0): both}
    for zh in range(1, far_z):
        chips[zh, 0] = send(both, zh=zh)
    for y in range(1, far_y):
        chips[0, y] = send(both, y=y)
    rows = [masked] + [send(masked, x=x, zl=zl) for x, zl in square[1:]]
    for zh in range(1, far_z):
        for y in range(1, far_y):
            chips[zh, y] = send(chips[zh, 0], y=y)
    order = sorted(chips, key=lambda k: (k[0] > 0 and k[1] > 0, k[0] > 0, k))
    swapped = {k: send(chips[k], core=1) for k in order}

    smem = pl.BlockSpec(memory_space=pltpu.SMEM)
    blocks = []
    for k in order:
        args = (shrink_code, *rows, chips[k], swapped[k])
        blocks.append(call(
            functools.partial(corr_kernel, len(rows), k == (0, 0)),
            args,
            jax.ShapeDtypeStruct((len(rows) * own, 2 * own), jnp.bfloat16),
            [smem] + [vspec() for _ in args[1:]],
        ))
    values = [v for k in order for v in (chips[k], swapped[k])]

    def partial_of(i, dtype):
        piece = pl.BlockSpec((own, 2 * own), lambda g: (i, 0))
        return call(
            functools.partial(apply_kernel, len(order), 2, days),
            (*blocks, *values),
            jax.ShapeDtypeStruct((own, ports), dtype),
            [piece for _ in blocks] + [vspec() for _ in values],
            (1,),
        )

    arrived = []
    for i in (3, 1, 2):
        x, zl = square[i]
        arrived.append(send(partial_of(i, jnp.bfloat16), x=x, zl=zl))
    mine = partial_of(0, jnp.float32)
    return call(
        final_kernel, (sigma, mine, *arrived), jax.ShapeDtypeStruct((own, ports), jnp.float32)
    )


def solution(mesh):
    in_specs = (P(("col", "row"), None), P(("col", "row")), P(), P(("col", "row"), None))
    out_specs = P(("col", "row"), None)
    body = functools.partial(per_device, mesh.shape["row"], mesh.shape["col"])
    return jax.shard_map(
        body, mesh=mesh, in_specs=in_specs, out_specs=out_specs, check_vma=False
    )
```

time: 181 us -> 69.3 us (0.38)
  waiting for transfers between devices: 88.9 us -> 35.8 us
  matrix products: 43.3 us -> 0 us
  starting transfers between devices: 0.08 us -> 15.7 us
  between operations: 13.8 us -> 0.76 us
  blocking collectives: 12.9 us -> 0 us
  Pallas kernels: 0 us -> 12.3 us
  loops' own time: 10.4 us -> 0 us
  other arithmetic: 6.43 us -> 0 us
    reduce_scatter x1 -> x0, waiting for transfers between devices: 49.8 us -> none  [per_device(): row_part = lax.psum_scatter(terms, 'col', scatter_dimension=0, tiled=True)]
    dot_general x24 -> x0, matrix products: 43.3 us -> none  [the longest x8 23.4 us: row_term(): return jnp.dot(shrunk, col_v, preferred_element_type=jnp.float32)]
    all_gather x2 -> x0, waiting for transfers between devices: 38.3 us -> none  [the longest x1 23.7 us: per_device(): row_y = lax.all_gather(masked, 'col', axis=0, tiled=True)]
    ppermute x0 -> x13, waiting for transfers between devices: none -> 35.8 us  [send(): return lax.ppermute(value, ('row', 'col'), pairs)]
    ppermute x0 -> x13, starting transfers between devices: none -> 15.7 us  [send(): return lax.ppermute(value, ('row', 'col'), pairs)]
    all_gather x1 -> x0, blocking collectives: 12.9 us -> none  [per_device(): lax.all_gather(masked, 'row', axis=0, tiled=True)]
    pallas_call x0 -> x10, Pallas kernels: none -> 12.3 us  [call(): pl.pallas_call(kernel, grid=grid, out_shape=outs, in_specs=specs or [vspe...]
    another operation x1 -> x0, loops' own time: 10.4 us -> none  [per_device(): lax.map(row_term, jnp.arange(ncol, dtype=jnp.int32))]
  transfers between devices with their start and end apart: 3 -> 13, of which waited for: 3 -> 7; matrix products, arithmetic and copies ran while one was open for 1% -> 0% of each run, Pallas kernels for 0% -> 12%
where the time goes in v1:
time: 69.3 us; the launch traced here: 69 us
  waiting for transfers between devices  35.8 us (52%)
  starting transfers between devices  15.7 us (23%)
  Pallas kernels  12.3 us (18%)
  local copies, waits for them, and re-layouts  4.5 us (6%)
  between operations  0.76 us (1%)
    ppermute x13, waiting for transfers between devices, send(): return lax.ppermute(value, ('row', 'col'), pairs)  35.8 us
    ppermute x13, starting transfers between devices, send(): return lax.ppermute(value, ('row', 'col'), pairs)  15.7 us
    pallas_call x10, Pallas kernels, call(): pl.pallas_call(kernel, grid=grid, out_shape=outs, in_specs=specs or [vspe...  12.3 us
    unnamed x10, local copies, waits for them, and re-layouts  4.5 us
  transfers between devices with their start and end apart: 13, of which 7 were waited for; matrix products, arithmetic and copies ran while one was open for 0% of the time, Pallas kernels for 12%

profile of v1, /device:TPU:0, one launch (start us, length us, event | category | flops | bytes accessed | tf_op | source)
XLA Modules:
  0.0 69.0 jit_solution(6745607330560371394)
XLA Ops:
  0.0 0.0 copy-start.4
  0.0 0.7 copy-done.4
  0.7 0.0 copy-start.2
  0.7 0.9 %copy-done.2 = bf16[256,512]{1,0:T(8,128)(2,1)S(1)} copy-done((bf16[256,512]{1,0:T(8,128)(2,1)S(1)}, bf16[256,512]{1,0:T(8,128)(2,1)}, u32[]{:S(2)}) %copy-start.2) | copy-done | bytes 262168
  1.6 0.0 copy-start.3
  1.6 0.9 %copy-done.3 = bf16[256,256]{1,0:T(8,128)(2,1)S(1)} copy-done((bf16[256,256]{1,0:T(8,128)(2,1)S(1)}, bf16[256,256]{1,0:T(8,128)(2,1)}, u32[]{:S(2)}) %copy-start.3) | copy-done | bytes 131096
  2.5 0.3 shard_map.46
  2.8 4.1 %collective-permute-start.6 = (bf16[256,768]{1,0:T(8,128)(2,1)S(1)}, bf16[256,768]{1,0:T(8,128)(2,1)S(1)}, u32[]{:S(2)}, u32[]{:S(2)}) collective-permute-start(bf16[256,768]{1,0:T(8,128)(2,1)S(1)} %get-tuple-element.10.refs_4_), channel_id=1, source_target_pairs={{0,4},{1,5},{2,6},{3,7},{4,0},{5,1},{6,2},{7,3},{8,12},{9,13},{10,... | collective-permute-start | bytes 1179656 | tf_op jit(solution)/shard_map/ppermute | solution.py:108
  6.9 1.5 %collective-permute-start.4 = (bf16[256,768]{1,0:T(8,128)(2,1)S(1)}, bf16[256,768]{1,0:T(8,128)(2,1)S(1)}, u32[]{:S(2)}, u32[]{:S(2)}) collective-permute-start(bf16[256,768]{1,0:T(8,128)(2,1)S(1)} %get-tuple-element.10.refs_4_), channel_id=1, source_target_pairs={{0,16},{1,17},{2,18},{3,19},{4,20},{5,21},{6,22},{7,23},{8,24},{9,... | collective-permute-start | bytes 1179656 | tf_op jit(solution)/shard_map/ppermute | solution.py:108
  8.4 16.0 %collective-permute-done.6.refs_4_.refs_8_ = bf16[256,768]{1,0:T(8,128)(2,1)S(1)} collective-permute-done((bf16[256,768]{1,0:T(8,128)(2,1)S(1)}, bf16[256,768]{1,0:T(8,128)(2,1)S(1)}, u32[]{:S(2)}, u32[]{:S(2)}) %collective-permute-start.6) | collective-permute-done | bytes 393248 | tf_op jit(solution)/shard_map/ppermute | solution.py:108
  24.4 1.6 %collective-permute-start.8 = (bf16[256,768]{1,0:T(8,128)(2,1)S(1)}, bf16[256,768]{1,0:T(8,128)(2,1)S(1)}, u32[]{:S(2)}, u32[]{:S(2)}) collective-permute-start(bf16[256,768]{1,0:T(8,128)(2,1)S(1)} %collective-permute-done.6.refs_4_.refs_8_), channel_id=1, source_target_pairs={{0,16},{1,17},{2,18},{3,19},{4,20},{5,21},{6,22},{7,23},{8,24},{9,... | collective-permute-start | bytes 1179656 | tf_op jit(solution)/shard_map/ppermute | solution.py:108
  26.0 1.6 %collective-permute-start.2 = (bf16[256,256]{1,0:T(8,128)(2,1)S(1)}, bf16[256,256]{1,0:T(8,128)(2,1)S(1)}, u32[]{:S(2)}, u32[]{:S(2)}) collective-permute-start(bf16[256,256]{1,0:T(8,128)(2,1)S(1)} %get-tuple-element.9.refs_0_), channel_id=1, source_target_pairs={{0,10},{1,11},{2,8},{3,9},{4,14},{5,15},{6,12},{7,13},{8,2},{9,3},... | collective-permute-start | bytes 393224 | tf_op jit(solution)/shard_map/ppermute | solution.py:108
  27.6 0.0 collective-permute-start.3
  27.6 0.0 collective-permute-done.4.refs_4_.refs_6_
  27.6 0.5 collective-permute-start.5
  28.1 0.0 collective-permute-start.7
  28.1 6.6 %collective-permute-done.8.refs_4_.refs_10_ = bf16[256,768]{1,0:T(8,128)(2,1)S(1)} collective-permute-done((bf16[256,768]{1,0:T(8,128)(2,1)S(1)}, bf16[256,768]{1,0:T(8,128)(2,1)S(1)}, u32[]{:S(2)}, u32[]{:S(2)}) %collective-permute-start.8) | collective-permute-done | bytes 393248 | tf_op jit(solution)/shard_map/ppermute | solution.py:108
  34.7 0.0 collective-permute-start.9
  34.7 0.0 collective-permute-done.2.refs_3_
  34.7 1.2 %collective-permute-start.1 = (bf16[256,256]{1,0:T(8,128)(2,1)S(1)}, bf16[256,256]{1,0:T(8,128)(2,1)S(1)}, u32[]{:S(2)}, u32[]{:S(2)}) collective-permute-start(bf16[256,256]{1,0:T(8,128)(2,1)S(1)} %get-tuple-element.9.refs_0_), channel_id=1, source_target_pairs={{0,8},{1,9},{2,10},{3,11},{4,12},{5,13},{6,14},{7,15},{8,0},{9,1},... | collective-permute-start | bytes 393224 | tf_op jit(solution)/shard_map/ppermute | solution.py:108
  36.0 4.7 %collective-permute-done.1.refs_2_ = bf16[256,256]{1,0:T(8,128)(2,1)S(1)} collective-permute-done((bf16[256,256]{1,0:T(8,128)(2,1)S(1)}, bf16[256,256]{1,0:T(8,128)(2,1)S(1)}, u32[]{:S(2)}, u32[]{:S(2)}) %collective-permute-start.1) | collective-permute-done | bytes 131104 | tf_op jit(solution)/shard_map/ppermute | solution.py:108
  40.7 1.5 %collective-permute-start = (bf16[256,256]{1,0:T(8,128)(2,1)S(1)}, bf16[256,256]{1,0:T(8,128)(2,1)S(1)}, u32[]{:S(2)}, u32[]{:S(2)}) collective-permute-start(bf16[256,256]{1,0:T(8,128)(2,1)S(1)} %get-tuple-element.9.refs_0_), channel_id=1, source_target_pairs={{0,2},{1,3},{2,0},{3,1},{4,6},{5,7},{6,4},{7,5},{8,10},{9,11},{10,... | collective-permute-start | bytes 393224 | tf_op jit(solution)/shard_map/ppermute | solution.py:108
  42.8 3.0 %collective-permute-done.refs_1_ = bf16[256,256]{1,0:T(8,128)(2,1)S(1)} collective-permute-done((bf16[256,256]{1,0:T(8,128)(2,1)S(1)}, bf16[256,256]{1,0:T(8,128)(2,1)S(1)}, u32[]{:S(2)}, u32[]{:S(2)}) %collective-permute-start) | collective-permute-done | bytes 131104 | tf_op jit(solution)/shard_map/ppermute | solution.py:108
  45.8 0.0 collective-permute-done.3.refs_5_
  45.8 1.1 %shard_map.47.refs_0_ = bf16[1024,512]{1,0:T(8,128)(2,1)S(1)} custom-call(s32[1]{0:T(128)S(6)} %copy.5.code_ref, bf16[256,256]{1,0:T(8,128)(2,1)S(1)} %get-tuple-element.9.refs_0_, bf16[256,256]{1,0:T(8,128)(2,1)S(1)} %collective-permute-done.refs_1_, bf16[256,256]{1,0:T(8,128)(2,1)S(1)} %collective-permute-done.1.refs_2_, ...), custom_call_target="tpu_custom_call" | custom-call | tf_op jit(solution)/shard_map/pallas_call | solution.py:86
  46.9 0.0 collective-permute-done.5.refs_5_.refs_7_
  46.9 1.1 %shard_map.48.refs_1_ = bf16[1024,512]{1,0:T(8,128)(2,1)S(1)} custom-call(s32[1]{0:T(128)S(6)} %copy.5.code_ref, bf16[256,256]{1,0:T(8,128)(2,1)S(1)} %get-tuple-element.9.refs_0_, bf16[256,256]{1,0:T(8,128)(2,1)S(1)} %collective-permute-done.refs_1_, bf16[256,256]{1,0:T(8,128)(2,1)S(1)} %collective-permute-done.1.refs_2_, ...), custom_call_target="tpu_custom_call" | custom-call | tf_op jit(solution)/shard_map/pallas_call | solution.py:86
  47.9 0.0 collective-permute-done.7.refs_5_.refs_9_
  47.9 1.1 %shard_map.49.refs_2_ = bf16[1024,512]{1,0:T(8,128)(2,1)S(1)} custom-call(s32[1]{0:T(128)S(6)} %copy.5.code_ref, bf16[256,256]{1,0:T(8,128)(2,1)S(1)} %get-tuple-element.9.refs_0_, bf16[256,256]{1,0:T(8,128)(2,1)S(1)} %collective-permute-done.refs_1_, bf16[256,256]{1,0:T(8,128)(2,1)S(1)} %collective-permute-done.1.refs_2_, ...), custom_call_target="tpu_custom_call" | custom-call | tf_op jit(solution)/shard_map/pallas_call | solution.py:86
  49.0 0.0 copy-start
  49.0 1.0 %copy-done = bf16[1024,512]{1,0:T(8,128)(2,1)} copy-done((bf16[1024,512]{1,0:T(8,128)(2,1)}, bf16[1024,512]{1,0:T(8,128)(2,1)S(1)}, u32[]{:S(2)}) %copy-start) | copy-done | bytes 1048600
  50.0 0.0 collective-permute-done.9.refs_5_.refs_11_
  50.0 1.0 %shard_map.50.refs_3_ = bf16[1024,512]{1,0:T(8,128)(2,1)S(1)} custom-call(s32[1]{0:T(128)S(6)} %copy.5.code_ref, bf16[256,256]{1,0:T(8,128)(2,1)S(1)} %get-tuple-element.9.refs_0_, bf16[256,256]{1,0:T(8,128)(2,1)S(1)} %collective-permute-done.refs_1_, bf16[256,256]{1,0:T(8,128)(2,1)S(1)} %collective-permute-done.1.refs_2_, ...), custom_call_target="tpu_custom_call" | custom-call | tf_op jit(solution)/shard_map/pallas_call | solution.py:86
  51.0 0.0 copy-start.1
  51.0 1.0 %copy-done.1 = bf16[1024,512]{1,0:T(8,128)(2,1)} copy-done((bf16[1024,512]{1,0:T(8,128)(2,1)}, bf16[1024,512]{1,0:T(8,128)(2,1)S(1)}, u32[]{:S(2)}) %copy-start.1) | copy-done | bytes 1048600
  52.0 1.7 %shard_map.52 = bf16[256,512]{1,0:T(8,128)(2,1)S(1)} custom-call(bf16[1024,512]{1,0:T(8,128)(2,1)S(1)} %shard_map.47.refs_0_, bf16[1024,512]{1,0:T(8,128)(2,1)S(1)} %shard_map.48.refs_1_, bf16[1024,512]{1,0:T(8,128)(2,1)} %copy-done, bf16[1024,512]{1,0:T(8,128)(2,1)} %copy-done.1, bf16[256,768]{1,0:T(8,128)(2,1)S(1)} %get-tuple-element.10.refs_4_, ...), custom_call_target="tpu_custom_call" | custom-call | tf_op jit(solution)/shard_map/pallas_call | solution.py:86
  53.8 2.5 %collective-permute-start.10 = (bf16[256,512]{1,0:T(8,128)(2,1)S(1)}, bf16[256,512]{1,0:T(8,128)(2,1)S(1)}, u32[]{:S(2)}, u32[]{:S(2)}) collective-permute-start(bf16[256,512]{1,0:T(8,128)(2,1)S(1)} %shard_map.52), channel_id=1, source_target_pairs={{0,10},{1,11},{2,8},{3,9},{4,14},{5,15},{6,12},{7,13},{8,2},{9,3},... | collective-permute-start | bytes 786440 | tf_op jit(solution)/shard_map/ppermute | solution.py:108
  56.2 1.7 %shard_map.53 = bf16[256,512]{1,0:T(8,128)(2,1)S(1)} custom-call(bf16[1024,512]{1,0:T(8,128)(2,1)S(1)} %shard_map.47.refs_0_, bf16[1024,512]{1,0:T(8,128)(2,1)S(1)} %shard_map.48.refs_1_, bf16[1024,512]{1,0:T(8,128)(2,1)} %copy-done, bf16[1024,512]{1,0:T(8,128)(2,1)} %copy-done.1, bf16[256,768]{1,0:T(8,128)(2,1)S(1)} %get-tuple-element.10.refs_4_, ...), custom_call_target="tpu_custom_call" | custom-call | tf_op jit(solution)/shard_map/pallas_call | solution.py:86
  58.0 0.4 collective-permute-start.11
  58.3 1.7 %shard_map.54 = bf16[256,512]{1,0:T(8,128)(2,1)S(1)} custom-call(bf16[1024,512]{1,0:T(8,128)(2,1)S(1)} %shard_map.47.refs_0_, bf16[1024,512]{1,0:T(8,128)(2,1)S(1)} %shard_map.48.refs_1_, bf16[1024,512]{1,0:T(8,128)(2,1)} %copy-done, bf16[1024,512]{1,0:T(8,128)(2,1)} %copy-done.1, bf16[256,768]{1,0:T(8,128)(2,1)S(1)} %get-tuple-element.10.refs_4_, ...), custom_call_target="tpu_custom_call" | custom-call | tf_op jit(solution)/shard_map/pallas_call | solution.py:86
  60.1 0.8 %collective-permute-start.12 = (bf16[256,512]{1,0:T(8,128)(2,1)S(1)}, bf16[256,512]{1,0:T(8,128)(2,1)S(1)}, u32[]{:S(2)}, u32[]{:S(2)}) collective-permute-start(bf16[256,512]{1,0:T(8,128)(2,1)S(1)} %shard_map.54), channel_id=1, source_target_pairs={{0,8},{1,9},{2,10},{3,11},{4,12},{5,13},{6,14},{7,15},{8,0},{9,1},... | collective-permute-start | bytes 786440 | tf_op jit(solution)/shard_map/ppermute | solution.py:108
  60.9 1.7 %shard_map.51.own_ref = f32[256,512]{1,0:T(8,128)S(1)} custom-call(bf16[1024,512]{1,0:T(8,128)(2,1)S(1)} %shard_map.47.refs_0_, bf16[1024,512]{1,0:T(8,128)(2,1)S(1)} %shard_map.48.refs_1_, bf16[1024,512]{1,0:T(8,128)(2,1)} %copy-done, bf16[1024,512]{1,0:T(8,128)(2,1)} %copy-done.1, bf16[256,768]{1,0:T(8,128)(2,1)S(1)} %get-tuple-element.10.refs_4_, ...), custom_call_target="tpu_custom_call" | custom-call | tf_op jit(solution)/shard_map/pallas_call | solution.py:86
  62.7 1.3 %collective-permute-done.10.refs_0_ = bf16[256,512]{1,0:T(8,128)(2,1)S(1)} collective-permute-done((bf16[256,512]{1,0:T(8,128)(2,1)S(1)}, bf16[256,512]{1,0:T(8,128)(2,1)S(1)}, u32[]{:S(2)}, u32[]{:S(2)}) %collective-permute-start.10) | collective-permute-done | bytes 262176 | tf_op jit(solution)/shard_map/ppermute | solution.py:108
  64.0 3.2 %collective-permute-done.11.refs_1_ = bf16[256,512]{1,0:T(8,128)(2,1)S(1)} collective-permute-done((bf16[256,512]{1,0:T(8,128)(2,1)S(1)}, bf16[256,512]{1,0:T(8,128)(2,1)S(1)}, u32[]{:S(2)}, u32[]{:S(2)}) %collective-permute-start.11) | collective-permute-done | bytes 262176 | tf_op jit(solution)/shard_map/ppermute | solution.py:108
  67.2 0.9 %collective-permute-done.12.refs_2_ = bf16[256,512]{1,0:T(8,128)(2,1)S(1)} collective-permute-done((bf16[256,512]{1,0:T(8,128)(2,1)S(1)}, bf16[256,512]{1,0:T(8,128)(2,1)S(1)}, u32[]{:S(2)}, u32[]{:S(2)}) %collective-permute-start.12) | collective-permute-done | bytes 262176 | tf_op jit(solution)/shard_map/ppermute | solution.py:108
  68.1 0.9 %shard_map.55 = f32[256,512]{1,0:T(8,128)} custom-call(f32[256,128]{1,0:T(8,128)S(1)} %get-tuple-element.8.sigma_ref, f32[256,512]{1,0:T(8,128)S(1)} %shard_map.51.own_ref, bf16[256,512]{1,0:T(8,128)(2,1)S(1)} %collective-permute-done.10.refs_0_, bf16[256,512]{1,0:T(8,128)(2,1)S(1)} %collective-permute-done.11.refs_1_, ...), custom_call_target="tpu_custom_call" | custom-call | tf_op jit(solution)/shard_map/pallas_call | solution.py:86
Async XLA Ops:
  0.0 0.7 copy-start.4
  0.7 0.9 %copy-start.2 = (bf16[256,512]{1,0:T(8,128)(2,1)S(1)}, bf16[256,512]{1,0:T(8,128)(2,1)}, u32[]{:S(2)}) copy-start(bf16[256,512]{1,0:T(8,128)(2,1)} %w_ref.1) | copy-start | bytes 786436
  1.6 0.9 %copy-start.3 = (bf16[256,256]{1,0:T(8,128)(2,1)S(1)}, bf16[256,256]{1,0:T(8,128)(2,1)}, u32[]{:S(2)}) copy-start(bf16[256,256]{1,0:T(8,128)(2,1)} %ret_ref.1) | copy-start | bytes 393220
  2.8 21.6 %collective-permute-start.6 = (bf16[256,768]{1,0:T(8,128)(2,1)S(1)}, bf16[256,768]{1,0:T(8,128)(2,1)S(1)}, u32[]{:S(2)}, u32[]{:S(2)}) collective-permute-start(bf16[256,768]{1,0:T(8,128)(2,1)S(1)} %get-tuple-element.10.refs_4_), channel_id=1, source_target_pairs={{0,4},{1,5},{2,6},{3,7},{4,0},{5,1},{6,2},{7,3},{8,12},{9,13},{10,... | collective-permute-start | bytes 1179656 | tf_op jit(solution)/shard_map/ppermute | solution.py:108
  6.9 20.7 %collective-permute-start.4 = (bf16[256,768]{1,0:T(8,128)(2,1)S(1)}, bf16[256,768]{1,0:T(8,128)(2,1)S(1)}, u32[]{:S(2)}, u32[]{:S(2)}) collective-permute-start(bf16[256,768]{1,0:T(8,128)(2,1)S(1)} %get-tuple-element.10.refs_4_), channel_id=1, source_target_pairs={{0,16},{1,17},{2,18},{3,19},{4,20},{5,21},{6,22},{7,23},{8,24},{9,... | collective-permute-start | bytes 1179656 | tf_op jit(solution)/shard_map/ppermute | solution.py:108
  24.4 10.3 %collective-permute-start.8 = (bf16[256,768]{1,0:T(8,128)(2,1)S(1)}, bf16[256,768]{1,0:T(8,128)(2,1)S(1)}, u32[]{:S(2)}, u32[]{:S(2)}) collective-permute-start(bf16[256,768]{1,0:T(8,128)(2,1)S(1)} %collective-permute-done.6.refs_4_.refs_8_), channel_id=1, source_target_pairs={{0,16},{1,17},{2,18},{3,19},{4,20},{5,21},{6,22},{7,23},{8,24},{9,... | collective-permute-start | bytes 1179656 | tf_op jit(solution)/shard_map/ppermute | solution.py:108
  26.0 8.7 %collective-permute-start.2 = (bf16[256,256]{1,0:T(8,128)(2,1)S(1)}, bf16[256,256]{1,0:T(8,128)(2,1)S(1)}, u32[]{:S(2)}, u32[]{:S(2)}) collective-permute-start(bf16[256,256]{1,0:T(8,128)(2,1)S(1)} %get-tuple-element.9.refs_0_), channel_id=1, source_target_pairs={{0,10},{1,11},{2,8},{3,9},{4,14},{5,15},{6,12},{7,13},{8,2},{9,3},... | collective-permute-start | bytes 393224 | tf_op jit(solution)/shard_map/ppermute | solution.py:108
  27.6 18.2 %collective-permute-start.3 = (bf16[256,768]{1,0:T(8,128)(2,1)S(1)}, bf16[256,768]{1,0:T(8,128)(2,1)S(1)}, u32[]{:S(2)}, u32[]{:S(2)}) collective-permute-start(bf16[256,768]{1,0:T(8,128)(2,1)S(1)} %get-tuple-element.10.refs_4_), channel_id=1, source_target_pairs={{0,1},{1,0},{2,3},{3,2},{4,5},{5,4},{6,7},{7,6},{8,9},{9,8},{10,11... | collective-permute-start | bytes 1179656 | tf_op jit(solution)/shard_map/ppermute | solution.py:108
  27.6 19.2 %collective-permute-start.5 = (bf16[256,768]{1,0:T(8,128)(2,1)S(1)}, bf16[256,768]{1,0:T(8,128)(2,1)S(1)}, u32[]{:S(2)}, u32[]{:S(2)}) collective-permute-start(bf16[256,768]{1,0:T(8,128)(2,1)S(1)} %collective-permute-done.4.refs_4_.refs_6_), channel_id=1, source_target_pairs={{0,1},{1,0},{2,3},{3,2},{4,5},{5,4},{6,7},{7,6},{8,9},{9,8},{10,11... | collective-permute-start | bytes 1179656 | tf_op jit(solution)/shard_map/ppermute | solution.py:108
  28.1 19.8 %collective-permute-start.7 = (bf16[256,768]{1,0:T(8,128)(2,1)S(1)}, bf16[256,768]{1,0:T(8,128)(2,1)S(1)}, u32[]{:S(2)}, u32[]{:S(2)}) collective-permute-start(bf16[256,768]{1,0:T(8,128)(2,1)S(1)} %collective-permute-done.6.refs_4_.refs_8_), channel_id=1, source_target_pairs={{0,1},{1,0},{2,3},{3,2},{4,5},{5,4},{6,7},{7,6},{8,9},{9,8},{10,11... | collective-permute-start | bytes 1179656 | tf_op jit(solution)/shard_map/ppermute | solution.py:108
  34.7 15.2 %collective-permute-start.9 = (bf16[256,768]{1,0:T(8,128)(2,1)S(1)}, bf16[256,768]{1,0:T(8,128)(2,1)S(1)}, u32[]{:S(2)}, u32[]{:S(2)}) collective-permute-start(bf16[256,768]{1,0:T(8,128)(2,1)S(1)} %collective-permute-done.8.refs_4_.refs_10_), channel_id=1, source_target_pairs={{0,1},{1,0},{2,3},{3,2},{4,5},{5,4},{6,7},{7,6},{8,9},{9,8},{10,11... | collective-permute-start | bytes 1179656 | tf_op jit(solution)/shard_map/ppermute | solution.py:108
  34.7 5.9 %collective-permute-start.1 = (bf16[256,256]{1,0:T(8,128)(2,1)S(1)}, bf16[256,256]{1,0:T(8,128)(2,1)S(1)}, u32[]{:S(2)}, u32[]{:S(2)}) collective-permute-start(bf16[256,256]{1,0:T(8,128)(2,1)S(1)} %get-tuple-element.9.refs_0_), channel_id=1, source_target_pairs={{0,8},{1,9},{2,10},{3,11},{4,12},{5,13},{6,14},{7,15},{8,0},{9,1},... | collective-permute-start | bytes 393224 | tf_op jit(solution)/shard_map/ppermute | solution.py:108
  40.7 5.1 %collective-permute-start = (bf16[256,256]{1,0:T(8,128)(2,1)S(1)}, bf16[256,256]{1,0:T(8,128)(2,1)S(1)}, u32[]{:S(2)}, u32[]{:S(2)}) collective-permute-start(bf16[256,256]{1,0:T(8,128)(2,1)S(1)} %get-tuple-element.9.refs_0_), channel_id=1, source_target_pairs={{0,2},{1,3},{2,0},{3,1},{4,6},{5,7},{6,4},{7,5},{8,10},{9,11},{10,... | collective-permute-start | bytes 393224 | tf_op jit(solution)/shard_map/ppermute | solution.py:108
  49.0 1.0 %copy-start = (bf16[1024,512]{1,0:T(8,128)(2,1)}, bf16[1024,512]{1,0:T(8,128)(2,1)S(1)}, u32[]{:S(2)}) copy-start(bf16[1024,512]{1,0:T(8,128)(2,1)S(1)} %shard_map.49.refs_2_) | copy-start | bytes 3145732
  51.0 1.0 %copy-start.1 = (bf16[1024,512]{1,0:T(8,128)(2,1)}, bf16[1024,512]{1,0:T(8,128)(2,1)S(1)}, u32[]{:S(2)}) copy-start(bf16[1024,512]{1,0:T(8,128)(2,1)S(1)} %shard_map.50.refs_3_) | copy-start | bytes 3145732
  53.8 10.2 %collective-permute-start.10 = (bf16[256,512]{1,0:T(8,128)(2,1)S(1)}, bf16[256,512]{1,0:T(8,128)(2,1)S(1)}, u32[]{:S(2)}, u32[]{:S(2)}) collective-permute-start(bf16[256,512]{1,0:T(8,128)(2,1)S(1)} %shard_map.52), channel_id=1, source_target_pairs={{0,10},{1,11},{2,8},{3,9},{4,14},{5,15},{6,12},{7,13},{8,2},{9,3},... | collective-permute-start | bytes 786440 | tf_op jit(solution)/shard_map/ppermute | solution.py:108
  58.0 9.2 %collective-permute-start.11 = (bf16[256,512]{1,0:T(8,128)(2,1)S(1)}, bf16[256,512]{1,0:T(8,128)(2,1)S(1)}, u32[]{:S(2)}, u32[]{:S(2)}) collective-permute-start(bf16[256,512]{1,0:T(8,128)(2,1)S(1)} %shard_map.53), channel_id=1, source_target_pairs={{0,2},{1,3},{2,0},{3,1},{4,6},{5,7},{6,4},{7,5},{8,10},{9,11},{10,... | collective-permute-start | bytes 786440 | tf_op jit(solution)/shard_map/ppermute | solution.py:108
  60.1 8.0 %collective-permute-start.12 = (bf16[256,512]{1,0:T(8,128)(2,1)S(1)}, bf16[256,512]{1,0:T(8,128)(2,1)S(1)}, u32[]{:S(2)}, u32[]{:S(2)}) collective-permute-start(bf16[256,512]{1,0:T(8,128)(2,1)S(1)} %shard_map.54), channel_id=1, source_target_pairs={{0,8},{1,9},{2,10},{3,11},{4,12},{5,13},{6,14},{7,15},{8,0},{9,1},... | collective-permute-start | bytes 786440 | tf_op jit(solution)/shard_map/ppermute | solution.py:108

commit v2 on v1

v2 whole, which is shorter than its diff:
```python
import functools

import jax
import jax.numpy as jnp
from jax import lax
from jax.experimental import pallas as pl
from jax.experimental.pallas import tpu as pltpu
from jax.sharding import PartitionSpec as P

DENOM = 256
VMEM = pltpu.VMEM


def vspec():
    return pl.BlockSpec(memory_space=VMEM)


def prep_kernel(start_hbm, ret_hbm, w_hbm, *refs):
    masked_ref, both_ref, sigma_ref, *piece_refs = refs[:-4]
    start_ref, ret_ref, w_ref, sems = refs[-4:]
    loads = [
        pltpu.make_async_copy(src, dst, sems.at[k])
        for k, (src, dst) in enumerate(((start_hbm, start_ref), (ret_hbm, ret_ref), (w_hbm, w_ref)))
    ]
    for load in loads:
        load.start()
    rows, days = ret_ref.shape
    loads[0].wait()
    loads[1].wait()
    start = jnp.broadcast_to(start_ref[...].astype(jnp.float32), (days, rows)).T
    day = lax.broadcasted_iota(jnp.int32, (rows, days), 1).astype(jnp.float32)
    y = jnp.where(day >= start, ret_ref[...].astype(jnp.float32), 0.0)
    sq = (y * y).astype(jnp.bfloat16).astype(jnp.float32)
    obs = jnp.where(y != 0.0, 1.0, 0.0)
    total = jnp.sum(sq, axis=1, keepdims=True)
    count = jnp.sum(obs, axis=1, keepdims=True)
    sigma = jnp.sqrt(total / jnp.maximum(count, 1.0) + 1e-06)
    sigma_ref[...] = jnp.broadcast_to(sigma, sigma_ref.shape)
    masked = y.astype(jnp.bfloat16)
    loads[2].wait()
    scaled = (sigma * w_ref[...].astype(jnp.float32)).astype(jnp.bfloat16)
    masked_ref[...] = masked
    both_ref[:, :days] = masked
    both_ref[:, days:] = scaled
    at = 0
    for ref in piece_refs:
        end = at + ref.shape[0]
        ref[:, :days] = masked[at:end]
        ref[:, days:] = scaled[at:end]
        at = end % rows


def nt(a, b):
    return lax.dot_general(a, b, (((1,), (1,)), ((), ())), preferred_element_type=jnp.float32)


def parts_of(y):
    wide = y.astype(jnp.float32)
    obs = jnp.where(wide != 0.0, 1.0, 0.0).astype(jnp.bfloat16)
    return y, obs, (wide * wide).astype(jnp.bfloat16)


def chip_kernel(nrows, ncols, nin, has_diag, code_ref, *refs):
    row_refs, col_refs = refs[:nrows], refs[nrows:nrows + ncols]
    in_refs, out_refs = refs[nrows + ncols:nrows + ncols + nin], refs[nrows + ncols + nin:]
    days = row_refs[0].shape[1]
    own = out_refs[0].shape[0]
    delta = code_ref[0].astype(jnp.float32) / DENOM
    keep = 1.0 - delta
    ys, values = [c[:, :days] for c in col_refs], [c[:, days:] for c in col_refs]
    while len(ys) > 1 and sum(y.shape[0] for y in ys[:2]) <= own:
        ys = [jnp.concatenate(ys[k:k + 2]) for k in range(0, len(ys), 2)]
    cols = [parts_of(y) for y in ys]
    values = jnp.concatenate(values)
    tiles = [r[t * own:(t + 1) * own] for r in row_refs for t in range(r.shape[0] // own)]
    for i, tile in enumerate(tiles):
        ry, ro, rs = parts_of(tile)
        shrunk = []
        for j, (cy, co, cs) in enumerate(cols):
            cross, left, right = nt(ry, cy), nt(rs, co), nt(ro, cs)
            part = keep * (cross * lax.rsqrt(left * right + 1e-06))
            if has_diag and i == 0 and j == 0:
                a = lax.broadcasted_iota(jnp.int32, part.shape, 0)
                b = lax.broadcasted_iota(jnp.int32, part.shape, 1)
                part = part + jnp.where(a == b, delta, 0.0)
            shrunk.append(part.astype(jnp.bfloat16))
        term = jnp.dot(jnp.concatenate(shrunk, 1), values, preferred_element_type=jnp.float32)
        if nin:
            term = term + in_refs[i][...]
        out_refs[i][...] = term.astype(out_refs[i].dtype)


def final_kernel(sigma_ref, *refs):
    out_ref = refs[-1]
    total = refs[0][...]
    for r in refs[1:-1]:
        total = total + r[...].astype(jnp.float32)
    out_ref[...] = sigma_ref[:, :1] * total


def join_kernel(a_ref, b_ref, out_ref):
    n = a_ref.shape[0]
    out_ref[:n] = a_ref[...]
    out_ref[n:] = b_ref[...]


def call(kernel, args, outs, specs=None, scratch=(), aliases=None):
    return pl.pallas_call(
        kernel,
        out_shape=outs,
        in_specs=specs or [vspec() for _ in args],
        out_specs=jax.tree.map(lambda _: vspec(), outs),
        scratch_shapes=scratch,
        input_output_aliases=aliases or {},
        compiler_params=pltpu.CompilerParams(vmem_limit_bytes=48 * 1024 * 1024),
    )(*args)


def after(value, *others):
    return lax.optimization_barrier((value, *others))[0]


def per_device(nrow, ncol, returns, start_day, shrink_code, weights):
    own, days = returns.shape
    ports = weights.shape[1]
    cut = own // 2
    far_y, far_z = nrow // 2, ncol // 4

    def send(value, y=0, x=0, zh=0, zl=0, core=0):
        pairs = []
        for r in range(nrow):
            for c in range(ncol):
                rr = (r // 2 + y) % far_y * 2 + (r % 2 + x) % 2
                cc = (c // 4 + zh) % far_z * 4 + (c // 2 % 2 + zl) % 2 * 2 + (c % 2 + core) % 2
                pairs.append((r * ncol + c, rr * ncol + cc))
        return lax.ppermute(value, ("row", "col"), pairs)

    smem = pl.BlockSpec(memory_space=pltpu.SMEM)
    shape = jax.ShapeDtypeStruct
    masked, both, sigma, low, high = call(
        prep_kernel,
        tuple(
            pltpu.with_memory_space_constraint(v, pltpu.HBM)
            for v in (start_day.reshape(1, own), returns, weights)
        ),
        (
            shape((own, days), jnp.bfloat16),
            shape((own, days + ports), jnp.bfloat16),
            shape((own, 128), jnp.float32),
            *(shape((n, days + ports), jnp.bfloat16) for n in (cut, own - cut)),
        ),
        [pl.BlockSpec(memory_space=pltpu.HBM)] * 3,
        [
            VMEM((1, own), jnp.int32),
            VMEM((own, days), jnp.bfloat16),
            VMEM((own, ports), jnp.bfloat16),
            pltpu.SemaphoreType.DMA((3,)),
        ],
    )
    far_low = {zh: send(low, zh=zh) for zh in range(1, far_z)}
    far_high = {zh: send(high, zh=zh) for zh in range(1, far_z)}
    near = {y: send(both, y=y) for y in range(1, far_y)}
    from_x = send(masked, x=1)
    from_z = send(masked, zl=1)
    from_xz = send(from_x, zl=1)
    rows = [masked, from_x, from_z, from_xz]
    gate = [from_z, from_xz, *far_low.values()]
    rows[2:] = [after(v, *gate) for v in rows[2:]]
    far_low = {zh: after(v, *gate) for zh, v in far_low.items()}
    total = []

    def chip(cols, last=False):
        args = (shrink_code, *rows, *cols, *total)
        nin = len(total)
        kinds = [jnp.float32] + [jnp.bfloat16 if last else jnp.float32] * 3
        total[:] = call(
            functools.partial(chip_kernel, len(rows), len(cols), nin, nin == 0),
            args,
            [VMEM((own, ports), kind) for kind in kinds],
            [smem] + [vspec() for _ in args[1:]],
            aliases={len(args) - nin + i: i for i in range(nin)} if not last else None,
        )

    pass_low = [send(v, y=y) for v in far_low.values() for y in near]
    low_swap = [send(v, core=1) for v in far_low.values()]
    far_high = {zh: after(v, *low_swap) for zh, v in far_high.items()}
    hold = list(far_high.values())
    pass_high = [send(v, y=y) for v in far_high.values() for y in near]
    high_swap = [send(v, core=1) for v in far_high.values()]
    own_swap = send(after(both, *hold), core=1)
    near = {y: after(v, *hold) for y, v in near.items()}
    near_swap = [send(v, core=1) for v in near.values()]
    chip([both, own_swap])
    for pair in zip(near.values(), near_swap):
        chip(pair)
    for four in zip(far_low.values(), far_high.values(), low_swap, high_swap):
        chip(four)
    pass_low = [after(v, *total) for v in pass_low]
    pass_high = [after(v, *total) for v in pass_high]
    low_swap = [send(v, core=1) for v in pass_low]
    high_swap = [send(v, core=1) for v in pass_high]
    tail = list(zip(pass_low, pass_high, low_swap, high_swap))
    for k, four in enumerate(tail):
        chip(four, k == len(tail) - 1)

    arrived = [total[0]]
    for i, x, zl in ((3, 1, 1), (1, 1, 0), (2, 0, 1)):
        arrived.append(send(total[i], x=x, zl=zl))
    return call(final_kernel, (sigma, *arrived), shape((own, ports), jnp.float32))


def solution(mesh):
    in_specs = (P(("col", "row"), None), P(("col", "row")), P(), P(("col", "row"), None))
    out_specs = P(("col", "row"), None)
    body = functools.partial(per_device, mesh.shape["row"], mesh.shape["col"])
    return jax.shard_map(
        body, mesh=mesh, in_specs=in_specs, out_specs=out_specs, check_vma=False
    )
```

time: 69.3 us -> 54.8 us (0.79)
  waiting for transfers between devices: 35.8 us -> 27.1 us
  local copies, waits for them, and re-layouts: 4.5 us -> 0 us
  Pallas kernels: 12.3 us -> 9.6 us
  starting transfers between devices: 15.7 us -> 17.1 us
    ppermute x13 -> x17, waiting for transfers between devices: 35.8 us -> 27.1 us  [send(): return lax.ppermute(value, ('row', 'col'), pairs)]
    unnamed x10 -> x0, local copies, waits for them, and re-layouts: 4.5 us -> none
    pallas_call x10 -> x6, Pallas kernels: 12.3 us -> 9.6 us  [call(): pl.pallas_call(kernel, out_shape=outs, in_specs=specs or [vspec() for _ i...]
    ppermute x13 -> x17, starting transfers between devices: 15.7 us -> 17.1 us  [send(): return lax.ppermute(value, ('row', 'col'), pairs)]
  transfers between devices with their start and end apart: 13 -> 17, of which waited for: 7 -> 7; matrix products, arithmetic and copies ran while one was open for 0% -> 0% of each run, Pallas kernels for 12% -> 11%
where the time goes in v2:
time: 54.8 us; the launch traced here: 54.6 us
  waiting for transfers between devices  27.1 us (49%)
  starting transfers between devices  17.1 us (31%)
  Pallas kernels  9.6 us (18%)
  between operations  0.75 us (1%)
    ppermute x17, waiting for transfers between devices, send(): return lax.ppermute(value, ('row', 'col'), pairs)  27.1 us
    ppermute x17, starting transfers between devices, send(): return lax.ppermute(value, ('row', 'col'), pairs)  17.1 us
    pallas_call x6, Pallas kernels, call(): pl.pallas_call(kernel, out_shape=outs, in_specs=specs or [vspec() for _ i...  9.6 us
  transfers between devices with their start and end apart: 17, of which 7 were waited for; matrix products, arithmetic and copies ran while one was open for 0% of the time, Pallas kernels for 11%

profile of v2, /device:TPU:0, one launch (start us, length us, event | category | flops | bytes accessed | tf_op | source)
XLA Modules:
  0.0 54.6 jit_solution(246881900958055978)
XLA Ops:
  0.0 1.2 %shard_map.46 = (bf16[256,256]{1,0:T(8,128)(2,1)S(1)}, bf16[256,768]{1,0:T(8,128)(2,1)S(1)}, f32[256,128]{1,0:T(8,128)S(1)}, bf16[128,768]{1,0:T(8,128)(2,1)S(1)}, bf16[128,768]{1,0:T(8,128)(2,1)S(1)}) custom-call(s32[1,256]{1,0:T(1,128)} %bitcast.1, bf16[256,256]{1,0:T(8,128)(2,1)} %ret_hbm.1, bf16[256,512]{1,0:T(8,128)(2,1)} %w_hbm.1), custom_call_target="tpu_custom_call" | custom-call | tf_op jit(solution)/shard_map/pallas_call | solution.py:108
  1.2 3.0 %collective-permute-start = (bf16[256,256]{1,0:T(8,128)(2,1)S(1)}, bf16[256,256]{1,0:T(8,128)(2,1)S(1)}, u32[]{:S(2)}, u32[]{:S(2)}) collective-permute-start(bf16[256,256]{1,0:T(8,128)(2,1)S(1)} %get-tuple-element.35.refs_0_), channel_id=1, source_target_pairs={{0,8},{1,9},{2,10},{3,11},{4,12},{5,13},{6,14},{7,15},{8,0},{9,1},... | collective-permute-start | bytes 393224 | tf_op jit(solution)/shard_map/ppermute | solution.py:136
  4.3 2.6 %collective-permute-start.3 = (bf16[128,768]{1,0:T(8,128)(2,1)S(1)}, bf16[128,768]{1,0:T(8,128)(2,1)S(1)}, u32[]{:S(2)}, u32[]{:S(2)}) collective-permute-start(bf16[128,768]{1,0:T(8,128)(2,1)S(1)} %get-tuple-element.36), channel_id=1, source_target_pairs={{0,4},{1,5},{2,6},{3,7},{4,0},{5,1},{6,2},{7,3},{8,12},{9,13},{10,... | collective-permute-start | bytes 589832 | tf_op jit(solution)/shard_map/ppermute | solution.py:136
  6.8 1.5 %collective-permute-start.8 = (bf16[256,768]{1,0:T(8,128)(2,1)S(1)}, bf16[256,768]{1,0:T(8,128)(2,1)S(1)}, u32[]{:S(2)}, u32[]{:S(2)}) collective-permute-start(bf16[256,768]{1,0:T(8,128)(2,1)S(1)} %get-tuple-element.44.refs_4_), channel_id=1, source_target_pairs={{0,16},{1,17},{2,18},{3,19},{4,20},{5,21},{6,22},{7,23},{8,24},{9,... | collective-permute-start | bytes 1179656 | tf_op jit(solution)/shard_map/ppermute | solution.py:136
  8.4 1.6 %collective-permute-start.1 = (bf16[256,256]{1,0:T(8,128)(2,1)S(1)}, bf16[256,256]{1,0:T(8,128)(2,1)S(1)}, u32[]{:S(2)}, u32[]{:S(2)}) collective-permute-start(bf16[256,256]{1,0:T(8,128)(2,1)S(1)} %get-tuple-element.35.refs_0_), channel_id=1, source_target_pairs={{0,2},{1,3},{2,0},{3,1},{4,6},{5,7},{6,4},{7,5},{8,10},{9,11},{10,... | collective-permute-start | bytes 393224 | tf_op jit(solution)/shard_map/ppermute | solution.py:136
  9.9 0.0 collective-permute-done.refs_1_
  9.9 0.5 collective-permute-start.2
  10.4 1.8 %collective-permute-start.5 = (bf16[128,768]{1,0:T(8,128)(2,1)S(1)}, bf16[128,768]{1,0:T(8,128)(2,1)S(1)}, u32[]{:S(2)}, u32[]{:S(2)}) collective-permute-start(bf16[128,768]{1,0:T(8,128)(2,1)S(1)} %get-tuple-element.40), channel_id=1, source_target_pairs={{0,4},{1,5},{2,6},{3,7},{4,0},{5,1},{6,2},{7,3},{8,12},{9,13},{10,... | collective-permute-start | bytes 589832 | tf_op jit(solution)/shard_map/ppermute | solution.py:136
  12.2 7.6 %collective-permute-done.1.refs_2_ = bf16[256,256]{1,0:T(8,128)(2,1)S(1)} collective-permute-done((bf16[256,256]{1,0:T(8,128)(2,1)S(1)}, bf16[256,256]{1,0:T(8,128)(2,1)S(1)}, u32[]{:S(2)}, u32[]{:S(2)}) %collective-permute-start.1) | collective-permute-done | bytes 131104 | tf_op jit(solution)/shard_map/ppermute | solution.py:136
  19.8 0.0 collective-permute-done.3.refs_4_
  19.8 1.4 %collective-permute-done.2.refs_3_ = bf16[256,256]{1,0:T(8,128)(2,1)S(1)} collective-permute-done((bf16[256,256]{1,0:T(8,128)(2,1)S(1)}, bf16[256,256]{1,0:T(8,128)(2,1)S(1)}, u32[]{:S(2)}, u32[]{:S(2)}) %collective-permute-start.2) | collective-permute-done | bytes 131104 | tf_op jit(solution)/shard_map/ppermute | solution.py:136
  21.2 0.0 collective-permute-start.6
  21.2 3.0 %collective-permute-done.5.refs_5_ = bf16[128,768]{1,0:T(8,128)(2,1)S(1)} collective-permute-done((bf16[128,768]{1,0:T(8,128)(2,1)S(1)}, bf16[128,768]{1,0:T(8,128)(2,1)S(1)}, u32[]{:S(2)}, u32[]{:S(2)}) %collective-permute-start.5) | collective-permute-done | bytes 196640 | tf_op jit(solution)/shard_map/ppermute | solution.py:136
  24.2 0.0 collective-permute-done.6.refs_6_
  24.2 0.0 collective-permute-start.10
  24.2 0.0 collective-permute-done.8.refs_4_
  24.2 0.5 collective-permute-start.9
  24.7 0.1 collective-permute-start.7
  24.8 1.5 %collective-permute-start.11 = (bf16[128,768]{1,0:T(8,128)(2,1)S(1)}, bf16[128,768]{1,0:T(8,128)(2,1)S(1)}, u32[]{:S(2)}, u32[]{:S(2)}) collective-permute-start(bf16[128,768]{1,0:T(8,128)(2,1)S(1)} %collective-permute-done.5.refs_5_), channel_id=1, source_target_pairs={{0,16},{1,17},{2,18},{3,19},{4,20},{5,21},{6,22},{7,23},{8,24},{9,... | collective-permute-start | bytes 589832 | tf_op jit(solution)/shard_map/ppermute | solution.py:136
  26.3 0.5 collective-permute-start.4
  27.5 0.0 collective-permute-done.10.refs_5_
  27.5 1.6 %shard_map.47 = (f32[256,512]{1,0:T(8,128)S(1)}, f32[256,512]{1,0:T(8,128)S(1)}, f32[256,512]{1,0:T(8,128)S(1)}, f32[256,512]{1,0:T(8,128)S(1)}) custom-call(s32[1]{0:T(128)S(6)} %copy.21.code_ref, bf16[256,256]{1,0:T(8,128)(2,1)S(1)} %get-tuple-element.35.refs_0_, bf16[256,256]{1,0:T(8,128)(2,1)S(1)} %collective-permute-done.refs_1_, ...), custom_call_target="tpu_custom_call" | custom-call | tf_op jit(solution)/shard_map/pallas_call | solution.py:108
  29.1 0.0 collective-permute-done.9.refs_5_
  29.1 2.0 %shard_map.48 = (f32[256,512]{1,0:T(8,128)S(1)}, f32[256,512]{1,0:T(8,128)S(1)}, f32[256,512]{1,0:T(8,128)S(1)}, f32[256,512]{1,0:T(8,128)S(1)}) custom-call(s32[1]{0:T(128)S(6)} %copy.21.code_ref, bf16[256,256]{1,0:T(8,128)(2,1)S(1)} %get-tuple-element.35.refs_0_, ...), custom_call_target="tpu_custom_call", output_to_operand_aliasing={{0}: (7, {}), {1}: (8, {}), {2}: (9, {}), {3}: (10, {})} | custom-call | tf_op jit(solution)/shard_map/pallas_call | solution.py:108
  31.1 0.0 collective-permute-done.7.refs_7_
  31.1 2.3 %shard_map.49 = (f32[256,512]{1,0:T(8,128)S(1)}, f32[256,512]{1,0:T(8,128)S(1)}, f32[256,512]{1,0:T(8,128)S(1)}, f32[256,512]{1,0:T(8,128)S(1)}) custom-call(s32[1]{0:T(128)S(6)} %copy.21.code_ref, bf16[256,256]{1,0:T(8,128)(2,1)S(1)} %get-tuple-element.35.refs_0_, ...), custom_call_target="tpu_custom_call", output_to_operand_aliasing={{0}: (9, {}), {1}: (10, {}), {2}: (11, {}), {3}: (12, {})} | custom-call | tf_op jit(solution)/shard_map/pallas_call | solution.py:108
  33.4 0.0 collective-permute-done.11.refs_5_
  33.4 0.1 collective-permute-start.13
  33.5 2.8 %collective-permute-done.4.refs_4_ = bf16[128,768]{1,0:T(8,128)(2,1)S(1)} collective-permute-done((bf16[128,768]{1,0:T(8,128)(2,1)S(1)}, bf16[128,768]{1,0:T(8,128)(2,1)S(1)}, u32[]{:S(2)}, u32[]{:S(2)}) %collective-permute-start.4) | collective-permute-done | bytes 196640 | tf_op jit(solution)/shard_map/ppermute | solution.py:136
  36.2 0.0 collective-permute-start.12
  36.2 0.0 collective-permute-done.13.refs_7_
  36.3 1.4 %collective-permute-done.12.refs_6_ = bf16[128,768]{1,0:T(8,128)(2,1)S(1)} collective-permute-done((bf16[128,768]{1,0:T(8,128)(2,1)S(1)}, bf16[128,768]{1,0:T(8,128)(2,1)S(1)}, u32[]{:S(2)}, u32[]{:S(2)}) %collective-permute-start.12) | collective-permute-done | bytes 196640 | tf_op jit(solution)/shard_map/ppermute | solution.py:136
  37.7 1.6 %shard_map.50 = (f32[256,512]{1,0:T(8,128)S(1)}, bf16[256,512]{1,0:T(8,128)(2,1)S(1)}, bf16[256,512]{1,0:T(8,128)(2,1)S(1)}, bf16[256,512]{1,0:T(8,128)(2,1)S(1)}) custom-call(s32[1]{0:T(128)S(6)} %copy.21.code_ref, bf16[256,256]{1,0:T(8,128)(2,1)S(1)} %get-tuple-element.35.refs_0_, bf16[256,256]{1,0:T(8,128)(2,1)S(1)} %collective-permute-done.refs_1_, ...), custom_call_target="tpu_custom_call" | custom-call | tf_op jit(solution)/shard_map/pallas_call | solution.py:108
  39.3 0.7 %collective-permute-start.14 = (bf16[256,512]{1,0:T(8,128)(2,1)S(1)}, bf16[256,512]{1,0:T(8,128)(2,1)S(1)}, u32[]{:S(2)}, u32[]{:S(2)}) collective-permute-start(bf16[256,512]{1,0:T(8,128)(2,1)S(1)} %get-tuple-element.60), channel_id=1, source_target_pairs={{0,10},{1,11},{2,8},{3,9},{4,14},{5,15},{6,12},{7,13},{8,2},{9,3},... | collective-permute-start | bytes 786440 | tf_op jit(solution)/shard_map/ppermute | solution.py:136
  40.0 1.5 %collective-permute-start.15 = (bf16[256,512]{1,0:T(8,128)(2,1)S(1)}, bf16[256,512]{1,0:T(8,128)(2,1)S(1)}, u32[]{:S(2)}, u32[]{:S(2)}) collective-permute-start(bf16[256,512]{1,0:T(8,128)(2,1)S(1)} %get-tuple-element.61), channel_id=1, source_target_pairs={{0,8},{1,9},{2,10},{3,11},{4,12},{5,13},{6,14},{7,15},{8,0},{9,1},... | collective-permute-start | bytes 786440 | tf_op jit(solution)/shard_map/ppermute | solution.py:136
  41.5 1.4 %collective-permute-start.16 = (bf16[256,512]{1,0:T(8,128)(2,1)S(1)}, bf16[256,512]{1,0:T(8,128)(2,1)S(1)}, u32[]{:S(2)}, u32[]{:S(2)}) collective-permute-start(bf16[256,512]{1,0:T(8,128)(2,1)S(1)} %get-tuple-element.62), channel_id=1, source_target_pairs={{0,2},{1,3},{2,0},{3,1},{4,6},{5,7},{6,4},{7,5},{8,10},{9,11},{10,... | collective-permute-start | bytes 786440 | tf_op jit(solution)/shard_map/ppermute | solution.py:136
  42.8 6.6 %collective-permute-done.14.refs_1_ = bf16[256,512]{1,0:T(8,128)(2,1)S(1)} collective-permute-done((bf16[256,512]{1,0:T(8,128)(2,1)S(1)}, bf16[256,512]{1,0:T(8,128)(2,1)S(1)}, u32[]{:S(2)}, u32[]{:S(2)}) %collective-permute-start.14) | collective-permute-done | bytes 262176 | tf_op jit(solution)/shard_map/ppermute | solution.py:136
  49.4 4.2 %collective-permute-done.15.refs_2_ = bf16[256,512]{1,0:T(8,128)(2,1)S(1)} collective-permute-done((bf16[256,512]{1,0:T(8,128)(2,1)S(1)}, bf16[256,512]{1,0:T(8,128)(2,1)S(1)}, u32[]{:S(2)}, u32[]{:S(2)}) %collective-permute-start.15) | collective-permute-done | bytes 262176 | tf_op jit(solution)/shard_map/ppermute | solution.py:136
  53.7 0.0 collective-permute-done.16.refs_3_
  53.7 0.9 %shard_map.51 = f32[256,512]{1,0:T(8,128)} custom-call(f32[256,128]{1,0:T(8,128)S(1)} %get-tuple-element.34.sigma_ref, f32[256,512]{1,0:T(8,128)S(1)} %get-tuple-element.59.refs_0_, bf16[256,512]{1,0:T(8,128)(2,1)S(1)} %collective-permute-done.14.refs_1_, bf16[256,512]{1,0:T(8,128)(2,1)S(1)} %collective-permute-done.15.refs_2_, ...), custom_call_target="tpu_custom_call" | custom-call | tf_op jit(solution)/shard_map/pallas_call | solution.py:108
Async XLA Ops:
  1.2 8.7 %collective-permute-start = (bf16[256,256]{1,0:T(8,128)(2,1)S(1)}, bf16[256,256]{1,0:T(8,128)(2,1)S(1)}, u32[]{:S(2)}, u32[]{:S(2)}) collective-permute-start(bf16[256,256]{1,0:T(8,128)(2,1)S(1)} %get-tuple-element.35.refs_0_), channel_id=1, source_target_pairs={{0,8},{1,9},{2,10},{3,11},{4,12},{5,13},{6,14},{7,15},{8,0},{9,1},... | collective-permute-start | bytes 393224 | tf_op jit(solution)/shard_map/ppermute | solution.py:136
  4.3 15.5 %collective-permute-start.3 = (bf16[128,768]{1,0:T(8,128)(2,1)S(1)}, bf16[128,768]{1,0:T(8,128)(2,1)S(1)}, u32[]{:S(2)}, u32[]{:S(2)}) collective-permute-start(bf16[128,768]{1,0:T(8,128)(2,1)S(1)} %get-tuple-element.36), channel_id=1, source_target_pairs={{0,4},{1,5},{2,6},{3,7},{4,0},{5,1},{6,2},{7,3},{8,12},{9,13},{10,... | collective-permute-start | bytes 589832 | tf_op jit(solution)/shard_map/ppermute | solution.py:136
  6.8 17.4 %collective-permute-start.8 = (bf16[256,768]{1,0:T(8,128)(2,1)S(1)}, bf16[256,768]{1,0:T(8,128)(2,1)S(1)}, u32[]{:S(2)}, u32[]{:S(2)}) collective-permute-start(bf16[256,768]{1,0:T(8,128)(2,1)S(1)} %get-tuple-element.44.refs_4_), channel_id=1, source_target_pairs={{0,16},{1,17},{2,18},{3,19},{4,20},{5,21},{6,22},{7,23},{8,24},{9,... | collective-permute-start | bytes 1179656 | tf_op jit(solution)/shard_map/ppermute | solution.py:136
  8.4 11.4 %collective-permute-start.1 = (bf16[256,256]{1,0:T(8,128)(2,1)S(1)}, bf16[256,256]{1,0:T(8,128)(2,1)S(1)}, u32[]{:S(2)}, u32[]{:S(2)}) collective-permute-start(bf16[256,256]{1,0:T(8,128)(2,1)S(1)} %get-tuple-element.35.refs_0_), channel_id=1, source_target_pairs={{0,2},{1,3},{2,0},{3,1},{4,6},{5,7},{6,4},{7,5},{8,10},{9,11},{10,... | collective-permute-start | bytes 393224 | tf_op jit(solution)/shard_map/ppermute | solution.py:136
  9.9 11.2 %collective-permute-start.2 = (bf16[256,256]{1,0:T(8,128)(2,1)S(1)}, bf16[256,256]{1,0:T(8,128)(2,1)S(1)}, u32[]{:S(2)}, u32[]{:S(2)}) collective-permute-start(bf16[256,256]{1,0:T(8,128)(2,1)S(1)} %collective-permute-done.refs_1_), channel_id=1, source_target_pairs={{0,2},{1,3},{2,0},{3,1},{4,6},{5,7},{6,4},{7,5},{8,10},{9,11},{10,... | collective-permute-start | bytes 393224 | tf_op jit(solution)/shard_map/ppermute | solution.py:136
  10.4 13.8 %collective-permute-start.5 = (bf16[128,768]{1,0:T(8,128)(2,1)S(1)}, bf16[128,768]{1,0:T(8,128)(2,1)S(1)}, u32[]{:S(2)}, u32[]{:S(2)}) collective-permute-start(bf16[128,768]{1,0:T(8,128)(2,1)S(1)} %get-tuple-element.40), channel_id=1, source_target_pairs={{0,4},{1,5},{2,6},{3,7},{4,0},{5,1},{6,2},{7,3},{8,12},{9,13},{10,... | collective-permute-start | bytes 589832 | tf_op jit(solution)/shard_map/ppermute | solution.py:136
  21.2 3.0 %collective-permute-start.6 = (bf16[128,768]{1,0:T(8,128)(2,1)S(1)}, bf16[128,768]{1,0:T(8,128)(2,1)S(1)}, u32[]{:S(2)}, u32[]{:S(2)}) collective-permute-start(bf16[128,768]{1,0:T(8,128)(2,1)S(1)} %collective-permute-done.3.refs_4_), channel_id=1, source_target_pairs={{0,1},{1,0},{2,3},{3,2},{4,5},{5,4},{6,7},{7,6},{8,9},{9,8},{10,11... | collective-permute-start | bytes 589832 | tf_op jit(solution)/shard_map/ppermute | solution.py:136
  24.2 3.3 %collective-permute-start.10 = (bf16[256,768]{1,0:T(8,128)(2,1)S(1)}, bf16[256,768]{1,0:T(8,128)(2,1)S(1)}, u32[]{:S(2)}, u32[]{:S(2)}) collective-permute-start(bf16[256,768]{1,0:T(8,128)(2,1)S(1)} %get-tuple-element.44.refs_4_), channel_id=1, source_target_pairs={{0,1},{1,0},{2,3},{3,2},{4,5},{5,4},{6,7},{7,6},{8,9},{9,8},{10,11... | collective-permute-start | bytes 1179656 | tf_op jit(solution)/shard_map/ppermute | solution.py:136
  24.2 4.9 %collective-permute-start.9 = (bf16[256,768]{1,0:T(8,128)(2,1)S(1)}, bf16[256,768]{1,0:T(8,128)(2,1)S(1)}, u32[]{:S(2)}, u32[]{:S(2)}) collective-permute-start(bf16[256,768]{1,0:T(8,128)(2,1)S(1)} %collective-permute-done.8.refs_4_), channel_id=1, source_target_pairs={{0,1},{1,0},{2,3},{3,2},{4,5},{5,4},{6,7},{7,6},{8,9},{9,8},{10,11... | collective-permute-start | bytes 1179656 | tf_op jit(solution)/shard_map/ppermute | solution.py:136
  24.7 6.4 %collective-permute-start.7 = (bf16[128,768]{1,0:T(8,128)(2,1)S(1)}, bf16[128,768]{1,0:T(8,128)(2,1)S(1)}, u32[]{:S(2)}, u32[]{:S(2)}) collective-permute-start(bf16[128,768]{1,0:T(8,128)(2,1)S(1)} %collective-permute-done.5.refs_5_), channel_id=1, source_target_pairs={{0,1},{1,0},{2,3},{3,2},{4,5},{5,4},{6,7},{7,6},{8,9},{9,8},{10,11... | collective-permute-start | bytes 589832 | tf_op jit(solution)/shard_map/ppermute | solution.py:136
  24.8 8.6 %collective-permute-start.11 = (bf16[128,768]{1,0:T(8,128)(2,1)S(1)}, bf16[128,768]{1,0:T(8,128)(2,1)S(1)}, u32[]{:S(2)}, u32[]{:S(2)}) collective-permute-start(bf16[128,768]{1,0:T(8,128)(2,1)S(1)} %collective-permute-done.5.refs_5_), channel_id=1, source_target_pairs={{0,16},{1,17},{2,18},{3,19},{4,20},{5,21},{6,22},{7,23},{8,24},{9,... | collective-permute-start | bytes 589832 | tf_op jit(solution)/shard_map/ppermute | solution.py:136
  26.3 9.9 %collective-permute-start.4 = (bf16[128,768]{1,0:T(8,128)(2,1)S(1)}, bf16[128,768]{1,0:T(8,128)(2,1)S(1)}, u32[]{:S(2)}, u32[]{:S(2)}) collective-permute-start(bf16[128,768]{1,0:T(8,128)(2,1)S(1)} %collective-permute-done.3.refs_4_), channel_id=1, source_target_pairs={{0,16},{1,17},{2,18},{3,19},{4,20},{5,21},{6,22},{7,23},{8,24},{9,... | collective-permute-start | bytes 589832 | tf_op jit(solution)/shard_map/ppermute | solution.py:136
  33.4 2.9 %collective-permute-start.13 = (bf16[128,768]{1,0:T(8,128)(2,1)S(1)}, bf16[128,768]{1,0:T(8,128)(2,1)S(1)}, u32[]{:S(2)}, u32[]{:S(2)}) collective-permute-start(bf16[128,768]{1,0:T(8,128)(2,1)S(1)} %collective-permute-done.11.refs_5_), channel_id=1, source_target_pairs={{0,1},{1,0},{2,3},{3,2},{4,5},{5,4},{6,7},{7,6},{8,9},{9,8},{10,11... | collective-permute-start | bytes 589832 | tf_op jit(solution)/shard_map/ppermute | solution.py:136
  36.2 1.4 %collective-permute-start.12 = (bf16[128,768]{1,0:T(8,128)(2,1)S(1)}, bf16[128,768]{1,0:T(8,128)(2,1)S(1)}, u32[]{:S(2)}, u32[]{:S(2)}) collective-permute-start(bf16[128,768]{1,0:T(8,128)(2,1)S(1)} %collective-permute-done.4.refs_4_), channel_id=1, source_target_pairs={{0,1},{1,0},{2,3},{3,2},{4,5},{5,4},{6,7},{7,6},{8,9},{9,8},{10,11... | collective-permute-start | bytes 589832 | tf_op jit(solution)/shard_map/ppermute | solution.py:136
  39.3 10.2 %collective-permute-start.14 = (bf16[256,512]{1,0:T(8,128)(2,1)S(1)}, bf16[256,512]{1,0:T(8,128)(2,1)S(1)}, u32[]{:S(2)}, u32[]{:S(2)}) collective-permute-start(bf16[256,512]{1,0:T(8,128)(2,1)S(1)} %get-tuple-element.60), channel_id=1, source_target_pairs={{0,10},{1,11},{2,8},{3,9},{4,14},{5,15},{6,12},{7,13},{8,2},{9,3},... | collective-permute-start | bytes 786440 | tf_op jit(solution)/shard_map/ppermute | solution.py:136
  40.0 13.7 %collective-permute-start.15 = (bf16[256,512]{1,0:T(8,128)(2,1)S(1)}, bf16[256,512]{1,0:T(8,128)(2,1)S(1)}, u32[]{:S(2)}, u32[]{:S(2)}) collective-permute-start(bf16[256,512]{1,0:T(8,128)(2,1)S(1)} %get-tuple-element.61), channel_id=1, source_target_pairs={{0,8},{1,9},{2,10},{3,11},{4,12},{5,13},{6,14},{7,15},{8,0},{9,1},... | collective-permute-start | bytes 786440 | tf_op jit(solution)/shard_map/ppermute | solution.py:136
  41.5 12.2 %collective-permute-start.16 = (bf16[256,512]{1,0:T(8,128)(2,1)S(1)}, bf16[256,512]{1,0:T(8,128)(2,1)S(1)}, u32[]{:S(2)}, u32[]{:S(2)}) collective-permute-start(bf16[256,512]{1,0:T(8,128)(2,1)S(1)} %get-tuple-element.62), channel_id=1, source_target_pairs={{0,2},{1,3},{2,0},{3,1},{4,6},{5,7},{6,4},{7,5},{8,10},{9,11},{10,... | collective-permute-start | bytes 786440 | tf_op jit(solution)/shard_map/ppermute | solution.py:136

commit v3 on v2

v3 whole, which is shorter than its diff:
```python
import functools

import jax
import jax.numpy as jnp
from jax import lax
from jax.experimental import pallas as pl
from jax.experimental.pallas import tpu as pltpu
from jax.sharding import PartitionSpec as P

DENOM = 256
VMEM = pltpu.VMEM


def vspec():
    return pl.BlockSpec(memory_space=VMEM)


def prep_kernel(start_hbm, ret_hbm, w_hbm, *refs):
    masked_ref, both_ref, sigma_ref, start_ref, ret_ref, w_ref, sems = refs
    loads = [
        pltpu.make_async_copy(src, dst, sems.at[k])
        for k, (src, dst) in enumerate(((start_hbm, start_ref), (ret_hbm, ret_ref), (w_hbm, w_ref)))
    ]
    for load in loads:
        load.start()
    rows, days = ret_ref.shape
    loads[0].wait()
    loads[1].wait()
    start = jnp.broadcast_to(start_ref[...].astype(jnp.float32), (days, rows)).T
    day = lax.broadcasted_iota(jnp.int32, (rows, days), 1).astype(jnp.float32)
    y = jnp.where(day >= start, ret_ref[...].astype(jnp.float32), 0.0)
    sigma = sigma_of(y)
    sigma_ref[...] = jnp.broadcast_to(sigma, sigma_ref.shape)
    masked = y.astype(jnp.bfloat16)
    masked_ref[...] = masked
    both_ref[:, :days] = masked
    loads[2].wait()
    both_ref[:, days:] = (sigma * w_ref[...].astype(jnp.float32)).astype(jnp.bfloat16)


def sigma_of(y):
    sq = (y * y).astype(jnp.bfloat16).astype(jnp.float32)
    obs = jnp.where(y != 0.0, 1.0, 0.0)
    total = jnp.sum(sq, axis=1, keepdims=True)
    count = jnp.sum(obs, axis=1, keepdims=True)
    return jnp.sqrt(total / jnp.maximum(count, 1.0) + 1e-06)


def nt(a, b):
    return lax.dot_general(a, b, (((1,), (1,)), ((), ())), preferred_element_type=jnp.float32)


def parts_of(y):
    wide = y.astype(jnp.float32)
    obs = jnp.where(wide != 0.0, 1.0, 0.0).astype(jnp.bfloat16)
    return y, obs, (wide * wide).astype(jnp.bfloat16)


def chip_kernel(nrows, pairs, nin, has_diag, code_ref, *refs):
    ncols = sum(pairs)
    row_refs, col_refs = refs[:nrows], refs[nrows:nrows + ncols]
    in_refs, out_refs = refs[nrows + ncols:nrows + ncols + nin], refs[nrows + ncols + nin:]
    own, days = row_refs[0].shape
    delta = code_ref[0].astype(jnp.float32) / DENOM
    keep = 1.0 - delta
    ys, values, at = [], [], 0
    for n in pairs:
        if n == 1:
            ys.append(col_refs[at][:, :days])
            values.append(col_refs[at][:, days:])
        else:
            y = col_refs[at][...]
            ys.append(y)
            sigma = sigma_of(y.astype(jnp.float32))
            values.append((sigma * col_refs[at + 1][...].astype(jnp.float32)).astype(jnp.bfloat16))
        at += n
    cols = [parts_of(y) for y in ys]
    values = jnp.concatenate(values)
    for i, r in enumerate(row_refs):
        ry, ro, rs = parts_of(r[...])
        shrunk = []
        for j, (cy, co, cs) in enumerate(cols):
            cross, left, right = nt(ry, cy), nt(rs, co), nt(ro, cs)
            part = keep * (cross * lax.rsqrt(left * right + 1e-06))
            if has_diag and i == 0 and j == 0:
                a = lax.broadcasted_iota(jnp.int32, part.shape, 0)
                b = lax.broadcasted_iota(jnp.int32, part.shape, 1)
                part = part + jnp.where(a == b, delta, 0.0)
            shrunk.append(part.astype(jnp.bfloat16))
        term = jnp.dot(jnp.concatenate(shrunk, 1), values, preferred_element_type=jnp.float32)
        if nin:
            term = term + in_refs[i][...]
        out_refs[i][...] = term.astype(out_refs[i].dtype)


def final_kernel(sigma_ref, *refs):
    out_ref = refs[-1]
    total = refs[0][...]
    for r in refs[1:-1]:
        total = total + r[...].astype(jnp.float32)
    out_ref[...] = sigma_ref[:, :1] * total


def call(kernel, args, outs, specs=None, scratch=(), aliases=None):
    return pl.pallas_call(
        kernel,
        out_shape=outs,
        in_specs=specs or [vspec() for _ in args],
        out_specs=jax.tree.map(lambda _: vspec(), outs),
        scratch_shapes=scratch,
        input_output_aliases=aliases or {},
        compiler_params=pltpu.CompilerParams(vmem_limit_bytes=48 * 1024 * 1024),
    )(*args)


def after(value, *others):
    return lax.optimization_barrier((value, *others))[0]


def per_device(nrow, ncol, returns, start_day, shrink_code, weights):
    own, days = returns.shape
    ports = weights.shape[1]
    far_y, far_z = nrow // 2, ncol // 4
    ys, zs = range(1, far_y), range(1, far_z)

    def send(value, y=0, x=0, zh=0, zl=0, core=0):
        pairs = []
        for r in range(nrow):
            for c in range(ncol):
                rr = (r // 2 + y) % far_y * 2 + (r % 2 + x) % 2
                cc = (c // 4 + zh) % far_z * 4 + (c // 2 % 2 + zl) % 2 * 2 + (c % 2 + core) % 2
                pairs.append((r * ncol + c, rr * ncol + cc))
        return lax.ppermute(value, ("row", "col"), pairs)

    smem = pl.BlockSpec(memory_space=pltpu.SMEM)
    shape = jax.ShapeDtypeStruct
    masked, both, sigma = call(
        prep_kernel,
        tuple(
            pltpu.with_memory_space_constraint(v, pltpu.HBM)
            for v in (start_day.reshape(1, own), returns, weights)
        ),
        (
            shape((own, days), jnp.bfloat16),
            shape((own, days + ports), jnp.bfloat16),
            shape((own, 128), jnp.float32),
        ),
        [pl.BlockSpec(memory_space=pltpu.HBM)] * 3,
        [
            VMEM((1, own), jnp.int32),
            VMEM((own, days), jnp.bfloat16),
            VMEM((own, ports), jnp.bfloat16),
            pltpu.SemaphoreType.DMA((3,)),
        ],
    )
    total, rows = [], []

    def chip(*pieces, last=False):
        args = (shrink_code, *rows, *(a for p in pieces for a in p), *total)
        nin = len(total)
        kinds = [jnp.float32] + [jnp.bfloat16 if last else jnp.float32] * 3
        total[:] = call(
            functools.partial(chip_kernel, len(rows), tuple(map(len, pieces)), nin, nin == 0),
            args,
            [VMEM((own, ports), kind) for kind in kinds],
            [smem] + [vspec() for _ in args[1:]],
            aliases={len(args) - nin + i: i for i in range(nin)} if not last else None,
        )
        return list(total)

    at = {}
    at["zl"] = [send(masked, zl=1)]
    at["zh_m"] = [send(masked, zh=k) for k in zs]
    at["xzl"] = [send(masked, x=1, zl=1)]
    at["own_s"] = [send(both, core=1)]
    at["zh_w"] = [send(weights, zh=k) for k in zs]
    at["fwd_w"] = [send(after(v, *at["xzl"]), y=k) for v in at["zh_w"] for k in ys]
    at["w_s"] = [send(v, core=1) for v in at["zh_w"]]
    at["x"] = [send(masked, x=1)]
    at["near"] = [send(both, y=k) for k in ys]
    at["near_s"] = [send(after(v, *at["zl"]), core=1) for v in at["near"]]
    at["fwd_m"] = [send(after(v, *at["near_s"], *at["w_s"]), y=k) for v in at["zh_m"] for k in ys]
    rows += [masked, at["x"][0], at["zl"][0], at["xzl"][0]]
    at["K1"] = chip((both,), (at["own_s"][0],))
    for a, b in zip(at["near"], at["near_s"]):
        at["K2"] = chip((after(a, *at["zh_m"]),), (b,))
    at["m_s"] = [send(after(v, *at["K1"]), core=1) for v in at["zh_m"]]
    for a, b, p, q in zip(at["zh_m"], at["zh_w"], at["m_s"], at["w_s"]):
        at["K3"] = chip((a, b), (p, q))
    at["fw_s"] = [send(after(v, *at["m_s"], *at["K3"], *at["zh_m"]), core=1) for v in at["fwd_w"]]
    at["fm_s"] = [send(after(v, *at["K3"]), core=1) for v in at["fwd_m"]]
    tail = list(zip(at["fwd_m"], at["fwd_w"], at["fm_s"], at["fw_s"]))
    for k, (a, b, p, q) in enumerate(tail):
        chip((a, b), (p, q), last=k == len(tail) - 1)

    arrived = [total[0]]
    for i, x, zl in ((3, 1, 1), (1, 1, 0), (2, 0, 1)):
        arrived.append(send(total[i], x=x, zl=zl))
    return call(final_kernel, (sigma, *arrived), shape((own, ports), jnp.float32))


def solution(mesh):
    in_specs = (P(("col", "row"), None), P(("col", "row")), P(), P(("col", "row"), None))
    out_specs = P(("col", "row"), None)
    body = functools.partial(per_device, mesh.shape["row"], mesh.shape["col"])
    return jax.shard_map(
        body, mesh=mesh, in_specs=in_specs, out_specs=out_specs, check_vma=False
    )
```

time: 54.8 us -> 52.1 us (0.951)
  waiting for transfers between devices: 27.1 us -> 22.7 us
  starting transfers between devices: 17.1 us -> 18.9 us
    ppermute x17, waiting for transfers between devices: 27.1 us -> 22.7 us  [send(): return lax.ppermute(value, ('row', 'col'), pairs)]
    ppermute x17, starting transfers between devices: 17.1 us -> 18.9 us  [send(): return lax.ppermute(value, ('row', 'col'), pairs)]
  transfers between devices with their start and end apart: 17 -> 17, of which waited for: 7 -> 8; matrix products, arithmetic and copies ran while one was open for 0% -> 0% of each run, Pallas kernels for 11% -> 11%
where the time goes in v3:
time: 52.1 us; the launch traced here: 52 us
  waiting for transfers between devices  22.7 us (44%)
  starting transfers between devices  18.9 us (36%)
  Pallas kernels  9.56 us (18%)
  between operations  0.74 us (1%)
    ppermute x17, waiting for transfers between devices, send(): return lax.ppermute(value, ('row', 'col'), pairs)  22.7 us
    ppermute x17, starting transfers between devices, send(): return lax.ppermute(value, ('row', 'col'), pairs)  18.9 us
    pallas_call x6, Pallas kernels, call(): pl.pallas_call(kernel, out_shape=outs, in_specs=specs or [vspec() for _ i...  9.56 us
  transfers between devices with their start and end apart: 17, of which 8 were waited for; matrix products, arithmetic and copies ran while one was open for 0% of the time, Pallas kernels for 11%

profile of v3, /device:TPU:0, one launch (start us, length us, event | category | flops | bytes accessed | tf_op | source)
XLA Modules:
  0.0 52.0 jit_solution(12537294386919699167)
XLA Ops:
  0.0 0.0 copy-start
  0.0 1.3 %shard_map.46 = (bf16[256,256]{1,0:T(8,128)(2,1)S(1)}, bf16[256,768]{1,0:T(8,128)(2,1)S(1)}, f32[256,128]{1,0:T(8,128)S(1)}) custom-call(s32[1,256]{1,0:T(1,128)} %bitcast.1, bf16[256,256]{1,0:T(8,128)(2,1)} %ret_hbm.1, bf16[256,512]{1,0:T(8,128)(2,1)} %w_hbm.1), custom_call_target="tpu_custom_call" | custom-call | tf_op jit(solution)/shard_map/pallas_call | solution.py:105
  1.3 3.0 %collective-permute-start.4 = (bf16[256,768]{1,0:T(8,128)(2,1)S(1)}, bf16[256,768]{1,0:T(8,128)(2,1)S(1)}, u32[]{:S(2)}, u32[]{:S(2)}) collective-permute-start(bf16[256,768]{1,0:T(8,128)(2,1)S(1)} %get-tuple-element.33.refs_4_), channel_id=1, source_target_pairs={{0,16},{1,17},{2,18},{3,19},{4,20},{5,21},{6,22},{7,23},{8,24},{9,... | collective-permute-start | bytes 1179656 | tf_op jit(solution)/shard_map/ppermute | solution.py:133
  4.3 1.6 %collective-permute-start.1 = (bf16[256,256]{1,0:T(8,128)(2,1)S(1)}, bf16[256,256]{1,0:T(8,128)(2,1)S(1)}, u32[]{:S(2)}, u32[]{:S(2)}) collective-permute-start(bf16[256,256]{1,0:T(8,128)(2,1)S(1)} %get-tuple-element.32.refs_0_), channel_id=1, source_target_pairs={{0,2},{1,3},{2,0},{3,1},{4,6},{5,7},{6,4},{7,5},{8,10},{9,11},{10,... | collective-permute-start | bytes 393224 | tf_op jit(solution)/shard_map/ppermute | solution.py:133
  5.9 0.0 collective-permute-start.10
  5.9 0.0 copy-done
  5.9 2.6 %collective-permute-start.6 = (bf16[256,512]{1,0:T(8,128)(2,1)S(1)}, bf16[256,512]{1,0:T(8,128)(2,1)S(1)}, u32[]{:S(2)}, u32[]{:S(2)}) collective-permute-start(bf16[256,512]{1,0:T(8,128)(2,1)S(1)} %copy-done), channel_id=1, source_target_pairs={{0,4},{1,5},{2,6},{3,7},{4,0},{5,1},{6,2},{7,3},{8,12},{9,13},{10,... | collective-permute-start | bytes 786440 | tf_op jit(solution)/shard_map/ppermute | solution.py:133
  8.5 1.4 %collective-permute-start.2 = (bf16[256,256]{1,0:T(8,128)(2,1)S(1)}, bf16[256,256]{1,0:T(8,128)(2,1)S(1)}, u32[]{:S(2)}, u32[]{:S(2)}) collective-permute-start(bf16[256,256]{1,0:T(8,128)(2,1)S(1)} %get-tuple-element.32.refs_0_), channel_id=1, source_target_pairs={{0,10},{1,11},{2,8},{3,9},{4,14},{5,15},{6,12},{7,13},{8,2},{9,3},... | collective-permute-start | bytes 393224 | tf_op jit(solution)/shard_map/ppermute | solution.py:133
  9.9 0.0 collective-permute-done.1.refs_2_
  9.9 3.6 %collective-permute-done.4.refs_4_ = bf16[256,768]{1,0:T(8,128)(2,1)S(1)} collective-permute-done((bf16[256,768]{1,0:T(8,128)(2,1)S(1)}, bf16[256,768]{1,0:T(8,128)(2,1)S(1)}, u32[]{:S(2)}, u32[]{:S(2)}) %collective-permute-start.4) | collective-permute-done | bytes 393248 | tf_op jit(solution)/shard_map/ppermute | solution.py:133
  13.4 0.0 collective-permute-start.5
  13.4 1.7 %collective-permute-start = (bf16[256,256]{1,0:T(8,128)(2,1)S(1)}, bf16[256,256]{1,0:T(8,128)(2,1)S(1)}, u32[]{:S(2)}, u32[]{:S(2)}) collective-permute-start(bf16[256,256]{1,0:T(8,128)(2,1)S(1)} %get-tuple-element.32.refs_0_), channel_id=1, source_target_pairs={{0,8},{1,9},{2,10},{3,11},{4,12},{5,13},{6,14},{7,15},{8,0},{9,1},... | collective-permute-start | bytes 393224 | tf_op jit(solution)/shard_map/ppermute | solution.py:133
  15.1 2.4 %collective-permute-done.2.refs_3_ = bf16[256,256]{1,0:T(8,128)(2,1)S(1)} collective-permute-done((bf16[256,256]{1,0:T(8,128)(2,1)S(1)}, bf16[256,256]{1,0:T(8,128)(2,1)S(1)}, u32[]{:S(2)}, u32[]{:S(2)}) %collective-permute-start.2) | collective-permute-done | bytes 131104 | tf_op jit(solution)/shard_map/ppermute | solution.py:133
  17.6 3.7 %collective-permute-start.3 = (bf16[256,256]{1,0:T(8,128)(2,1)S(1)}, bf16[256,256]{1,0:T(8,128)(2,1)S(1)}, u32[]{:S(2)}, u32[]{:S(2)}) collective-permute-start(bf16[256,256]{1,0:T(8,128)(2,1)S(1)} %get-tuple-element.32.refs_0_), channel_id=1, source_target_pairs={{0,4},{1,5},{2,6},{3,7},{4,0},{5,1},{6,2},{7,3},{8,12},{9,13},{10,... | collective-permute-start | bytes 393224 | tf_op jit(solution)/shard_map/ppermute | solution.py:133
  21.3 0.0 collective-permute-done.6.refs_5_
  21.3 0.0 collective-permute-start.7
  21.3 0.0 collective-permute-done.refs_1_
  21.3 0.6 %collective-permute-start.9 = (bf16[256,512]{1,0:T(8,128)(2,1)S(1)}, bf16[256,512]{1,0:T(8,128)(2,1)S(1)}, u32[]{:S(2)}, u32[]{:S(2)}) collective-permute-start(bf16[256,512]{1,0:T(8,128)(2,1)S(1)} %collective-permute-done.6.refs_5_), channel_id=1, source_target_pairs={{0,16},{1,17},{2,18},{3,19},{4,20},{5,21},{6,22},{7,23},{8,24},{9,... | collective-permute-start | bytes 786440 | tf_op jit(solution)/shard_map/ppermute | solution.py:133
  22.5 0.0 collective-permute-done.10.refs_5_
  22.6 1.6 %shard_map.47 = (f32[256,512]{1,0:T(8,128)S(1)}, f32[256,512]{1,0:T(8,128)S(1)}, f32[256,512]{1,0:T(8,128)S(1)}, f32[256,512]{1,0:T(8,128)S(1)}) custom-call(s32[1]{0:T(128)S(6)} %copy.21.code_ref, bf16[256,256]{1,0:T(8,128)(2,1)S(1)} %get-tuple-element.32.refs_0_, bf16[256,256]{1,0:T(8,128)(2,1)S(1)} %collective-permute-done.refs_1_, ...), custom_call_target="tpu_custom_call" | custom-call | tf_op jit(solution)/shard_map/pallas_call | solution.py:105
  24.1 2.9 %collective-permute-done.3.refs_4_ = bf16[256,256]{1,0:T(8,128)(2,1)S(1)} collective-permute-done((bf16[256,256]{1,0:T(8,128)(2,1)S(1)}, bf16[256,256]{1,0:T(8,128)(2,1)S(1)}, u32[]{:S(2)}, u32[]{:S(2)}) %collective-permute-start.3) | collective-permute-done | bytes 131104 | tf_op jit(solution)/shard_map/ppermute | solution.py:133
  27.1 0.0 collective-permute-start.11
  27.1 0.0 collective-permute-done.7.refs_7_
  27.1 0.0 collective-permute-done.5.refs_5_
  27.1 0.6 %collective-permute-start.8 = (bf16[256,256]{1,0:T(8,128)(2,1)S(1)}, bf16[256,256]{1,0:T(8,128)(2,1)S(1)}, u32[]{:S(2)}, u32[]{:S(2)}) collective-permute-start(bf16[256,256]{1,0:T(8,128)(2,1)S(1)} %collective-permute-done.3.refs_4_), channel_id=1, source_target_pairs={{0,16},{1,17},{2,18},{3,19},{4,20},{5,21},{6,22},{7,23},{8,24},{9,... | collective-permute-start | bytes 393224 | tf_op jit(solution)/shard_map/ppermute | solution.py:133
  27.6 2.0 %shard_map.48 = (f32[256,512]{1,0:T(8,128)S(1)}, f32[256,512]{1,0:T(8,128)S(1)}, f32[256,512]{1,0:T(8,128)S(1)}, f32[256,512]{1,0:T(8,128)S(1)}) custom-call(s32[1]{0:T(128)S(6)} %copy.21.code_ref, bf16[256,256]{1,0:T(8,128)(2,1)S(1)} %get-tuple-element.32.refs_0_, ...), custom_call_target="tpu_custom_call", output_to_operand_aliasing={{0}: (7, {}), {1}: (8, {}), {2}: (9, {}), {3}: (10, {})} | custom-call | tf_op jit(solution)/shard_map/pallas_call | solution.py:105
  29.7 0.0 collective-permute-done.11.refs_6_
  29.7 2.1 %shard_map.49 = (f32[256,512]{1,0:T(8,128)S(1)}, f32[256,512]{1,0:T(8,128)S(1)}, f32[256,512]{1,0:T(8,128)S(1)}, f32[256,512]{1,0:T(8,128)S(1)}) custom-call(s32[1]{0:T(128)S(6)} %copy.21.code_ref, bf16[256,256]{1,0:T(8,128)(2,1)S(1)} %get-tuple-element.32.refs_0_, ...), custom_call_target="tpu_custom_call", output_to_operand_aliasing={{0}: (9, {}), {1}: (10, {}), {2}: (11, {}), {3}: (12, {})} | custom-call | tf_op jit(solution)/shard_map/pallas_call | solution.py:105
  31.7 0.0 collective-permute-done.9.refs_5_
  31.7 0.2 collective-permute-start.13
  32.0 1.0 %collective-permute-done.8.refs_4_ = bf16[256,256]{1,0:T(8,128)(2,1)S(1)} collective-permute-done((bf16[256,256]{1,0:T(8,128)(2,1)S(1)}, bf16[256,256]{1,0:T(8,128)(2,1)S(1)}, u32[]{:S(2)}, u32[]{:S(2)}) %collective-permute-start.8) | collective-permute-done | bytes 131104 | tf_op jit(solution)/shard_map/ppermute | solution.py:133
  33.0 0.0 collective-permute-start.12
  33.0 0.3 collective-permute-done.13.refs_7_
  33.3 1.0 %collective-permute-done.12.refs_6_ = bf16[256,256]{1,0:T(8,128)(2,1)S(1)} collective-permute-done((bf16[256,256]{1,0:T(8,128)(2,1)S(1)}, bf16[256,256]{1,0:T(8,128)(2,1)S(1)}, u32[]{:S(2)}, u32[]{:S(2)}) %collective-permute-start.12) | collective-permute-done | bytes 131104 | tf_op jit(solution)/shard_map/ppermute | solution.py:133
  34.3 1.7 %shard_map.50 = (f32[256,512]{1,0:T(8,128)S(1)}, bf16[256,512]{1,0:T(8,128)(2,1)S(1)}, bf16[256,512]{1,0:T(8,128)(2,1)S(1)}, bf16[256,512]{1,0:T(8,128)(2,1)S(1)}) custom-call(s32[1]{0:T(128)S(6)} %copy.21.code_ref, bf16[256,256]{1,0:T(8,128)(2,1)S(1)} %get-tuple-element.32.refs_0_, bf16[256,256]{1,0:T(8,128)(2,1)S(1)} %collective-permute-done.refs_1_, ...), custom_call_target="tpu_custom_call" | custom-call | tf_op jit(solution)/shard_map/pallas_call | solution.py:105
  36.1 2.2 %collective-permute-start.14 = (bf16[256,512]{1,0:T(8,128)(2,1)S(1)}, bf16[256,512]{1,0:T(8,128)(2,1)S(1)}, u32[]{:S(2)}, u32[]{:S(2)}) collective-permute-start(bf16[256,512]{1,0:T(8,128)(2,1)S(1)} %get-tuple-element.54), channel_id=1, source_target_pairs={{0,10},{1,11},{2,8},{3,9},{4,14},{5,15},{6,12},{7,13},{8,2},{9,3},... | collective-permute-start | bytes 786440 | tf_op jit(solution)/shard_map/ppermute | solution.py:133
  38.2 1.0 %collective-permute-start.15 = (bf16[256,512]{1,0:T(8,128)(2,1)S(1)}, bf16[256,512]{1,0:T(8,128)(2,1)S(1)}, u32[]{:S(2)}, u32[]{:S(2)}) collective-permute-start(bf16[256,512]{1,0:T(8,128)(2,1)S(1)} %get-tuple-element.55), channel_id=1, source_target_pairs={{0,8},{1,9},{2,10},{3,11},{4,12},{5,13},{6,14},{7,15},{8,0},{9,1},... | collective-permute-start | bytes 786440 | tf_op jit(solution)/shard_map/ppermute | solution.py:133
  39.2 0.4 collective-permute-start.16
  39.6 6.6 %collective-permute-done.14.refs_1_ = bf16[256,512]{1,0:T(8,128)(2,1)S(1)} collective-permute-done((bf16[256,512]{1,0:T(8,128)(2,1)S(1)}, bf16[256,512]{1,0:T(8,128)(2,1)S(1)}, u32[]{:S(2)}, u32[]{:S(2)}) %collective-permute-start.14) | collective-permute-done | bytes 262176 | tf_op jit(solution)/shard_map/ppermute | solution.py:133
  46.2 4.8 %collective-permute-done.15.refs_2_ = bf16[256,512]{1,0:T(8,128)(2,1)S(1)} collective-permute-done((bf16[256,512]{1,0:T(8,128)(2,1)S(1)}, bf16[256,512]{1,0:T(8,128)(2,1)S(1)}, u32[]{:S(2)}, u32[]{:S(2)}) %collective-permute-start.15) | collective-permute-done | bytes 262176 | tf_op jit(solution)/shard_map/ppermute | solution.py:133
  51.0 0.0 collective-permute-done.16.refs_3_
  51.0 0.9 %shard_map.51 = f32[256,512]{1,0:T(8,128)} custom-call(f32[256,128]{1,0:T(8,128)S(1)} %get-tuple-element.31.sigma_ref, f32[256,512]{1,0:T(8,128)S(1)} %get-tuple-element.53.refs_0_, bf16[256,512]{1,0:T(8,128)(2,1)S(1)} %collective-permute-done.14.refs_1_, bf16[256,512]{1,0:T(8,128)(2,1)S(1)} %collective-permute-done.15.refs_2_, ...), custom_call_target="tpu_custom_call" | custom-call | tf_op jit(solution)/shard_map/pallas_call | solution.py:105
Async XLA Ops:
  0.0 5.9 %copy-start = (bf16[256,512]{1,0:T(8,128)(2,1)S(1)}, bf16[256,512]{1,0:T(8,128)(2,1)}, u32[]{:S(2)}) copy-start(bf16[256,512]{1,0:T(8,128)(2,1)} %w_hbm.1) | copy-start | bytes 786436
  1.3 12.1 %collective-permute-start.4 = (bf16[256,768]{1,0:T(8,128)(2,1)S(1)}, bf16[256,768]{1,0:T(8,128)(2,1)S(1)}, u32[]{:S(2)}, u32[]{:S(2)}) collective-permute-start(bf16[256,768]{1,0:T(8,128)(2,1)S(1)} %get-tuple-element.33.refs_4_), channel_id=1, source_target_pairs={{0,16},{1,17},{2,18},{3,19},{4,20},{5,21},{6,22},{7,23},{8,24},{9,... | collective-permute-start | bytes 1179656 | tf_op jit(solution)/shard_map/ppermute | solution.py:133
  4.3 5.6 %collective-permute-start.1 = (bf16[256,256]{1,0:T(8,128)(2,1)S(1)}, bf16[256,256]{1,0:T(8,128)(2,1)S(1)}, u32[]{:S(2)}, u32[]{:S(2)}) collective-permute-start(bf16[256,256]{1,0:T(8,128)(2,1)S(1)} %get-tuple-element.32.refs_0_), channel_id=1, source_target_pairs={{0,2},{1,3},{2,0},{3,1},{4,6},{5,7},{6,4},{7,5},{8,10},{9,11},{10,... | collective-permute-start | bytes 393224 | tf_op jit(solution)/shard_map/ppermute | solution.py:133
  5.9 16.7 %collective-permute-start.10 = (bf16[256,768]{1,0:T(8,128)(2,1)S(1)}, bf16[256,768]{1,0:T(8,128)(2,1)S(1)}, u32[]{:S(2)}, u32[]{:S(2)}) collective-permute-start(bf16[256,768]{1,0:T(8,128)(2,1)S(1)} %get-tuple-element.33.refs_4_), channel_id=1, source_target_pairs={{0,1},{1,0},{2,3},{3,2},{4,5},{5,4},{6,7},{7,6},{8,9},{9,8},{10,11... | collective-permute-start | bytes 1179656 | tf_op jit(solution)/shard_map/ppermute | solution.py:133
  5.9 15.4 %collective-permute-start.6 = (bf16[256,512]{1,0:T(8,128)(2,1)S(1)}, bf16[256,512]{1,0:T(8,128)(2,1)S(1)}, u32[]{:S(2)}, u32[]{:S(2)}) collective-permute-start(bf16[256,512]{1,0:T(8,128)(2,1)S(1)} %copy-done), channel_id=1, source_target_pairs={{0,4},{1,5},{2,6},{3,7},{4,0},{5,1},{6,2},{7,3},{8,12},{9,13},{10,... | collective-permute-start | bytes 786440 | tf_op jit(solution)/shard_map/ppermute | solution.py:133
  8.5 9.1 %collective-permute-start.2 = (bf16[256,256]{1,0:T(8,128)(2,1)S(1)}, bf16[256,256]{1,0:T(8,128)(2,1)S(1)}, u32[]{:S(2)}, u32[]{:S(2)}) collective-permute-start(bf16[256,256]{1,0:T(8,128)(2,1)S(1)} %get-tuple-element.32.refs_0_), channel_id=1, source_target_pairs={{0,10},{1,11},{2,8},{3,9},{4,14},{5,15},{6,12},{7,13},{8,2},{9,3},... | collective-permute-start | bytes 393224 | tf_op jit(solution)/shard_map/ppermute | solution.py:133
  13.4 13.7 %collective-permute-start.5 = (bf16[256,768]{1,0:T(8,128)(2,1)S(1)}, bf16[256,768]{1,0:T(8,128)(2,1)S(1)}, u32[]{:S(2)}, u32[]{:S(2)}) collective-permute-start(bf16[256,768]{1,0:T(8,128)(2,1)S(1)} %collective-permute-done.4.refs_4_), channel_id=1, source_target_pairs={{0,1},{1,0},{2,3},{3,2},{4,5},{5,4},{6,7},{7,6},{8,9},{9,8},{10,11... | collective-permute-start | bytes 1179656 | tf_op jit(solution)/shard_map/ppermute | solution.py:133
  13.4 7.9 %collective-permute-start = (bf16[256,256]{1,0:T(8,128)(2,1)S(1)}, bf16[256,256]{1,0:T(8,128)(2,1)S(1)}, u32[]{:S(2)}, u32[]{:S(2)}) collective-permute-start(bf16[256,256]{1,0:T(8,128)(2,1)S(1)} %get-tuple-element.32.refs_0_), channel_id=1, source_target_pairs={{0,8},{1,9},{2,10},{3,11},{4,12},{5,13},{6,14},{7,15},{8,0},{9,1},... | collective-permute-start | bytes 393224 | tf_op jit(solution)/shard_map/ppermute | solution.py:133
  17.6 9.5 %collective-permute-start.3 = (bf16[256,256]{1,0:T(8,128)(2,1)S(1)}, bf16[256,256]{1,0:T(8,128)(2,1)S(1)}, u32[]{:S(2)}, u32[]{:S(2)}) collective-permute-start(bf16[256,256]{1,0:T(8,128)(2,1)S(1)} %get-tuple-element.32.refs_0_), channel_id=1, source_target_pairs={{0,4},{1,5},{2,6},{3,7},{4,0},{5,1},{6,2},{7,3},{8,12},{9,13},{10,... | collective-permute-start | bytes 393224 | tf_op jit(solution)/shard_map/ppermute | solution.py:133
  21.3 5.8 %collective-permute-start.7 = (bf16[256,512]{1,0:T(8,128)(2,1)S(1)}, bf16[256,512]{1,0:T(8,128)(2,1)S(1)}, u32[]{:S(2)}, u32[]{:S(2)}) collective-permute-start(bf16[256,512]{1,0:T(8,128)(2,1)S(1)} %collective-permute-done.6.refs_5_), channel_id=1, source_target_pairs={{0,1},{1,0},{2,3},{3,2},{4,5},{5,4},{6,7},{7,6},{8,9},{9,8},{10,11... | collective-permute-start | bytes 786440 | tf_op jit(solution)/shard_map/ppermute | solution.py:133
  21.3 10.4 %collective-permute-start.9 = (bf16[256,512]{1,0:T(8,128)(2,1)S(1)}, bf16[256,512]{1,0:T(8,128)(2,1)S(1)}, u32[]{:S(2)}, u32[]{:S(2)}) collective-permute-start(bf16[256,512]{1,0:T(8,128)(2,1)S(1)} %collective-permute-done.6.refs_5_), channel_id=1, source_target_pairs={{0,16},{1,17},{2,18},{3,19},{4,20},{5,21},{6,22},{7,23},{8,24},{9,... | collective-permute-start | bytes 786440 | tf_op jit(solution)/shard_map/ppermute | solution.py:133
  27.1 2.6 %collective-permute-start.11 = (bf16[256,256]{1,0:T(8,128)(2,1)S(1)}, bf16[256,256]{1,0:T(8,128)(2,1)S(1)}, u32[]{:S(2)}, u32[]{:S(2)}) collective-permute-start(bf16[256,256]{1,0:T(8,128)(2,1)S(1)} %collective-permute-done.3.refs_4_), channel_id=1, source_target_pairs={{0,1},{1,0},{2,3},{3,2},{4,5},{5,4},{6,7},{7,6},{8,9},{9,8},{10,11... | collective-permute-start | bytes 393224 | tf_op jit(solution)/shard_map/ppermute | solution.py:133
  27.1 5.9 %collective-permute-start.8 = (bf16[256,256]{1,0:T(8,128)(2,1)S(1)}, bf16[256,256]{1,0:T(8,128)(2,1)S(1)}, u32[]{:S(2)}, u32[]{:S(2)}) collective-permute-start(bf16[256,256]{1,0:T(8,128)(2,1)S(1)} %collective-permute-done.3.refs_4_), channel_id=1, source_target_pairs={{0,16},{1,17},{2,18},{3,19},{4,20},{5,21},{6,22},{7,23},{8,24},{9,... | collective-permute-start | bytes 393224 | tf_op jit(solution)/shard_map/ppermute | solution.py:133
  31.7 1.6 %collective-permute-start.13 = (bf16[256,512]{1,0:T(8,128)(2,1)S(1)}, bf16[256,512]{1,0:T(8,128)(2,1)S(1)}, u32[]{:S(2)}, u32[]{:S(2)}) collective-permute-start(bf16[256,512]{1,0:T(8,128)(2,1)S(1)} %collective-permute-done.9.refs_5_), channel_id=1, source_target_pairs={{0,1},{1,0},{2,3},{3,2},{4,5},{5,4},{6,7},{7,6},{8,9},{9,8},{10,11... | collective-permute-start | bytes 786440 | tf_op jit(solution)/shard_map/ppermute | solution.py:133
  33.0 1.3 %collective-permute-start.12 = (bf16[256,256]{1,0:T(8,128)(2,1)S(1)}, bf16[256,256]{1,0:T(8,128)(2,1)S(1)}, u32[]{:S(2)}, u32[]{:S(2)}) collective-permute-start(bf16[256,256]{1,0:T(8,128)(2,1)S(1)} %collective-permute-done.8.refs_4_), channel_id=1, source_target_pairs={{0,1},{1,0},{2,3},{3,2},{4,5},{5,4},{6,7},{7,6},{8,9},{9,8},{10,11... | collective-permute-start | bytes 393224 | tf_op jit(solution)/shard_map/ppermute | solution.py:133
  36.1 10.2 %collective-permute-start.14 = (bf16[256,512]{1,0:T(8,128)(2,1)S(1)}, bf16[256,512]{1,0:T(8,128)(2,1)S(1)}, u32[]{:S(2)}, u32[]{:S(2)}) collective-permute-start(bf16[256,512]{1,0:T(8,128)(2,1)S(1)} %get-tuple-element.54), channel_id=1, source_target_pairs={{0,10},{1,11},{2,8},{3,9},{4,14},{5,15},{6,12},{7,13},{8,2},{9,3},... | collective-permute-start | bytes 786440 | tf_op jit(solution)/shard_map/ppermute | solution.py:133
  38.2 12.8 %collective-permute-start.15 = (bf16[256,512]{1,0:T(8,128)(2,1)S(1)}, bf16[256,512]{1,0:T(8,128)(2,1)S(1)}, u32[]{:S(2)}, u32[]{:S(2)}) collective-permute-start(bf16[256,512]{1,0:T(8,128)(2,1)S(1)} %get-tuple-element.55), channel_id=1, source_target_pairs={{0,8},{1,9},{2,10},{3,11},{4,12},{5,13},{6,14},{7,15},{8,0},{9,1},... | collective-permute-start | bytes 786440 | tf_op jit(solution)/shard_map/ppermute | solution.py:133
  39.2 11.8 %collective-permute-start.16 = (bf16[256,512]{1,0:T(8,128)(2,1)S(1)}, bf16[256,512]{1,0:T(8,128)(2,1)S(1)}, u32[]{:S(2)}, u32[]{:S(2)}) collective-permute-start(bf16[256,512]{1,0:T(8,128)(2,1)S(1)} %get-tuple-element.56), channel_id=1, source_target_pairs={{0,2},{1,3},{2,0},{3,1},{4,6},{5,7},{6,4},{7,5},{8,10},{9,11},{10,... | collective-permute-start | bytes 786440 | tf_op jit(solution)/shard_map/ppermute | solution.py:133

commit v4 on v3

--- a/solution.py
+++ b/solution.py
@@ -156,39 +156,45 @@
     total, rows = [], []
 
     def chip(*pieces, last=False):
-        args = (shrink_code, *rows, *(a for p in pieces for a in p), *total)
-        nin = len(total)
-        kinds = [jnp.float32] + [jnp.bfloat16 if last else jnp.float32] * 3
-        total[:] = call(
-            functools.partial(chip_kernel, len(rows), tuple(map(len, pieces)), nin, nin == 0),
-            args,
-            [VMEM((own, ports), kind) for kind in kinds],
-            [smem] + [vspec() for _ in args[1:]],
-            aliases={len(args) - nin + i: i for i in range(nin)} if not last else None,
-        )
+        first = not total
+        new = {}
+        for part in ((3,), (1, 2, 0)) if last else (range(4),):
+            into = [] if first else [total[i] for i in part]
+            args = (shrink_code, *(rows[i] for i in part), *(a for p in pieces for a in p), *into)
+            kinds = [jnp.bfloat16 if last and i else jnp.float32 for i in part]
+            made = call(
+                functools.partial(chip_kernel, len(part), tuple(map(len, pieces)), len(into), first),
+                args,
+                [VMEM((own, ports), kind) for kind in kinds],
+                [smem] + [vspec() for _ in args[1:]],
+                aliases=None if last else {len(args) - len(into) + k: k for k in range(len(into))},
+            )
+            new.update(zip(part, made))
+        total[:] = [new[i] for i in range(4)]
         return list(total)
 
     at = {}
+    at["zh_w"] = [send(weights, zh=k) for k in zs]
+    at["zh_m"] = [send(masked, zh=k) for k in zs]
+    at["near_w"] = [send(weights, y=k) for k in ys]
+    at["near_m"] = [send(masked, y=k) for k in ys]
+    at["fwd_w"] = [send(v, y=k) for v in at["zh_w"] for k in ys]
+    at["m_s"] = [send(v, core=1) for v in at["zh_m"]]
+    at["w_s"] = [send(after(v, *at["zh_m"]), core=1) for v in at["zh_w"]]
+    at["nw_s"] = [send(v, core=1) for v in at["near_w"]]
     at["zl"] = [send(masked, zl=1)]
-    at["zh_m"] = [send(masked, zh=k) for k in zs]
-    at["xzl"] = [send(masked, x=1, zl=1)]
-    at["own_s"] = [send(both, core=1)]
-    at["zh_w"] = [send(weights, zh=k) for k in zs]
-    at["fwd_w"] = [send(after(v, *at["xzl"]), y=k) for v in at["zh_w"] for k in ys]
-    at["w_s"] = [send(v, core=1) for v in at["zh_w"]]
-    at["x"] = [send(masked, x=1)]
-    at["near"] = [send(both, y=k) for k in ys]
-    at["near_s"] = [send(after(v, *at["zl"]), core=1) for v in at["near"]]
-    at["fwd_m"] = [send(after(v, *at["near_s"], *at["w_s"]), y=k) for v in at["zh_m"] for k in ys]
+    at["x"] = [send(after(masked, *at["zl"]), x=1)]
+    at["own_s"] = [send(after(both, *at["near_m"], *at["zl"]), core=1)]
+    at["xzl"] = [send(at["x"][0], zl=1)]
+    at["nm_s"] = [send(after(v, *at["zl"]), core=1) for v in at["near_m"]]
+    at["fwd_m"] = [send(after(v, *at["xzl"]), y=k) for v in at["zh_m"] for k in ys]
     rows += [masked, at["x"][0], at["zl"][0], at["xzl"][0]]
-    at["K1"] = chip((both,), (at["own_s"][0],))
-    for a, b in zip(at["near"], at["near_s"]):
-        at["K2"] = chip((after(a, *at["zh_m"]),), (b,))
-    at["m_s"] = [send(after(v, *at["K1"]), core=1) for v in at["zh_m"]]
+    at["K1"] = chip((after(both, *at["zh_w"]),), (at["own_s"][0],), *zip((*at["near_m"], *at["nm_s"]), (*at["near_w"], *at["nw_s"])))
+    at["K2"] = at["K1"]
+    at["fw_s"] = [send(v, core=1) for v in at["fwd_w"]]
     for a, b, p, q in zip(at["zh_m"], at["zh_w"], at["m_s"], at["w_s"]):
         at["K3"] = chip((a, b), (p, q))
-    at["fw_s"] = [send(after(v, *at["m_s"], *at["K3"], *at["zh_m"]), core=1) for v in at["fwd_w"]]
-    at["fm_s"] = [send(after(v, *at["K3"]), core=1) for v in at["fwd_m"]]
+    at["fm_s"] = [send(after(v, *at["K2"]), core=1) for v in at["fwd_m"]]
     tail = list(zip(at["fwd_m"], at["fwd_w"], at["fm_s"], at["fw_s"]))
     for k, (a, b, p, q) in enumerate(tail):
         chip((a, b), (p, q), last=k == len(tail) - 1)

time: 52.1 us -> 49.3 us (0.946)
  waiting for transfers between devices: 22.7 us -> 17.9 us
  starting transfers between devices: 18.9 us -> 21.1 us
    ppermute x17 -> x19, waiting for transfers between devices: 22.7 us -> 17.9 us  [send(): return lax.ppermute(value, ('row', 'col'), pairs)]
    ppermute x17 -> x19, starting transfers between devices: 18.9 us -> 21.1 us  [send(): return lax.ppermute(value, ('row', 'col'), pairs)]
  transfers between devices with their start and end apart: 17 -> 19, of which waited for: 8 -> 6; matrix products, arithmetic and copies ran while one was open for 0% -> 0% of each run, Pallas kernels for 11% -> 16%
where the time goes in v4:
time: 49.3 us; the launch traced here: 49.1 us
  starting transfers between devices  21.1 us (43%)
  waiting for transfers between devices  17.9 us (36%)
  Pallas kernels  9.42 us (19%)
  between operations  0.74 us (2%)
    ppermute x19, starting transfers between devices, send(): return lax.ppermute(value, ('row', 'col'), pairs)  21.1 us
    ppermute x19, waiting for transfers between devices, send(): return lax.ppermute(value, ('row', 'col'), pairs)  17.9 us
    pallas_call x6, Pallas kernels, call(): pl.pallas_call(kernel, out_shape=outs, in_specs=specs or [vspec() for _ i...  9.42 us
  transfers between devices with their start and end apart: 19, of which 6 were waited for; matrix products, arithmetic and copies ran while one was open for 0% of the time, Pallas kernels for 16%

profile of v4, /device:TPU:0, one launch (start us, length us, event | category | flops | bytes accessed | tf_op | source)
XLA Modules:
  0.0 49.1 jit_solution(15062664504527320994)
XLA Ops:
  0.0 0.0 copy-start
  0.0 4.0 %collective-permute-start.5 = (bf16[256,512]{1,0:T(8,128)(2,1)}, bf16[256,512]{1,0:T(8,128)(2,1)S(1)}, u32[]{:S(2)}, u32[]{:S(2)}) collective-permute-start(bf16[256,512]{1,0:T(8,128)(2,1)} %w_hbm.1), channel_id=1, source_target_pairs={{0,4},{1,5},{2,6},{3,7},{4,0},{5,1},{6,2},{7,3},{8,12},{9,13},{10,... | collective-permute-start | bytes 786440 | tf_op jit(solution)/shard_map/ppermute | solution.py:133
  4.0 1.2 %shard_map.46 = (bf16[256,256]{1,0:T(8,128)(2,1)S(1)}, bf16[256,768]{1,0:T(8,128)(2,1)S(1)}, f32[256,128]{1,0:T(8,128)S(1)}) custom-call(s32[1,256]{1,0:T(1,128)} %bitcast.1, bf16[256,256]{1,0:T(8,128)(2,1)} %ret_hbm.1, bf16[256,512]{1,0:T(8,128)(2,1)} %w_hbm.1), custom_call_target="tpu_custom_call" | custom-call | tf_op jit(solution)/shard_map/pallas_call | solution.py:105
  5.3 1.6 %collective-permute-start = (bf16[256,256]{1,0:T(8,128)(2,1)S(1)}, bf16[256,256]{1,0:T(8,128)(2,1)S(1)}, u32[]{:S(2)}, u32[]{:S(2)}) collective-permute-start(bf16[256,256]{1,0:T(8,128)(2,1)S(1)} %get-tuple-element.28.refs_0_.refs_2_), channel_id=1, source_target_pairs={{0,2},{1,3},{2,0},{3,1},{4,6},{5,7},{6,4},{7,5},{8,10},{9,11},{10,... | collective-permute-start | bytes 393224 | tf_op jit(solution)/shard_map/ppermute | solution.py:133
  6.9 1.5 %collective-permute-start.7 = (bf16[256,256]{1,0:T(8,128)(2,1)S(1)}, bf16[256,256]{1,0:T(8,128)(2,1)S(1)}, u32[]{:S(2)}, u32[]{:S(2)}) collective-permute-start(bf16[256,256]{1,0:T(8,128)(2,1)S(1)} %get-tuple-element.28.refs_0_.refs_2_), channel_id=1, source_target_pairs={{0,16},{1,17},{2,18},{3,19},{4,20},{5,21},{6,22},{7,23},{8,24},{9,... | collective-permute-start | bytes 393224 | tf_op jit(solution)/shard_map/ppermute | solution.py:133
  8.4 0.0 copy-done
  8.4 0.5 %collective-permute-start.9 = (bf16[256,512]{1,0:T(8,128)(2,1)S(1)}, bf16[256,512]{1,0:T(8,128)(2,1)S(1)}, u32[]{:S(2)}, u32[]{:S(2)}) collective-permute-start(bf16[256,512]{1,0:T(8,128)(2,1)S(1)} %copy-done), channel_id=1, source_target_pairs={{0,16},{1,17},{2,18},{3,19},{4,20},{5,21},{6,22},{7,23},{8,24},{9,... | collective-permute-start | bytes 786440 | tf_op jit(solution)/shard_map/ppermute | solution.py:133
  8.9 3.7 %collective-permute-done.refs_2_.refs_1_ = bf16[256,256]{1,0:T(8,128)(2,1)S(1)} collective-permute-done((bf16[256,256]{1,0:T(8,128)(2,1)S(1)}, bf16[256,256]{1,0:T(8,128)(2,1)S(1)}, u32[]{:S(2)}, u32[]{:S(2)}) %collective-permute-start) | collective-permute-done | bytes 131104 | tf_op jit(solution)/shard_map/ppermute | solution.py:133
  12.7 1.5 %collective-permute-start.1 = (bf16[256,256]{1,0:T(8,128)(2,1)S(1)}, bf16[256,256]{1,0:T(8,128)(2,1)S(1)}, u32[]{:S(2)}, u32[]{:S(2)}) collective-permute-start(bf16[256,256]{1,0:T(8,128)(2,1)S(1)} %get-tuple-element.28.refs_0_.refs_2_), channel_id=1, source_target_pairs={{0,8},{1,9},{2,10},{3,11},{4,12},{5,13},{6,14},{7,15},{8,0},{9,1},... | collective-permute-start | bytes 393224 | tf_op jit(solution)/shard_map/ppermute | solution.py:133
  14.2 0.0 collective-permute-done.7.refs_6_
  14.2 0.0 collective-permute-start.8
  14.2 2.4 %collective-permute-start.2 = (bf16[256,256]{1,0:T(8,128)(2,1)S(1)}, bf16[256,256]{1,0:T(8,128)(2,1)S(1)}, u32[]{:S(2)}, u32[]{:S(2)}) collective-permute-start(bf16[256,256]{1,0:T(8,128)(2,1)S(1)} %get-tuple-element.28.refs_0_.refs_2_), channel_id=1, source_target_pairs={{0,4},{1,5},{2,6},{3,7},{4,0},{5,1},{6,2},{7,3},{8,12},{9,13},{10,... | collective-permute-start | bytes 393224 | tf_op jit(solution)/shard_map/ppermute | solution.py:133
  16.6 0.0 collective-permute-done.5.refs_5_
  16.6 1.5 %collective-permute-start.6 = (bf16[256,512]{1,0:T(8,128)(2,1)S(1)}, bf16[256,512]{1,0:T(8,128)(2,1)S(1)}, u32[]{:S(2)}, u32[]{:S(2)}) collective-permute-start(bf16[256,512]{1,0:T(8,128)(2,1)S(1)} %collective-permute-done.5.refs_5_), channel_id=1, source_target_pairs={{0,16},{1,17},{2,18},{3,19},{4,20},{5,21},{6,22},{7,23},{8,24},{9,... | collective-permute-start | bytes 786440 | tf_op jit(solution)/shard_map/ppermute | solution.py:133
  18.1 0.0 collective-permute-done.1.refs_1_.refs_0_
  18.1 2.0 %collective-permute-start.3 = (bf16[256,256]{1,0:T(8,128)(2,1)S(1)}, bf16[256,256]{1,0:T(8,128)(2,1)S(1)}, u32[]{:S(2)}, u32[]{:S(2)}) collective-permute-start(bf16[256,256]{1,0:T(8,128)(2,1)S(1)} %collective-permute-done.1.refs_1_.refs_0_), channel_id=1, source_target_pairs={{0,2},{1,3},{2,0},{3,1},{4,6},{5,7},{6,4},{7,5},{8,10},{9,11},{10,... | collective-permute-start | bytes 393224 | tf_op jit(solution)/shard_map/ppermute | solution.py:133
  20.1 0.0 collective-permute-done.9.refs_7_
  20.1 0.0 collective-permute-start.11
  20.1 3.8 %collective-permute-done.2.refs_4_ = bf16[256,256]{1,0:T(8,128)(2,1)S(1)} collective-permute-done((bf16[256,256]{1,0:T(8,128)(2,1)S(1)}, bf16[256,256]{1,0:T(8,128)(2,1)S(1)}, u32[]{:S(2)}, u32[]{:S(2)}) %collective-permute-start.2) | collective-permute-done | bytes 131104 | tf_op jit(solution)/shard_map/ppermute | solution.py:133
  23.9 0.0 collective-permute-start.10
  23.9 0.3 collective-permute-done.3.refs_3_.refs_0_
  24.2 1.2 %collective-permute-start.4 = (bf16[256,256]{1,0:T(8,128)(2,1)S(1)}, bf16[256,256]{1,0:T(8,128)(2,1)S(1)}, u32[]{:S(2)}, u32[]{:S(2)}) collective-permute-start(bf16[256,256]{1,0:T(8,128)(2,1)S(1)} %collective-permute-done.2.refs_4_), channel_id=1, source_target_pairs={{0,16},{1,17},{2,18},{3,19},{4,20},{5,21},{6,22},{7,23},{8,24},{9,... | collective-permute-start | bytes 393224 | tf_op jit(solution)/shard_map/ppermute | solution.py:133
  25.4 0.0 collective-permute-done.10.refs_8_
  25.4 0.2 collective-permute-start.15
  25.6 0.0 collective-permute-done.6.refs_4_.refs_2_
  25.6 0.3 collective-permute-start.13
  26.6 0.0 collective-permute-done.8.refs_5_
  26.6 0.3 collective-permute-start.14
  26.9 0.0 collective-permute-done.11.refs_9_
  26.9 3.1 %shard_map.47 = (f32[256,512]{1,0:T(8,128)S(1)}, f32[256,512]{1,0:T(8,128)S(1)}, f32[256,512]{1,0:T(8,128)S(1)}, f32[256,512]{1,0:T(8,128)S(1)}) custom-call(s32[1]{0:T(128)S(6)} %copy.13.code_ref, bf16[256,256]{1,0:T(8,128)(2,1)S(1)} %get-tuple-element.28.refs_0_.refs_2_, bf16[256,256]{1,0:T(8,128)(2,1)S(1)} %collective-permute-done.1.refs_1_.refs_0_, ...), custom_call_target="tpu_custom_call" | custom-call | tf_op jit(solution)/shard_map/pallas_call | solution.py:105
  30.0 0.0 collective-permute-done.4.refs_3_.refs_1_
  30.0 0.3 collective-permute-start.12
  30.3 0.0 collective-permute-done.14.refs_6_
  30.3 0.0 collective-permute-done.15.refs_7_
  30.3 2.0 %shard_map.48 = (f32[256,512]{1,0:T(8,128)S(1)}, f32[256,512]{1,0:T(8,128)S(1)}, f32[256,512]{1,0:T(8,128)S(1)}, f32[256,512]{1,0:T(8,128)S(1)}) custom-call(s32[1]{0:T(128)S(6)} %copy.13.code_ref, bf16[256,256]{1,0:T(8,128)(2,1)S(1)} %get-tuple-element.28.refs_0_.refs_2_, ...), custom_call_target="tpu_custom_call", output_to_operand_aliasing={{0}: (9, {}), {1}: (10, {}), {2}: (11, {}), {3}: (12, {})} | custom-call | tf_op jit(solution)/shard_map/pallas_call | solution.py:105
  32.4 0.0 collective-permute-done.12.refs_5_.refs_3_
  32.4 0.0 collective-permute-done.13.refs_6_.refs_4_
  32.4 0.7 %shard_map.50 = bf16[256,512]{1,0:T(8,128)(2,1)S(1)} custom-call(s32[1]{0:T(128)S(6)} %copy.13.code_ref, bf16[256,256]{1,0:T(8,128)(2,1)S(1)} %collective-permute-done.3.refs_3_.refs_0_, bf16[256,256]{1,0:T(8,128)(2,1)S(1)} %collective-permute-done.4.refs_3_.refs_1_, bf16[256,512]{1,0:T(8,128)(2,1)S(1)} %collective-permute-done.6.refs_4_.refs_2_, ...), custom_call_target="tpu_custom_call" | custom-call | tf_op jit(solution)/shard_map/pallas_call | solution.py:105
  33.1 2.2 %collective-permute-start.16 = (bf16[256,512]{1,0:T(8,128)(2,1)S(1)}, bf16[256,512]{1,0:T(8,128)(2,1)S(1)}, u32[]{:S(2)}, u32[]{:S(2)}) collective-permute-start(bf16[256,512]{1,0:T(8,128)(2,1)S(1)} %shard_map.50), channel_id=1, source_target_pairs={{0,10},{1,11},{2,8},{3,9},{4,14},{5,15},{6,12},{7,13},{8,2},{9,3},... | collective-permute-start | bytes 786440 | tf_op jit(solution)/shard_map/ppermute | solution.py:133
  35.4 1.4 %shard_map.49 = (bf16[256,512]{1,0:T(8,128)(2,1)S(1)}, bf16[256,512]{1,0:T(8,128)(2,1)S(1)}, f32[256,512]{1,0:T(8,128)S(1)}) custom-call(s32[1]{0:T(128)S(6)} %copy.13.code_ref, bf16[256,256]{1,0:T(8,128)(2,1)S(1)} %collective-permute-done.1.refs_1_.refs_0_, bf16[256,256]{1,0:T(8,128)(2,1)S(1)} %collective-permute-done.refs_2_.refs_1_, ...), custom_call_target="tpu_custom_call" | custom-call | tf_op jit(solution)/shard_map/pallas_call | solution.py:105
  36.8 0.8 %collective-permute-start.17 = (bf16[256,512]{1,0:T(8,128)(2,1)S(1)}, bf16[256,512]{1,0:T(8,128)(2,1)S(1)}, u32[]{:S(2)}, u32[]{:S(2)}) collective-permute-start(bf16[256,512]{1,0:T(8,128)(2,1)S(1)} %get-tuple-element.45), channel_id=1, source_target_pairs={{0,8},{1,9},{2,10},{3,11},{4,12},{5,13},{6,14},{7,15},{8,0},{9,1},... | collective-permute-start | bytes 786440 | tf_op jit(solution)/shard_map/ppermute | solution.py:133
  37.6 0.6 %collective-permute-start.18 = (bf16[256,512]{1,0:T(8,128)(2,1)S(1)}, bf16[256,512]{1,0:T(8,128)(2,1)S(1)}, u32[]{:S(2)}, u32[]{:S(2)}) collective-permute-start(bf16[256,512]{1,0:T(8,128)(2,1)S(1)} %get-tuple-element.46), channel_id=1, source_target_pairs={{0,2},{1,3},{2,0},{3,1},{4,6},{5,7},{6,4},{7,5},{8,10},{9,11},{10,... | collective-permute-start | bytes 786440 | tf_op jit(solution)/shard_map/ppermute | solution.py:133
  38.2 5.1 %collective-permute-done.16.refs_1_ = bf16[256,512]{1,0:T(8,128)(2,1)S(1)} collective-permute-done((bf16[256,512]{1,0:T(8,128)(2,1)S(1)}, bf16[256,512]{1,0:T(8,128)(2,1)S(1)}, u32[]{:S(2)}, u32[]{:S(2)}) %collective-permute-start.16) | collective-permute-done | bytes 262176 | tf_op jit(solution)/shard_map/ppermute | solution.py:133
  43.3 4.9 %collective-permute-done.17.refs_2_ = bf16[256,512]{1,0:T(8,128)(2,1)S(1)} collective-permute-done((bf16[256,512]{1,0:T(8,128)(2,1)S(1)}, bf16[256,512]{1,0:T(8,128)(2,1)S(1)}, u32[]{:S(2)}, u32[]{:S(2)}) %collective-permute-start.17) | collective-permute-done | bytes 262176 | tf_op jit(solution)/shard_map/ppermute | solution.py:133
  48.2 0.1 collective-permute-done.18.refs_3_
  48.2 0.9 %shard_map.51 = f32[256,512]{1,0:T(8,128)} custom-call(f32[256,128]{1,0:T(8,128)S(1)} %get-tuple-element.26.sigma_ref, f32[256,512]{1,0:T(8,128)S(1)} %get-tuple-element.43.refs_0_, bf16[256,512]{1,0:T(8,128)(2,1)S(1)} %collective-permute-done.16.refs_1_, bf16[256,512]{1,0:T(8,128)(2,1)S(1)} %collective-permute-done.17.refs_2_, ...), custom_call_target="tpu_custom_call" | custom-call | tf_op jit(solution)/shard_map/pallas_call | solution.py:105
Async XLA Ops:
  0.0 8.4 %copy-start = (bf16[256,512]{1,0:T(8,128)(2,1)S(1)}, bf16[256,512]{1,0:T(8,128)(2,1)}, u32[]{:S(2)}) copy-start(bf16[256,512]{1,0:T(8,128)(2,1)} %w_hbm.1) | copy-start | bytes 786436
  0.0 16.6 %collective-permute-start.5 = (bf16[256,512]{1,0:T(8,128)(2,1)}, bf16[256,512]{1,0:T(8,128)(2,1)S(1)}, u32[]{:S(2)}, u32[]{:S(2)}) collective-permute-start(bf16[256,512]{1,0:T(8,128)(2,1)} %w_hbm.1), channel_id=1, source_target_pairs={{0,4},{1,5},{2,6},{3,7},{4,0},{5,1},{6,2},{7,3},{8,12},{9,13},{10,... | collective-permute-start | bytes 786440 | tf_op jit(solution)/shard_map/ppermute | solution.py:133
  5.3 7.4 %collective-permute-start = (bf16[256,256]{1,0:T(8,128)(2,1)S(1)}, bf16[256,256]{1,0:T(8,128)(2,1)S(1)}, u32[]{:S(2)}, u32[]{:S(2)}) collective-permute-start(bf16[256,256]{1,0:T(8,128)(2,1)S(1)} %get-tuple-element.28.refs_0_.refs_2_), channel_id=1, source_target_pairs={{0,2},{1,3},{2,0},{3,1},{4,6},{5,7},{6,4},{7,5},{8,10},{9,11},{10,... | collective-permute-start | bytes 393224 | tf_op jit(solution)/shard_map/ppermute | solution.py:133
  6.9 7.2 %collective-permute-start.7 = (bf16[256,256]{1,0:T(8,128)(2,1)S(1)}, bf16[256,256]{1,0:T(8,128)(2,1)S(1)}, u32[]{:S(2)}, u32[]{:S(2)}) collective-permute-start(bf16[256,256]{1,0:T(8,128)(2,1)S(1)} %get-tuple-element.28.refs_0_.refs_2_), channel_id=1, source_target_pairs={{0,16},{1,17},{2,18},{3,19},{4,20},{5,21},{6,22},{7,23},{8,24},{9,... | collective-permute-start | bytes 393224 | tf_op jit(solution)/shard_map/ppermute | solution.py:133
  8.4 11.7 %collective-permute-start.9 = (bf16[256,512]{1,0:T(8,128)(2,1)S(1)}, bf16[256,512]{1,0:T(8,128)(2,1)S(1)}, u32[]{:S(2)}, u32[]{:S(2)}) collective-permute-start(bf16[256,512]{1,0:T(8,128)(2,1)S(1)} %copy-done), channel_id=1, source_target_pairs={{0,16},{1,17},{2,18},{3,19},{4,20},{5,21},{6,22},{7,23},{8,24},{9,... | collective-permute-start | bytes 786440 | tf_op jit(solution)/shard_map/ppermute | solution.py:133
  12.7 5.4 %collective-permute-start.1 = (bf16[256,256]{1,0:T(8,128)(2,1)S(1)}, bf16[256,256]{1,0:T(8,128)(2,1)S(1)}, u32[]{:S(2)}, u32[]{:S(2)}) collective-permute-start(bf16[256,256]{1,0:T(8,128)(2,1)S(1)} %get-tuple-element.28.refs_0_.refs_2_), channel_id=1, source_target_pairs={{0,8},{1,9},{2,10},{3,11},{4,12},{5,13},{6,14},{7,15},{8,0},{9,1},... | collective-permute-start | bytes 393224 | tf_op jit(solution)/shard_map/ppermute | solution.py:133
  14.2 12.4 %collective-permute-start.8 = (bf16[256,768]{1,0:T(8,128)(2,1)S(1)}, bf16[256,768]{1,0:T(8,128)(2,1)S(1)}, u32[]{:S(2)}, u32[]{:S(2)}) collective-permute-start(bf16[256,768]{1,0:T(8,128)(2,1)S(1)} %get-tuple-element.32.refs_4_), channel_id=1, source_target_pairs={{0,1},{1,0},{2,3},{3,2},{4,5},{5,4},{6,7},{7,6},{8,9},{9,8},{10,11... | collective-permute-start | bytes 1179656 | tf_op jit(solution)/shard_map/ppermute | solution.py:133
  14.2 9.7 %collective-permute-start.2 = (bf16[256,256]{1,0:T(8,128)(2,1)S(1)}, bf16[256,256]{1,0:T(8,128)(2,1)S(1)}, u32[]{:S(2)}, u32[]{:S(2)}) collective-permute-start(bf16[256,256]{1,0:T(8,128)(2,1)S(1)} %get-tuple-element.28.refs_0_.refs_2_), channel_id=1, source_target_pairs={{0,4},{1,5},{2,6},{3,7},{4,0},{5,1},{6,2},{7,3},{8,12},{9,13},{10,... | collective-permute-start | bytes 393224 | tf_op jit(solution)/shard_map/ppermute | solution.py:133
  16.6 9.1 %collective-permute-start.6 = (bf16[256,512]{1,0:T(8,128)(2,1)S(1)}, bf16[256,512]{1,0:T(8,128)(2,1)S(1)}, u32[]{:S(2)}, u32[]{:S(2)}) collective-permute-start(bf16[256,512]{1,0:T(8,128)(2,1)S(1)} %collective-permute-done.5.refs_5_), channel_id=1, source_target_pairs={{0,16},{1,17},{2,18},{3,19},{4,20},{5,21},{6,22},{7,23},{8,24},{9,... | collective-permute-start | bytes 786440 | tf_op jit(solution)/shard_map/ppermute | solution.py:133
  18.1 6.1 %collective-permute-start.3 = (bf16[256,256]{1,0:T(8,128)(2,1)S(1)}, bf16[256,256]{1,0:T(8,128)(2,1)S(1)}, u32[]{:S(2)}, u32[]{:S(2)}) collective-permute-start(bf16[256,256]{1,0:T(8,128)(2,1)S(1)} %collective-permute-done.1.refs_1_.refs_0_), channel_id=1, source_target_pairs={{0,2},{1,3},{2,0},{3,1},{4,6},{5,7},{6,4},{7,5},{8,10},{9,11},{10,... | collective-permute-start | bytes 393224 | tf_op jit(solution)/shard_map/ppermute | solution.py:133
  20.1 6.7 %collective-permute-start.11 = (bf16[256,512]{1,0:T(8,128)(2,1)S(1)}, bf16[256,512]{1,0:T(8,128)(2,1)S(1)}, u32[]{:S(2)}, u32[]{:S(2)}) collective-permute-start(bf16[256,512]{1,0:T(8,128)(2,1)S(1)} %collective-permute-done.9.refs_7_), channel_id=1, source_target_pairs={{0,1},{1,0},{2,3},{3,2},{4,5},{5,4},{6,7},{7,6},{8,9},{9,8},{10,11... | collective-permute-start | bytes 786440 | tf_op jit(solution)/shard_map/ppermute | solution.py:133
  23.9 1.5 %collective-permute-start.10 = (bf16[256,256]{1,0:T(8,128)(2,1)S(1)}, bf16[256,256]{1,0:T(8,128)(2,1)S(1)}, u32[]{:S(2)}, u32[]{:S(2)}) collective-permute-start(bf16[256,256]{1,0:T(8,128)(2,1)S(1)} %collective-permute-done.7.refs_6_), channel_id=1, source_target_pairs={{0,1},{1,0},{2,3},{3,2},{4,5},{5,4},{6,7},{7,6},{8,9},{9,8},{10,11... | collective-permute-start | bytes 393224 | tf_op jit(solution)/shard_map/ppermute | solution.py:133
  24.2 5.8 %collective-permute-start.4 = (bf16[256,256]{1,0:T(8,128)(2,1)S(1)}, bf16[256,256]{1,0:T(8,128)(2,1)S(1)}, u32[]{:S(2)}, u32[]{:S(2)}) collective-permute-start(bf16[256,256]{1,0:T(8,128)(2,1)S(1)} %collective-permute-done.2.refs_4_), channel_id=1, source_target_pairs={{0,16},{1,17},{2,18},{3,19},{4,20},{5,21},{6,22},{7,23},{8,24},{9,... | collective-permute-start | bytes 393224 | tf_op jit(solution)/shard_map/ppermute | solution.py:133
  25.4 5.0 %collective-permute-start.15 = (bf16[256,512]{1,0:T(8,128)(2,1)S(1)}, bf16[256,512]{1,0:T(8,128)(2,1)S(1)}, u32[]{:S(2)}, u32[]{:S(2)}) collective-permute-start(bf16[256,512]{1,0:T(8,128)(2,1)S(1)} %collective-permute-done.5.refs_5_), channel_id=1, source_target_pairs={{0,1},{1,0},{2,3},{3,2},{4,5},{5,4},{6,7},{7,6},{8,9},{9,8},{10,11... | collective-permute-start | bytes 786440 | tf_op jit(solution)/shard_map/ppermute | solution.py:133
  25.6 6.8 %collective-permute-start.13 = (bf16[256,512]{1,0:T(8,128)(2,1)S(1)}, bf16[256,512]{1,0:T(8,128)(2,1)S(1)}, u32[]{:S(2)}, u32[]{:S(2)}) collective-permute-start(bf16[256,512]{1,0:T(8,128)(2,1)S(1)} %collective-permute-done.6.refs_4_.refs_2_), channel_id=1, source_target_pairs={{0,1},{1,0},{2,3},{3,2},{4,5},{5,4},{6,7},{7,6},{8,9},{9,8},{10,11... | collective-permute-start | bytes 786440 | tf_op jit(solution)/shard_map/ppermute | solution.py:133
  26.6 3.8 %collective-permute-start.14 = (bf16[256,256]{1,0:T(8,128)(2,1)S(1)}, bf16[256,256]{1,0:T(8,128)(2,1)S(1)}, u32[]{:S(2)}, u32[]{:S(2)}) collective-permute-start(bf16[256,256]{1,0:T(8,128)(2,1)S(1)} %collective-permute-done.2.refs_4_), channel_id=1, source_target_pairs={{0,1},{1,0},{2,3},{3,2},{4,5},{5,4},{6,7},{7,6},{8,9},{9,8},{10,11... | collective-permute-start | bytes 393224 | tf_op jit(solution)/shard_map/ppermute | solution.py:133
  30.0 2.4 %collective-permute-start.12 = (bf16[256,256]{1,0:T(8,128)(2,1)S(1)}, bf16[256,256]{1,0:T(8,128)(2,1)S(1)}, u32[]{:S(2)}, u32[]{:S(2)}) collective-permute-start(bf16[256,256]{1,0:T(8,128)(2,1)S(1)} %collective-permute-done.4.refs_3_.refs_1_), channel_id=1, source_target_pairs={{0,1},{1,0},{2,3},{3,2},{4,5},{5,4},{6,7},{7,6},{8,9},{9,8},{10,11... | collective-permute-start | bytes 393224 | tf_op jit(solution)/shard_map/ppermute | solution.py:133
  33.1 10.2 %collective-permute-start.16 = (bf16[256,512]{1,0:T(8,128)(2,1)S(1)}, bf16[256,512]{1,0:T(8,128)(2,1)S(1)}, u32[]{:S(2)}, u32[]{:S(2)}) collective-permute-start(bf16[256,512]{1,0:T(8,128)(2,1)S(1)} %shard_map.50), channel_id=1, source_target_pairs={{0,10},{1,11},{2,8},{3,9},{4,14},{5,15},{6,12},{7,13},{8,2},{9,3},... | collective-permute-start | bytes 786440 | tf_op jit(solution)/shard_map/ppermute | solution.py:133
  36.8 11.4 %collective-permute-start.17 = (bf16[256,512]{1,0:T(8,128)(2,1)S(1)}, bf16[256,512]{1,0:T(8,128)(2,1)S(1)}, u32[]{:S(2)}, u32[]{:S(2)}) collective-permute-start(bf16[256,512]{1,0:T(8,128)(2,1)S(1)} %get-tuple-element.45), channel_id=1, source_target_pairs={{0,8},{1,9},{2,10},{3,11},{4,12},{5,13},{6,14},{7,15},{8,0},{9,1},... | collective-permute-start | bytes 786440 | tf_op jit(solution)/shard_map/ppermute | solution.py:133
  37.6 10.6 %collective-permute-start.18 = (bf16[256,512]{1,0:T(8,128)(2,1)S(1)}, bf16[256,512]{1,0:T(8,128)(2,1)S(1)}, u32[]{:S(2)}, u32[]{:S(2)}) collective-permute-start(bf16[256,512]{1,0:T(8,128)(2,1)S(1)} %get-tuple-element.46), channel_id=1, source_target_pairs={{0,2},{1,3},{2,0},{3,1},{4,6},{5,7},{6,4},{7,5},{8,10},{9,11},{10,... | collective-permute-start | bytes 786440 | tf_op jit(solution)/shard_map/ppermute | solution.py:133

commit v5 on v4

--- a/solution.py
+++ b/solution.py
@@ -178,16 +178,16 @@
     at["zh_m"] = [send(masked, zh=k) for k in zs]
     at["near_w"] = [send(weights, y=k) for k in ys]
     at["near_m"] = [send(masked, y=k) for k in ys]
+    at["x"] = [send(masked, x=1)]
+    at["xzl"] = [send(at["x"][0], zl=1)]
     at["fwd_w"] = [send(v, y=k) for v in at["zh_w"] for k in ys]
+    at["nm_s"] = [send(v, core=1) for v in at["near_m"]]
     at["m_s"] = [send(v, core=1) for v in at["zh_m"]]
+    at["fwd_m"] = [send(after(v, *at["xzl"]), y=k) for v in at["zh_m"] for k in ys]
     at["w_s"] = [send(after(v, *at["zh_m"]), core=1) for v in at["zh_w"]]
     at["nw_s"] = [send(v, core=1) for v in at["near_w"]]
     at["zl"] = [send(masked, zl=1)]
-    at["x"] = [send(after(masked, *at["zl"]), x=1)]
     at["own_s"] = [send(after(both, *at["near_m"], *at["zl"]), core=1)]
-    at["xzl"] = [send(at["x"][0], zl=1)]
-    at["nm_s"] = [send(after(v, *at["zl"]), core=1) for v in at["near_m"]]
-    at["fwd_m"] = [send(after(v, *at["xzl"]), y=k) for v in at["zh_m"] for k in ys]
     rows += [masked, at["x"][0], at["zl"][0], at["xzl"][0]]
     at["K1"] = chip((after(both, *at["zh_w"]),), (at["own_s"][0],), *zip((*at["near_m"], *at["nm_s"]), (*at["near_w"], *at["nw_s"])))
     at["K2"] = at["K1"]

time: 49.3 us -> 48.6 us (0.986)
  starting transfers between devices: 21.1 us -> 18.6 us
  waiting for transfers between devices: 17.9 us -> 19.7 us
    ppermute x19, starting transfers between devices: 21.1 us -> 18.6 us  [send(): return lax.ppermute(value, ('row', 'col'), pairs)]
    ppermute x19, waiting for transfers between devices: 17.9 us -> 19.7 us  [send(): return lax.ppermute(value, ('row', 'col'), pairs)]
  transfers between devices with their start and end apart: 19 -> 19, of which waited for: 6 -> 8; matrix products, arithmetic and copies ran while one was open for 0% -> 0% of each run, Pallas kernels for 16% -> 16%
where the time goes in v5:
time: 48.6 us; the launch traced here: 48.4 us
  waiting for transfers between devices  19.7 us (41%)
  starting transfers between devices  18.6 us (38%)
  Pallas kernels  9.41 us (19%)
  between operations  0.74 us (2%)
    ppermute x19, waiting for transfers between devices, send(): return lax.ppermute(value, ('row', 'col'), pairs)  19.7 us
    ppermute x19, starting transfers between devices, send(): return lax.ppermute(value, ('row', 'col'), pairs)  18.6 us
    pallas_call x6, Pallas kernels, call(): pl.pallas_call(kernel, out_shape=outs, in_specs=specs or [vspec() for _ i...  9.41 us
  transfers between devices with their start and end apart: 19, of which 8 were waited for; matrix products, arithmetic and copies ran while one was open for 0% of the time, Pallas kernels for 16%

profile of v5, /device:TPU:0, one launch (start us, length us, event | category | flops | bytes accessed | tf_op | source)
XLA Modules:
  0.0 48.4 jit_solution(6020813402145392580)
XLA Ops:
  0.0 0.0 copy-start
  0.0 4.0 %collective-permute-start.5 = (bf16[256,512]{1,0:T(8,128)(2,1)}, bf16[256,512]{1,0:T(8,128)(2,1)S(1)}, u32[]{:S(2)}, u32[]{:S(2)}) collective-permute-start(bf16[256,512]{1,0:T(8,128)(2,1)} %w_hbm.1), channel_id=1, source_target_pairs={{0,4},{1,5},{2,6},{3,7},{4,0},{5,1},{6,2},{7,3},{8,12},{9,13},{10,... | collective-permute-start | bytes 786440 | tf_op jit(solution)/shard_map/ppermute | solution.py:133
  4.0 1.2 %shard_map.46 = (bf16[256,256]{1,0:T(8,128)(2,1)S(1)}, bf16[256,768]{1,0:T(8,128)(2,1)S(1)}, f32[256,128]{1,0:T(8,128)S(1)}) custom-call(s32[1,256]{1,0:T(1,128)} %bitcast.1, bf16[256,256]{1,0:T(8,128)(2,1)} %ret_hbm.1, bf16[256,512]{1,0:T(8,128)(2,1)} %w_hbm.1), custom_call_target="tpu_custom_call" | custom-call | tf_op jit(solution)/shard_map/pallas_call | solution.py:105
  5.3 1.6 %collective-permute-start.1 = (bf16[256,256]{1,0:T(8,128)(2,1)S(1)}, bf16[256,256]{1,0:T(8,128)(2,1)S(1)}, u32[]{:S(2)}, u32[]{:S(2)}) collective-permute-start(bf16[256,256]{1,0:T(8,128)(2,1)S(1)} %get-tuple-element.25.refs_0_.refs_2_), channel_id=1, source_target_pairs={{0,2},{1,3},{2,0},{3,1},{4,6},{5,7},{6,4},{7,5},{8,10},{9,11},{10,... | collective-permute-start | bytes 393224 | tf_op jit(solution)/shard_map/ppermute | solution.py:133
  6.9 1.5 %collective-permute-start.7 = (bf16[256,256]{1,0:T(8,128)(2,1)S(1)}, bf16[256,256]{1,0:T(8,128)(2,1)S(1)}, u32[]{:S(2)}, u32[]{:S(2)}) collective-permute-start(bf16[256,256]{1,0:T(8,128)(2,1)S(1)} %get-tuple-element.25.refs_0_.refs_2_), channel_id=1, source_target_pairs={{0,16},{1,17},{2,18},{3,19},{4,20},{5,21},{6,22},{7,23},{8,24},{9,... | collective-permute-start | bytes 393224 | tf_op jit(solution)/shard_map/ppermute | solution.py:133
  8.4 0.0 copy-done
  8.4 0.5 %collective-permute-start.9 = (bf16[256,512]{1,0:T(8,128)(2,1)S(1)}, bf16[256,512]{1,0:T(8,128)(2,1)S(1)}, u32[]{:S(2)}, u32[]{:S(2)}) collective-permute-start(bf16[256,512]{1,0:T(8,128)(2,1)S(1)} %copy-done), channel_id=1, source_target_pairs={{0,16},{1,17},{2,18},{3,19},{4,20},{5,21},{6,22},{7,23},{8,24},{9,... | collective-permute-start | bytes 786440 | tf_op jit(solution)/shard_map/ppermute | solution.py:133
  8.9 1.5 %collective-permute-start = (bf16[256,256]{1,0:T(8,128)(2,1)S(1)}, bf16[256,256]{1,0:T(8,128)(2,1)S(1)}, u32[]{:S(2)}, u32[]{:S(2)}) collective-permute-start(bf16[256,256]{1,0:T(8,128)(2,1)S(1)} %get-tuple-element.25.refs_0_.refs_2_), channel_id=1, source_target_pairs={{0,8},{1,9},{2,10},{3,11},{4,12},{5,13},{6,14},{7,15},{8,0},{9,1},... | collective-permute-start | bytes 393224 | tf_op jit(solution)/shard_map/ppermute | solution.py:133
  10.4 2.2 %collective-permute-done.1.refs_2_.refs_1_ = bf16[256,256]{1,0:T(8,128)(2,1)S(1)} collective-permute-done((bf16[256,256]{1,0:T(8,128)(2,1)S(1)}, bf16[256,256]{1,0:T(8,128)(2,1)S(1)}, u32[]{:S(2)}, u32[]{:S(2)}) %collective-permute-start.1) | collective-permute-done | bytes 131104 | tf_op jit(solution)/shard_map/ppermute | solution.py:133
  12.7 0.7 %collective-permute-done.7.refs_6_ = bf16[256,256]{1,0:T(8,128)(2,1)S(1)} collective-permute-done((bf16[256,256]{1,0:T(8,128)(2,1)S(1)}, bf16[256,256]{1,0:T(8,128)(2,1)S(1)}, u32[]{:S(2)}, u32[]{:S(2)}) %collective-permute-start.7) | collective-permute-done | bytes 131104 | tf_op jit(solution)/shard_map/ppermute | solution.py:133
  13.4 0.0 collective-permute-start.8
  13.4 1.7 %collective-permute-start.2 = (bf16[256,256]{1,0:T(8,128)(2,1)S(1)}, bf16[256,256]{1,0:T(8,128)(2,1)S(1)}, u32[]{:S(2)}, u32[]{:S(2)}) collective-permute-start(bf16[256,256]{1,0:T(8,128)(2,1)S(1)} %get-tuple-element.25.refs_0_.refs_2_), channel_id=1, source_target_pairs={{0,4},{1,5},{2,6},{3,7},{4,0},{5,1},{6,2},{7,3},{8,12},{9,13},{10,... | collective-permute-start | bytes 393224 | tf_op jit(solution)/shard_map/ppermute | solution.py:133
  15.1 1.2 %collective-permute-done.5.refs_5_ = bf16[256,512]{1,0:T(8,128)(2,1)S(1)} collective-permute-done((bf16[256,512]{1,0:T(8,128)(2,1)}, bf16[256,512]{1,0:T(8,128)(2,1)S(1)}, u32[]{:S(2)}, u32[]{:S(2)}) %collective-permute-start.5) | collective-permute-done | bytes 262176 | tf_op jit(solution)/shard_map/ppermute | solution.py:133
  16.2 1.5 %collective-permute-start.6 = (bf16[256,512]{1,0:T(8,128)(2,1)S(1)}, bf16[256,512]{1,0:T(8,128)(2,1)S(1)}, u32[]{:S(2)}, u32[]{:S(2)}) collective-permute-start(bf16[256,512]{1,0:T(8,128)(2,1)S(1)} %collective-permute-done.5.refs_5_), channel_id=1, source_target_pairs={{0,16},{1,17},{2,18},{3,19},{4,20},{5,21},{6,22},{7,23},{8,24},{9,... | collective-permute-start | bytes 786440 | tf_op jit(solution)/shard_map/ppermute | solution.py:133
  17.8 0.0 collective-permute-done.refs_1_.refs_0_
  17.8 0.9 %collective-permute-start.3 = (bf16[256,256]{1,0:T(8,128)(2,1)S(1)}, bf16[256,256]{1,0:T(8,128)(2,1)S(1)}, u32[]{:S(2)}, u32[]{:S(2)}) collective-permute-start(bf16[256,256]{1,0:T(8,128)(2,1)S(1)} %collective-permute-done.refs_1_.refs_0_), channel_id=1, source_target_pairs={{0,2},{1,3},{2,0},{3,1},{4,6},{5,7},{6,4},{7,5},{8,10},{9,11},{10,... | collective-permute-start | bytes 393224 | tf_op jit(solution)/shard_map/ppermute | solution.py:133
  18.6 0.0 collective-permute-done.9.refs_7_
  18.6 0.0 collective-permute-start.11
  18.6 4.5 %collective-permute-done.2.refs_4_ = bf16[256,256]{1,0:T(8,128)(2,1)S(1)} collective-permute-done((bf16[256,256]{1,0:T(8,128)(2,1)S(1)}, bf16[256,256]{1,0:T(8,128)(2,1)S(1)}, u32[]{:S(2)}, u32[]{:S(2)}) %collective-permute-start.2) | collective-permute-done | bytes 131104 | tf_op jit(solution)/shard_map/ppermute | solution.py:133
  23.1 0.0 collective-permute-start.10
  23.1 1.1 %collective-permute-done.3.refs_3_.refs_0_ = bf16[256,256]{1,0:T(8,128)(2,1)S(1)} collective-permute-done((bf16[256,256]{1,0:T(8,128)(2,1)S(1)}, bf16[256,256]{1,0:T(8,128)(2,1)S(1)}, u32[]{:S(2)}, u32[]{:S(2)}) %collective-permute-start.3) | collective-permute-done | bytes 131104 | tf_op jit(solution)/shard_map/ppermute | solution.py:133
  24.2 0.5 %collective-permute-start.4 = (bf16[256,256]{1,0:T(8,128)(2,1)S(1)}, bf16[256,256]{1,0:T(8,128)(2,1)S(1)}, u32[]{:S(2)}, u32[]{:S(2)}) collective-permute-start(bf16[256,256]{1,0:T(8,128)(2,1)S(1)} %collective-permute-done.2.refs_4_), channel_id=1, source_target_pairs={{0,16},{1,17},{2,18},{3,19},{4,20},{5,21},{6,22},{7,23},{8,24},{9,... | collective-permute-start | bytes 393224 | tf_op jit(solution)/shard_map/ppermute | solution.py:133
  24.7 0.0 collective-permute-done.10.refs_8_
  24.7 0.1 collective-permute-start.15
  24.9 0.0 collective-permute-done.6.refs_4_.refs_2_
  24.9 0.4 collective-permute-start.13
  25.9 0.0 collective-permute-done.8.refs_5_
  25.9 0.2 collective-permute-start.14
  26.1 0.0 collective-permute-done.11.refs_9_
  26.1 3.1 %shard_map.47 = (f32[256,512]{1,0:T(8,128)S(1)}, f32[256,512]{1,0:T(8,128)S(1)}, f32[256,512]{1,0:T(8,128)S(1)}, f32[256,512]{1,0:T(8,128)S(1)}) custom-call(s32[1]{0:T(128)S(6)} %copy.13.code_ref, bf16[256,256]{1,0:T(8,128)(2,1)S(1)} %get-tuple-element.25.refs_0_.refs_2_, bf16[256,256]{1,0:T(8,128)(2,1)S(1)} %collective-permute-done.refs_1_.refs_0_, ...), custom_call_target="tpu_custom_call" | custom-call | tf_op jit(solution)/shard_map/pallas_call | solution.py:105
  29.2 0.0 collective-permute-done.4.refs_3_.refs_1_
  29.2 0.4 collective-permute-start.12
  29.7 0.0 collective-permute-done.14.refs_6_
  29.7 0.0 collective-permute-done.15.refs_7_
  29.7 2.0 %shard_map.48 = (f32[256,512]{1,0:T(8,128)S(1)}, f32[256,512]{1,0:T(8,128)S(1)}, f32[256,512]{1,0:T(8,128)S(1)}, f32[256,512]{1,0:T(8,128)S(1)}) custom-call(s32[1]{0:T(128)S(6)} %copy.13.code_ref, bf16[256,256]{1,0:T(8,128)(2,1)S(1)} %get-tuple-element.25.refs_0_.refs_2_, ...), custom_call_target="tpu_custom_call", output_to_operand_aliasing={{0}: (9, {}), {1}: (10, {}), {2}: (11, {}), {3}: (12, {})} | custom-call | tf_op jit(solution)/shard_map/pallas_call | solution.py:105
  31.7 0.0 collective-permute-done.12.refs_5_.refs_3_
  31.7 0.0 collective-permute-done.13.refs_6_.refs_4_
  31.8 0.7 %shard_map.50 = bf16[256,512]{1,0:T(8,128)(2,1)S(1)} custom-call(s32[1]{0:T(128)S(6)} %copy.13.code_ref, bf16[256,256]{1,0:T(8,128)(2,1)S(1)} %collective-permute-done.3.refs_3_.refs_0_, bf16[256,256]{1,0:T(8,128)(2,1)S(1)} %collective-permute-done.4.refs_3_.refs_1_, bf16[256,512]{1,0:T(8,128)(2,1)S(1)} %collective-permute-done.6.refs_4_.refs_2_, ...), custom_call_target="tpu_custom_call" | custom-call | tf_op jit(solution)/shard_map/pallas_call | solution.py:105
  32.5 1.6 %collective-permute-start.16 = (bf16[256,512]{1,0:T(8,128)(2,1)S(1)}, bf16[256,512]{1,0:T(8,128)(2,1)S(1)}, u32[]{:S(2)}, u32[]{:S(2)}) collective-permute-start(bf16[256,512]{1,0:T(8,128)(2,1)S(1)} %shard_map.50), channel_id=1, source_target_pairs={{0,10},{1,11},{2,8},{3,9},{4,14},{5,15},{6,12},{7,13},{8,2},{9,3},... | collective-permute-start | bytes 786440 | tf_op jit(solution)/shard_map/ppermute | solution.py:133
  34.1 1.4 %shard_map.49 = (bf16[256,512]{1,0:T(8,128)(2,1)S(1)}, bf16[256,512]{1,0:T(8,128)(2,1)S(1)}, f32[256,512]{1,0:T(8,128)S(1)}) custom-call(s32[1]{0:T(128)S(6)} %copy.13.code_ref, bf16[256,256]{1,0:T(8,128)(2,1)S(1)} %collective-permute-done.refs_1_.refs_0_, bf16[256,256]{1,0:T(8,128)(2,1)S(1)} %collective-permute-done.1.refs_2_.refs_1_, ...), custom_call_target="tpu_custom_call" | custom-call | tf_op jit(solution)/shard_map/pallas_call | solution.py:105
  35.5 0.6 %collective-permute-start.17 = (bf16[256,512]{1,0:T(8,128)(2,1)S(1)}, bf16[256,512]{1,0:T(8,128)(2,1)S(1)}, u32[]{:S(2)}, u32[]{:S(2)}) collective-permute-start(bf16[256,512]{1,0:T(8,128)(2,1)S(1)} %get-tuple-element.41), channel_id=1, source_target_pairs={{0,8},{1,9},{2,10},{3,11},{4,12},{5,13},{6,14},{7,15},{8,0},{9,1},... | collective-permute-start | bytes 786440 | tf_op jit(solution)/shard_map/ppermute | solution.py:133
  36.1 1.4 %collective-permute-start.18 = (bf16[256,512]{1,0:T(8,128)(2,1)S(1)}, bf16[256,512]{1,0:T(8,128)(2,1)S(1)}, u32[]{:S(2)}, u32[]{:S(2)}) collective-permute-start(bf16[256,512]{1,0:T(8,128)(2,1)S(1)} %get-tuple-element.42), channel_id=1, source_target_pairs={{0,2},{1,3},{2,0},{3,1},{4,6},{5,7},{6,4},{7,5},{8,10},{9,11},{10,... | collective-permute-start | bytes 786440 | tf_op jit(solution)/shard_map/ppermute | solution.py:133
  37.5 5.1 %collective-permute-done.16.refs_1_ = bf16[256,512]{1,0:T(8,128)(2,1)S(1)} collective-permute-done((bf16[256,512]{1,0:T(8,128)(2,1)S(1)}, bf16[256,512]{1,0:T(8,128)(2,1)S(1)}, u32[]{:S(2)}, u32[]{:S(2)}) %collective-permute-start.16) | collective-permute-done | bytes 262176 | tf_op jit(solution)/shard_map/ppermute | solution.py:133
  42.6 4.8 %collective-permute-done.17.refs_2_ = bf16[256,512]{1,0:T(8,128)(2,1)S(1)} collective-permute-done((bf16[256,512]{1,0:T(8,128)(2,1)S(1)}, bf16[256,512]{1,0:T(8,128)(2,1)S(1)}, u32[]{:S(2)}, u32[]{:S(2)}) %collective-permute-start.17) | collective-permute-done | bytes 262176 | tf_op jit(solution)/shard_map/ppermute | solution.py:133
  47.4 0.1 collective-permute-done.18.refs_3_
  47.5 0.9 %shard_map.51 = f32[256,512]{1,0:T(8,128)} custom-call(f32[256,128]{1,0:T(8,128)S(1)} %get-tuple-element.24.sigma_ref, f32[256,512]{1,0:T(8,128)S(1)} %get-tuple-element.39.refs_0_, bf16[256,512]{1,0:T(8,128)(2,1)S(1)} %collective-permute-done.16.refs_1_, bf16[256,512]{1,0:T(8,128)(2,1)S(1)} %collective-permute-done.17.refs_2_, ...), custom_call_target="tpu_custom_call" | custom-call | tf_op jit(solution)/shard_map/pallas_call | solution.py:105
Async XLA Ops:
  0.0 8.4 %copy-start = (bf16[256,512]{1,0:T(8,128)(2,1)S(1)}, bf16[256,512]{1,0:T(8,128)(2,1)}, u32[]{:S(2)}) copy-start(bf16[256,512]{1,0:T(8,128)(2,1)} %w_hbm.1) | copy-start | bytes 786436
  0.0 16.2 %collective-permute-start.5 = (bf16[256,512]{1,0:T(8,128)(2,1)}, bf16[256,512]{1,0:T(8,128)(2,1)S(1)}, u32[]{:S(2)}, u32[]{:S(2)}) collective-permute-start(bf16[256,512]{1,0:T(8,128)(2,1)} %w_hbm.1), channel_id=1, source_target_pairs={{0,4},{1,5},{2,6},{3,7},{4,0},{5,1},{6,2},{7,3},{8,12},{9,13},{10,... | collective-permute-start | bytes 786440 | tf_op jit(solution)/shard_map/ppermute | solution.py:133
  5.3 7.4 %collective-permute-start.1 = (bf16[256,256]{1,0:T(8,128)(2,1)S(1)}, bf16[256,256]{1,0:T(8,128)(2,1)S(1)}, u32[]{:S(2)}, u32[]{:S(2)}) collective-permute-start(bf16[256,256]{1,0:T(8,128)(2,1)S(1)} %get-tuple-element.25.refs_0_.refs_2_), channel_id=1, source_target_pairs={{0,2},{1,3},{2,0},{3,1},{4,6},{5,7},{6,4},{7,5},{8,10},{9,11},{10,... | collective-permute-start | bytes 393224 | tf_op jit(solution)/shard_map/ppermute | solution.py:133
  6.9 6.4 %collective-permute-start.7 = (bf16[256,256]{1,0:T(8,128)(2,1)S(1)}, bf16[256,256]{1,0:T(8,128)(2,1)S(1)}, u32[]{:S(2)}, u32[]{:S(2)}) collective-permute-start(bf16[256,256]{1,0:T(8,128)(2,1)S(1)} %get-tuple-element.25.refs_0_.refs_2_), channel_id=1, source_target_pairs={{0,16},{1,17},{2,18},{3,19},{4,20},{5,21},{6,22},{7,23},{8,24},{9,... | collective-permute-start | bytes 393224 | tf_op jit(solution)/shard_map/ppermute | solution.py:133
  8.4 10.2 %collective-permute-start.9 = (bf16[256,512]{1,0:T(8,128)(2,1)S(1)}, bf16[256,512]{1,0:T(8,128)(2,1)S(1)}, u32[]{:S(2)}, u32[]{:S(2)}) collective-permute-start(bf16[256,512]{1,0:T(8,128)(2,1)S(1)} %copy-done), channel_id=1, source_target_pairs={{0,16},{1,17},{2,18},{3,19},{4,20},{5,21},{6,22},{7,23},{8,24},{9,... | collective-permute-start | bytes 786440 | tf_op jit(solution)/shard_map/ppermute | solution.py:133
  8.9 8.8 %collective-permute-start = (bf16[256,256]{1,0:T(8,128)(2,1)S(1)}, bf16[256,256]{1,0:T(8,128)(2,1)S(1)}, u32[]{:S(2)}, u32[]{:S(2)}) collective-permute-start(bf16[256,256]{1,0:T(8,128)(2,1)S(1)} %get-tuple-element.25.refs_0_.refs_2_), channel_id=1, source_target_pairs={{0,8},{1,9},{2,10},{3,11},{4,12},{5,13},{6,14},{7,15},{8,0},{9,1},... | collective-permute-start | bytes 393224 | tf_op jit(solution)/shard_map/ppermute | solution.py:133
  13.4 12.5 %collective-permute-start.8 = (bf16[256,768]{1,0:T(8,128)(2,1)S(1)}, bf16[256,768]{1,0:T(8,128)(2,1)S(1)}, u32[]{:S(2)}, u32[]{:S(2)}) collective-permute-start(bf16[256,768]{1,0:T(8,128)(2,1)S(1)} %get-tuple-element.29.refs_4_), channel_id=1, source_target_pairs={{0,1},{1,0},{2,3},{3,2},{4,5},{5,4},{6,7},{7,6},{8,9},{9,8},{10,11... | collective-permute-start | bytes 1179656 | tf_op jit(solution)/shard_map/ppermute | solution.py:133
  13.4 9.7 %collective-permute-start.2 = (bf16[256,256]{1,0:T(8,128)(2,1)S(1)}, bf16[256,256]{1,0:T(8,128)(2,1)S(1)}, u32[]{:S(2)}, u32[]{:S(2)}) collective-permute-start(bf16[256,256]{1,0:T(8,128)(2,1)S(1)} %get-tuple-element.25.refs_0_.refs_2_), channel_id=1, source_target_pairs={{0,4},{1,5},{2,6},{3,7},{4,0},{5,1},{6,2},{7,3},{8,12},{9,13},{10,... | collective-permute-start | bytes 393224 | tf_op jit(solution)/shard_map/ppermute | solution.py:133
  16.2 8.6 %collective-permute-start.6 = (bf16[256,512]{1,0:T(8,128)(2,1)S(1)}, bf16[256,512]{1,0:T(8,128)(2,1)S(1)}, u32[]{:S(2)}, u32[]{:S(2)}) collective-permute-start(bf16[256,512]{1,0:T(8,128)(2,1)S(1)} %collective-permute-done.5.refs_5_), channel_id=1, source_target_pairs={{0,16},{1,17},{2,18},{3,19},{4,20},{5,21},{6,22},{7,23},{8,24},{9,... | collective-permute-start | bytes 786440 | tf_op jit(solution)/shard_map/ppermute | solution.py:133
  17.8 6.4 %collective-permute-start.3 = (bf16[256,256]{1,0:T(8,128)(2,1)S(1)}, bf16[256,256]{1,0:T(8,128)(2,1)S(1)}, u32[]{:S(2)}, u32[]{:S(2)}) collective-permute-start(bf16[256,256]{1,0:T(8,128)(2,1)S(1)} %collective-permute-done.refs_1_.refs_0_), channel_id=1, source_target_pairs={{0,2},{1,3},{2,0},{3,1},{4,6},{5,7},{6,4},{7,5},{8,10},{9,11},{10,... | collective-permute-start | bytes 393224 | tf_op jit(solution)/shard_map/ppermute | solution.py:133
  18.6 7.5 %collective-permute-start.11 = (bf16[256,512]{1,0:T(8,128)(2,1)S(1)}, bf16[256,512]{1,0:T(8,128)(2,1)S(1)}, u32[]{:S(2)}, u32[]{:S(2)}) collective-permute-start(bf16[256,512]{1,0:T(8,128)(2,1)S(1)} %collective-permute-done.9.refs_7_), channel_id=1, source_target_pairs={{0,1},{1,0},{2,3},{3,2},{4,5},{5,4},{6,7},{7,6},{8,9},{9,8},{10,11... | collective-permute-start | bytes 786440 | tf_op jit(solution)/shard_map/ppermute | solution.py:133
  23.1 1.6 %collective-permute-start.10 = (bf16[256,256]{1,0:T(8,128)(2,1)S(1)}, bf16[256,256]{1,0:T(8,128)(2,1)S(1)}, u32[]{:S(2)}, u32[]{:S(2)}) collective-permute-start(bf16[256,256]{1,0:T(8,128)(2,1)S(1)} %collective-permute-done.7.refs_6_), channel_id=1, source_target_pairs={{0,1},{1,0},{2,3},{3,2},{4,5},{5,4},{6,7},{7,6},{8,9},{9,8},{10,11... | collective-permute-start | bytes 393224 | tf_op jit(solution)/shard_map/ppermute | solution.py:133
  24.2 5.0 %collective-permute-start.4 = (bf16[256,256]{1,0:T(8,128)(2,1)S(1)}, bf16[256,256]{1,0:T(8,128)(2,1)S(1)}, u32[]{:S(2)}, u32[]{:S(2)}) collective-permute-start(bf16[256,256]{1,0:T(8,128)(2,1)S(1)} %collective-permute-done.2.refs_4_), channel_id=1, source_target_pairs={{0,16},{1,17},{2,18},{3,19},{4,20},{5,21},{6,22},{7,23},{8,24},{9,... | collective-permute-start | bytes 393224 | tf_op jit(solution)/shard_map/ppermute | solution.py:133
  24.7 5.0 %collective-permute-start.15 = (bf16[256,512]{1,0:T(8,128)(2,1)S(1)}, bf16[256,512]{1,0:T(8,128)(2,1)S(1)}, u32[]{:S(2)}, u32[]{:S(2)}) collective-permute-start(bf16[256,512]{1,0:T(8,128)(2,1)S(1)} %collective-permute-done.5.refs_5_), channel_id=1, source_target_pairs={{0,1},{1,0},{2,3},{3,2},{4,5},{5,4},{6,7},{7,6},{8,9},{9,8},{10,11... | collective-permute-start | bytes 786440 | tf_op jit(solution)/shard_map/ppermute | solution.py:133
  24.9 6.9 %collective-permute-start.13 = (bf16[256,512]{1,0:T(8,128)(2,1)S(1)}, bf16[256,512]{1,0:T(8,128)(2,1)S(1)}, u32[]{:S(2)}, u32[]{:S(2)}) collective-permute-start(bf16[256,512]{1,0:T(8,128)(2,1)S(1)} %collective-permute-done.6.refs_4_.refs_2_), channel_id=1, source_target_pairs={{0,1},{1,0},{2,3},{3,2},{4,5},{5,4},{6,7},{7,6},{8,9},{9,8},{10,11... | collective-permute-start | bytes 786440 | tf_op jit(solution)/shard_map/ppermute | solution.py:133
  25.9 3.8 %collective-permute-start.14 = (bf16[256,256]{1,0:T(8,128)(2,1)S(1)}, bf16[256,256]{1,0:T(8,128)(2,1)S(1)}, u32[]{:S(2)}, u32[]{:S(2)}) collective-permute-start(bf16[256,256]{1,0:T(8,128)(2,1)S(1)} %collective-permute-done.2.refs_4_), channel_id=1, source_target_pairs={{0,1},{1,0},{2,3},{3,2},{4,5},{5,4},{6,7},{7,6},{8,9},{9,8},{10,11... | collective-permute-start | bytes 393224 | tf_op jit(solution)/shard_map/ppermute | solution.py:133
  29.2 2.5 %collective-permute-start.12 = (bf16[256,256]{1,0:T(8,128)(2,1)S(1)}, bf16[256,256]{1,0:T(8,128)(2,1)S(1)}, u32[]{:S(2)}, u32[]{:S(2)}) collective-permute-start(bf16[256,256]{1,0:T(8,128)(2,1)S(1)} %collective-permute-done.4.refs_3_.refs_1_), channel_id=1, source_target_pairs={{0,1},{1,0},{2,3},{3,2},{4,5},{5,4},{6,7},{7,6},{8,9},{9,8},{10,11... | collective-permute-start | bytes 393224 | tf_op jit(solution)/shard_map/ppermute | solution.py:133
  32.5 10.2 %collective-permute-start.16 = (bf16[256,512]{1,0:T(8,128)(2,1)S(1)}, bf16[256,512]{1,0:T(8,128)(2,1)S(1)}, u32[]{:S(2)}, u32[]{:S(2)}) collective-permute-start(bf16[256,512]{1,0:T(8,128)(2,1)S(1)} %shard_map.50), channel_id=1, source_target_pairs={{0,10},{1,11},{2,8},{3,9},{4,14},{5,15},{6,12},{7,13},{8,2},{9,3},... | collective-permute-start | bytes 786440 | tf_op jit(solution)/shard_map/ppermute | solution.py:133
  35.5 11.9 %collective-permute-start.17 = (bf16[256,512]{1,0:T(8,128)(2,1)S(1)}, bf16[256,512]{1,0:T(8,128)(2,1)S(1)}, u32[]{:S(2)}, u32[]{:S(2)}) collective-permute-start(bf16[256,512]{1,0:T(8,128)(2,1)S(1)} %get-tuple-element.41), channel_id=1, source_target_pairs={{0,8},{1,9},{2,10},{3,11},{4,12},{5,13},{6,14},{7,15},{8,0},{9,1},... | collective-permute-start | bytes 786440 | tf_op jit(solution)/shard_map/ppermute | solution.py:133
  36.1 11.4 %collective-permute-start.18 = (bf16[256,512]{1,0:T(8,128)(2,1)S(1)}, bf16[256,512]{1,0:T(8,128)(2,1)S(1)}, u32[]{:S(2)}, u32[]{:S(2)}) collective-permute-start(bf16[256,512]{1,0:T(8,128)(2,1)S(1)} %get-tuple-element.42), channel_id=1, source_target_pairs={{0,2},{1,3},{2,0},{3,1},{4,6},{5,7},{6,4},{7,5},{8,10},{9,11},{10,... | collective-permute-start | bytes 786440 | tf_op jit(solution)/shard_map/ppermute | solution.py:133

commit v6 on v5

--- a/solution.py
+++ b/solution.py
@@ -177,21 +177,21 @@
     at["zh_w"] = [send(weights, zh=k) for k in zs]
     at["zh_m"] = [send(masked, zh=k) for k in zs]
     at["near_w"] = [send(weights, y=k) for k in ys]
-    at["near_m"] = [send(masked, y=k) for k in ys]
     at["x"] = [send(masked, x=1)]
     at["xzl"] = [send(at["x"][0], zl=1)]
     at["fwd_w"] = [send(v, y=k) for v in at["zh_w"] for k in ys]
-    at["nm_s"] = [send(v, core=1) for v in at["near_m"]]
+    at["fw_s"] = [send(v, core=1) for v in at["fwd_w"]]
     at["m_s"] = [send(v, core=1) for v in at["zh_m"]]
     at["fwd_m"] = [send(after(v, *at["xzl"]), y=k) for v in at["zh_m"] for k in ys]
-    at["w_s"] = [send(after(v, *at["zh_m"]), core=1) for v in at["zh_w"]]
+    at["w_s"] = [send(v, core=1) for v in at["zh_w"]]
     at["nw_s"] = [send(v, core=1) for v in at["near_w"]]
     at["zl"] = [send(masked, zl=1)]
-    at["own_s"] = [send(after(both, *at["near_m"], *at["zl"]), core=1)]
+    at["own_s"] = [send(after(both, *at["zl"]), core=1)]
+    at["near_m"] = [send(masked, y=k) for k in ys]
+    at["nm_s"] = [send(v, core=1) for v in at["near_m"]]
     rows += [masked, at["x"][0], at["zl"][0], at["xzl"][0]]
-    at["K1"] = chip((after(both, *at["zh_w"]),), (at["own_s"][0],), *zip((*at["near_m"], *at["nm_s"]), (*at["near_w"], *at["nw_s"])))
+    at["K1"] = chip((after(both, *at["zh_w"], *at["near_w"]),), (at["own_s"][0],), *zip((*at["near_m"], *at["nm_s"]), (*at["near_w"], *at["nw_s"])))
     at["K2"] = at["K1"]
-    at["fw_s"] = [send(v, core=1) for v in at["fwd_w"]]
     for a, b, p, q in zip(at["zh_m"], at["zh_w"], at["m_s"], at["w_s"]):
         at["K3"] = chip((a, b), (p, q))
     at["fm_s"] = [send(after(v, *at["K2"]), core=1) for v in at["fwd_m"]]

time: 48.6 us -> 48.2 us (level)
  waiting for transfers between devices: 19.7 us -> 19 us
    ppermute x19, waiting for transfers between devices: 19.7 us -> 19 us  [send(): return lax.ppermute(value, ('row', 'col'), pairs)]
where the time goes in v6:
time: 48.2 us; the launch traced here: 48.1 us
  starting transfers between devices  19 us (39%)
  waiting for transfers between devices  19 us (39%)
  Pallas kernels  9.42 us (20%)
  between operations  0.74 us (2%)
    ppermute x19, starting transfers between devices, send(): return lax.ppermute(value, ('row', 'col'), pairs)  19 us
    ppermute x19, waiting for transfers between devices, send(): return lax.ppermute(value, ('row', 'col'), pairs)  19 us
    pallas_call x6, Pallas kernels, call(): pl.pallas_call(kernel, out_shape=outs, in_specs=specs or [vspec() for _ i...  9.42 us
  transfers between devices with their start and end apart: 19, of which 8 were waited for; matrix products, arithmetic and copies ran while one was open for 0% of the time, Pallas kernels for 16%

profile of v6, /device:TPU:0, one launch (start us, length us, event | category | flops | bytes accessed | tf_op | source)
XLA Modules:
  0.0 48.1 jit_solution(10915942917594034791)
XLA Ops:
  0.0 0.0 copy-start
  0.0 4.0 %collective-permute-start.5 = (bf16[256,512]{1,0:T(8,128)(2,1)}, bf16[256,512]{1,0:T(8,128)(2,1)S(1)}, u32[]{:S(2)}, u32[]{:S(2)}) collective-permute-start(bf16[256,512]{1,0:T(8,128)(2,1)} %w_hbm.1), channel_id=1, source_target_pairs={{0,4},{1,5},{2,6},{3,7},{4,0},{5,1},{6,2},{7,3},{8,12},{9,13},{10,... | collective-permute-start | bytes 786440 | tf_op jit(solution)/shard_map/ppermute | solution.py:133
  4.0 1.2 %shard_map.46 = (bf16[256,256]{1,0:T(8,128)(2,1)S(1)}, bf16[256,768]{1,0:T(8,128)(2,1)S(1)}, f32[256,128]{1,0:T(8,128)S(1)}) custom-call(s32[1,256]{1,0:T(1,128)} %bitcast.1, bf16[256,256]{1,0:T(8,128)(2,1)} %ret_hbm.1, bf16[256,512]{1,0:T(8,128)(2,1)} %w_hbm.1), custom_call_target="tpu_custom_call" | custom-call | tf_op jit(solution)/shard_map/pallas_call | solution.py:105
  5.3 1.6 %collective-permute-start.1 = (bf16[256,256]{1,0:T(8,128)(2,1)S(1)}, bf16[256,256]{1,0:T(8,128)(2,1)S(1)}, u32[]{:S(2)}, u32[]{:S(2)}) collective-permute-start(bf16[256,256]{1,0:T(8,128)(2,1)S(1)} %get-tuple-element.24.refs_0_.refs_2_), channel_id=1, source_target_pairs={{0,2},{1,3},{2,0},{3,1},{4,6},{5,7},{6,4},{7,5},{8,10},{9,11},{10,... | collective-permute-start | bytes 393224 | tf_op jit(solution)/shard_map/ppermute | solution.py:133
  6.9 0.0 copy-done
  6.9 1.5 %collective-permute-start.7 = (bf16[256,512]{1,0:T(8,128)(2,1)S(1)}, bf16[256,512]{1,0:T(8,128)(2,1)S(1)}, u32[]{:S(2)}, u32[]{:S(2)}) collective-permute-start(bf16[256,512]{1,0:T(8,128)(2,1)S(1)} %copy-done), channel_id=1, source_target_pairs={{0,16},{1,17},{2,18},{3,19},{4,20},{5,21},{6,22},{7,23},{8,24},{9,... | collective-permute-start | bytes 786440 | tf_op jit(solution)/shard_map/ppermute | solution.py:133
  8.4 1.5 %collective-permute-start = (bf16[256,256]{1,0:T(8,128)(2,1)S(1)}, bf16[256,256]{1,0:T(8,128)(2,1)S(1)}, u32[]{:S(2)}, u32[]{:S(2)}) collective-permute-start(bf16[256,256]{1,0:T(8,128)(2,1)S(1)} %get-tuple-element.24.refs_0_.refs_2_), channel_id=1, source_target_pairs={{0,8},{1,9},{2,10},{3,11},{4,12},{5,13},{6,14},{7,15},{8,0},{9,1},... | collective-permute-start | bytes 393224 | tf_op jit(solution)/shard_map/ppermute | solution.py:133
  9.9 0.5 %collective-permute-start.9 = (bf16[256,256]{1,0:T(8,128)(2,1)S(1)}, bf16[256,256]{1,0:T(8,128)(2,1)S(1)}, u32[]{:S(2)}, u32[]{:S(2)}) collective-permute-start(bf16[256,256]{1,0:T(8,128)(2,1)S(1)} %get-tuple-element.24.refs_0_.refs_2_), channel_id=1, source_target_pairs={{0,16},{1,17},{2,18},{3,19},{4,20},{5,21},{6,22},{7,23},{8,24},{9,... | collective-permute-start | bytes 393224 | tf_op jit(solution)/shard_map/ppermute | solution.py:133
  10.4 2.2 %collective-permute-done.1.refs_2_.refs_1_ = bf16[256,256]{1,0:T(8,128)(2,1)S(1)} collective-permute-done((bf16[256,256]{1,0:T(8,128)(2,1)S(1)}, bf16[256,256]{1,0:T(8,128)(2,1)S(1)}, u32[]{:S(2)}, u32[]{:S(2)}) %collective-permute-start.1) | collective-permute-done | bytes 131104 | tf_op jit(solution)/shard_map/ppermute | solution.py:133
  12.7 0.0 collective-permute-start.8
  12.7 0.7 %collective-permute-done.refs_1_.refs_0_ = bf16[256,256]{1,0:T(8,128)(2,1)S(1)} collective-permute-done((bf16[256,256]{1,0:T(8,128)(2,1)S(1)}, bf16[256,256]{1,0:T(8,128)(2,1)S(1)}, u32[]{:S(2)}, u32[]{:S(2)}) %collective-permute-start) | collective-permute-done | bytes 131104 | tf_op jit(solution)/shard_map/ppermute | solution.py:133
  13.4 1.7 %collective-permute-start.2 = (bf16[256,256]{1,0:T(8,128)(2,1)S(1)}, bf16[256,256]{1,0:T(8,128)(2,1)S(1)}, u32[]{:S(2)}, u32[]{:S(2)}) collective-permute-start(bf16[256,256]{1,0:T(8,128)(2,1)S(1)} %get-tuple-element.24.refs_0_.refs_2_), channel_id=1, source_target_pairs={{0,4},{1,5},{2,6},{3,7},{4,0},{5,1},{6,2},{7,3},{8,12},{9,13},{10,... | collective-permute-start | bytes 393224 | tf_op jit(solution)/shard_map/ppermute | solution.py:133
  15.1 1.2 %collective-permute-done.5.refs_5_ = bf16[256,512]{1,0:T(8,128)(2,1)S(1)} collective-permute-done((bf16[256,512]{1,0:T(8,128)(2,1)}, bf16[256,512]{1,0:T(8,128)(2,1)S(1)}, u32[]{:S(2)}, u32[]{:S(2)}) %collective-permute-start.5) | collective-permute-done | bytes 262176 | tf_op jit(solution)/shard_map/ppermute | solution.py:133
  16.2 1.5 %collective-permute-start.6 = (bf16[256,512]{1,0:T(8,128)(2,1)S(1)}, bf16[256,512]{1,0:T(8,128)(2,1)S(1)}, u32[]{:S(2)}, u32[]{:S(2)}) collective-permute-start(bf16[256,512]{1,0:T(8,128)(2,1)S(1)} %collective-permute-done.5.refs_5_), channel_id=1, source_target_pairs={{0,16},{1,17},{2,18},{3,19},{4,20},{5,21},{6,22},{7,23},{8,24},{9,... | collective-permute-start | bytes 786440 | tf_op jit(solution)/shard_map/ppermute | solution.py:133
  17.8 0.0 collective-permute-done.9.refs_6_
  17.8 0.9 %collective-permute-start.3 = (bf16[256,256]{1,0:T(8,128)(2,1)S(1)}, bf16[256,256]{1,0:T(8,128)(2,1)S(1)}, u32[]{:S(2)}, u32[]{:S(2)}) collective-permute-start(bf16[256,256]{1,0:T(8,128)(2,1)S(1)} %collective-permute-done.refs_1_.refs_0_), channel_id=1, source_target_pairs={{0,2},{1,3},{2,0},{3,1},{4,6},{5,7},{6,4},{7,5},{8,10},{9,11},{10,... | collective-permute-start | bytes 393224 | tf_op jit(solution)/shard_map/ppermute | solution.py:133
  18.6 0.0 collective-permute-done.7.refs_7_
  18.6 0.0 collective-permute-start.11
  18.6 3.8 %collective-permute-done.2.refs_4_ = bf16[256,256]{1,0:T(8,128)(2,1)S(1)} collective-permute-done((bf16[256,256]{1,0:T(8,128)(2,1)S(1)}, bf16[256,256]{1,0:T(8,128)(2,1)S(1)}, u32[]{:S(2)}, u32[]{:S(2)}) %collective-permute-start.2) | collective-permute-done | bytes 131104 | tf_op jit(solution)/shard_map/ppermute | solution.py:133
  22.4 0.0 collective-permute-start.10
  22.4 1.1 %collective-permute-done.3.refs_3_.refs_0_ = bf16[256,256]{1,0:T(8,128)(2,1)S(1)} collective-permute-done((bf16[256,256]{1,0:T(8,128)(2,1)S(1)}, bf16[256,256]{1,0:T(8,128)(2,1)S(1)}, u32[]{:S(2)}, u32[]{:S(2)}) %collective-permute-start.3) | collective-permute-done | bytes 131104 | tf_op jit(solution)/shard_map/ppermute | solution.py:133
  23.5 1.0 %collective-permute-start.4 = (bf16[256,256]{1,0:T(8,128)(2,1)S(1)}, bf16[256,256]{1,0:T(8,128)(2,1)S(1)}, u32[]{:S(2)}, u32[]{:S(2)}) collective-permute-start(bf16[256,256]{1,0:T(8,128)(2,1)S(1)} %collective-permute-done.2.refs_4_), channel_id=1, source_target_pairs={{0,16},{1,17},{2,18},{3,19},{4,20},{5,21},{6,22},{7,23},{8,24},{9,... | collective-permute-start | bytes 393224 | tf_op jit(solution)/shard_map/ppermute | solution.py:133
  24.5 0.0 collective-permute-done.10.refs_8_
  24.5 0.0 collective-permute-start.15
  24.5 0.0 collective-permute-done.6.refs_4_.refs_2_
  24.5 0.5 %collective-permute-start.13 = (bf16[256,512]{1,0:T(8,128)(2,1)S(1)}, bf16[256,512]{1,0:T(8,128)(2,1)S(1)}, u32[]{:S(2)}, u32[]{:S(2)}) collective-permute-start(bf16[256,512]{1,0:T(8,128)(2,1)S(1)} %collective-permute-done.6.refs_4_.refs_2_), channel_id=1, source_target_pairs={{0,1},{1,0},{2,3},{3,2},{4,5},{5,4},{6,7},{7,6},{8,9},{9,8},{10,11... | collective-permute-start | bytes 786440 | tf_op jit(solution)/shard_map/ppermute | solution.py:133
  25.7 0.0 collective-permute-done.8.refs_5_
  25.7 0.1 collective-permute-start.14
  25.8 0.0 collective-permute-done.11.refs_9_
  25.8 3.1 %shard_map.47 = (f32[256,512]{1,0:T(8,128)S(1)}, f32[256,512]{1,0:T(8,128)S(1)}, f32[256,512]{1,0:T(8,128)S(1)}, f32[256,512]{1,0:T(8,128)S(1)}) custom-call(s32[1]{0:T(128)S(6)} %copy.13.code_ref, bf16[256,256]{1,0:T(8,128)(2,1)S(1)} %get-tuple-element.24.refs_0_.refs_2_, bf16[256,256]{1,0:T(8,128)(2,1)S(1)} %collective-permute-done.refs_1_.refs_0_, ...), custom_call_target="tpu_custom_call" | custom-call | tf_op jit(solution)/shard_map/pallas_call | solution.py:105
  28.9 0.0 collective-permute-done.4.refs_3_.refs_1_
  28.9 0.5 %collective-permute-start.12 = (bf16[256,256]{1,0:T(8,128)(2,1)S(1)}, bf16[256,256]{1,0:T(8,128)(2,1)S(1)}, u32[]{:S(2)}, u32[]{:S(2)}) collective-permute-start(bf16[256,256]{1,0:T(8,128)(2,1)S(1)} %collective-permute-done.4.refs_3_.refs_1_), channel_id=1, source_target_pairs={{0,1},{1,0},{2,3},{3,2},{4,5},{5,4},{6,7},{7,6},{8,9},{9,8},{10,11... | collective-permute-start | bytes 393224 | tf_op jit(solution)/shard_map/ppermute | solution.py:133
  29.5 0.0 collective-permute-done.14.refs_6_
  29.5 0.0 collective-permute-done.15.refs_7_
  29.5 2.0 %shard_map.48 = (f32[256,512]{1,0:T(8,128)S(1)}, f32[256,512]{1,0:T(8,128)S(1)}, f32[256,512]{1,0:T(8,128)S(1)}, f32[256,512]{1,0:T(8,128)S(1)}) custom-call(s32[1]{0:T(128)S(6)} %copy.13.code_ref, bf16[256,256]{1,0:T(8,128)(2,1)S(1)} %get-tuple-element.24.refs_0_.refs_2_, ...), custom_call_target="tpu_custom_call", output_to_operand_aliasing={{0}: (9, {}), {1}: (10, {}), {2}: (11, {}), {3}: (12, {})} | custom-call | tf_op jit(solution)/shard_map/pallas_call | solution.py:105
  31.5 0.0 collective-permute-done.12.refs_5_.refs_3_
  31.5 0.0 collective-permute-done.13.refs_6_.refs_4_
  31.5 0.7 %shard_map.50 = bf16[256,512]{1,0:T(8,128)(2,1)S(1)} custom-call(s32[1]{0:T(128)S(6)} %copy.13.code_ref, bf16[256,256]{1,0:T(8,128)(2,1)S(1)} %collective-permute-done.3.refs_3_.refs_0_, bf16[256,256]{1,0:T(8,128)(2,1)S(1)} %collective-permute-done.4.refs_3_.refs_1_, bf16[256,512]{1,0:T(8,128)(2,1)S(1)} %collective-permute-done.6.refs_4_.refs_2_, ...), custom_call_target="tpu_custom_call" | custom-call | tf_op jit(solution)/shard_map/pallas_call | solution.py:105
  32.2 1.8 %collective-permute-start.16 = (bf16[256,512]{1,0:T(8,128)(2,1)S(1)}, bf16[256,512]{1,0:T(8,128)(2,1)S(1)}, u32[]{:S(2)}, u32[]{:S(2)}) collective-permute-start(bf16[256,512]{1,0:T(8,128)(2,1)S(1)} %shard_map.50), channel_id=1, source_target_pairs={{0,10},{1,11},{2,8},{3,9},{4,14},{5,15},{6,12},{7,13},{8,2},{9,3},... | collective-permute-start | bytes 786440 | tf_op jit(solution)/shard_map/ppermute | solution.py:133
  34.1 1.4 %shard_map.49 = (bf16[256,512]{1,0:T(8,128)(2,1)S(1)}, bf16[256,512]{1,0:T(8,128)(2,1)S(1)}, f32[256,512]{1,0:T(8,128)S(1)}) custom-call(s32[1]{0:T(128)S(6)} %copy.13.code_ref, bf16[256,256]{1,0:T(8,128)(2,1)S(1)} %collective-permute-done.refs_1_.refs_0_, bf16[256,256]{1,0:T(8,128)(2,1)S(1)} %collective-permute-done.1.refs_2_.refs_1_, ...), custom_call_target="tpu_custom_call" | custom-call | tf_op jit(solution)/shard_map/pallas_call | solution.py:105
  35.5 0.6 %collective-permute-start.17 = (bf16[256,512]{1,0:T(8,128)(2,1)S(1)}, bf16[256,512]{1,0:T(8,128)(2,1)S(1)}, u32[]{:S(2)}, u32[]{:S(2)}) collective-permute-start(bf16[256,512]{1,0:T(8,128)(2,1)S(1)} %get-tuple-element.39), channel_id=1, source_target_pairs={{0,8},{1,9},{2,10},{3,11},{4,12},{5,13},{6,14},{7,15},{8,0},{9,1},... | collective-permute-start | bytes 786440 | tf_op jit(solution)/shard_map/ppermute | solution.py:133
  36.1 1.2 %collective-permute-start.18 = (bf16[256,512]{1,0:T(8,128)(2,1)S(1)}, bf16[256,512]{1,0:T(8,128)(2,1)S(1)}, u32[]{:S(2)}, u32[]{:S(2)}) collective-permute-start(bf16[256,512]{1,0:T(8,128)(2,1)S(1)} %get-tuple-element.40), channel_id=1, source_target_pairs={{0,2},{1,3},{2,0},{3,1},{4,6},{5,7},{6,4},{7,5},{8,10},{9,11},{10,... | collective-permute-start | bytes 786440 | tf_op jit(solution)/shard_map/ppermute | solution.py:133
  37.3 5.1 %collective-permute-done.16.refs_1_ = bf16[256,512]{1,0:T(8,128)(2,1)S(1)} collective-permute-done((bf16[256,512]{1,0:T(8,128)(2,1)S(1)}, bf16[256,512]{1,0:T(8,128)(2,1)S(1)}, u32[]{:S(2)}, u32[]{:S(2)}) %collective-permute-start.16) | collective-permute-done | bytes 262176 | tf_op jit(solution)/shard_map/ppermute | solution.py:133
  42.4 4.7 %collective-permute-done.17.refs_2_ = bf16[256,512]{1,0:T(8,128)(2,1)S(1)} collective-permute-done((bf16[256,512]{1,0:T(8,128)(2,1)S(1)}, bf16[256,512]{1,0:T(8,128)(2,1)S(1)}, u32[]{:S(2)}, u32[]{:S(2)}) %collective-permute-start.17) | collective-permute-done | bytes 262176 | tf_op jit(solution)/shard_map/ppermute | solution.py:133
  47.1 0.1 collective-permute-done.18.refs_3_
  47.2 0.9 %shard_map.51 = f32[256,512]{1,0:T(8,128)} custom-call(f32[256,128]{1,0:T(8,128)S(1)} %get-tuple-element.23.sigma_ref, f32[256,512]{1,0:T(8,128)S(1)} %get-tuple-element.37.refs_0_, bf16[256,512]{1,0:T(8,128)(2,1)S(1)} %collective-permute-done.16.refs_1_, bf16[256,512]{1,0:T(8,128)(2,1)S(1)} %collective-permute-done.17.refs_2_, ...), custom_call_target="tpu_custom_call" | custom-call | tf_op jit(solution)/shard_map/pallas_call | solution.py:105
Async XLA Ops:
  0.0 6.9 %copy-start = (bf16[256,512]{1,0:T(8,128)(2,1)S(1)}, bf16[256,512]{1,0:T(8,128)(2,1)}, u32[]{:S(2)}) copy-start(bf16[256,512]{1,0:T(8,128)(2,1)} %w_hbm.1) | copy-start | bytes 786436
  0.0 16.2 %collective-permute-start.5 = (bf16[256,512]{1,0:T(8,128)(2,1)}, bf16[256,512]{1,0:T(8,128)(2,1)S(1)}, u32[]{:S(2)}, u32[]{:S(2)}) collective-permute-start(bf16[256,512]{1,0:T(8,128)(2,1)} %w_hbm.1), channel_id=1, source_target_pairs={{0,4},{1,5},{2,6},{3,7},{4,0},{5,1},{6,2},{7,3},{8,12},{9,13},{10,... | collective-permute-start | bytes 786440 | tf_op jit(solution)/shard_map/ppermute | solution.py:133
  5.3 7.4 %collective-permute-start.1 = (bf16[256,256]{1,0:T(8,128)(2,1)S(1)}, bf16[256,256]{1,0:T(8,128)(2,1)S(1)}, u32[]{:S(2)}, u32[]{:S(2)}) collective-permute-start(bf16[256,256]{1,0:T(8,128)(2,1)S(1)} %get-tuple-element.24.refs_0_.refs_2_), channel_id=1, source_target_pairs={{0,2},{1,3},{2,0},{3,1},{4,6},{5,7},{6,4},{7,5},{8,10},{9,11},{10,... | collective-permute-start | bytes 393224 | tf_op jit(solution)/shard_map/ppermute | solution.py:133
  6.9 11.7 %collective-permute-start.7 = (bf16[256,512]{1,0:T(8,128)(2,1)S(1)}, bf16[256,512]{1,0:T(8,128)(2,1)S(1)}, u32[]{:S(2)}, u32[]{:S(2)}) collective-permute-start(bf16[256,512]{1,0:T(8,128)(2,1)S(1)} %copy-done), channel_id=1, source_target_pairs={{0,16},{1,17},{2,18},{3,19},{4,20},{5,21},{6,22},{7,23},{8,24},{9,... | collective-permute-start | bytes 786440 | tf_op jit(solution)/shard_map/ppermute | solution.py:133
  8.4 5.0 %collective-permute-start = (bf16[256,256]{1,0:T(8,128)(2,1)S(1)}, bf16[256,256]{1,0:T(8,128)(2,1)S(1)}, u32[]{:S(2)}, u32[]{:S(2)}) collective-permute-start(bf16[256,256]{1,0:T(8,128)(2,1)S(1)} %get-tuple-element.24.refs_0_.refs_2_), channel_id=1, source_target_pairs={{0,8},{1,9},{2,10},{3,11},{4,12},{5,13},{6,14},{7,15},{8,0},{9,1},... | collective-permute-start | bytes 393224 | tf_op jit(solution)/shard_map/ppermute | solution.py:133
  9.9 7.8 %collective-permute-start.9 = (bf16[256,256]{1,0:T(8,128)(2,1)S(1)}, bf16[256,256]{1,0:T(8,128)(2,1)S(1)}, u32[]{:S(2)}, u32[]{:S(2)}) collective-permute-start(bf16[256,256]{1,0:T(8,128)(2,1)S(1)} %get-tuple-element.24.refs_0_.refs_2_), channel_id=1, source_target_pairs={{0,16},{1,17},{2,18},{3,19},{4,20},{5,21},{6,22},{7,23},{8,24},{9,... | collective-permute-start | bytes 393224 | tf_op jit(solution)/shard_map/ppermute | solution.py:133
  12.7 13.0 %collective-permute-start.8 = (bf16[256,768]{1,0:T(8,128)(2,1)S(1)}, bf16[256,768]{1,0:T(8,128)(2,1)S(1)}, u32[]{:S(2)}, u32[]{:S(2)}) collective-permute-start(bf16[256,768]{1,0:T(8,128)(2,1)S(1)} %get-tuple-element.28.refs_4_), channel_id=1, source_target_pairs={{0,1},{1,0},{2,3},{3,2},{4,5},{5,4},{6,7},{7,6},{8,9},{9,8},{10,11... | collective-permute-start | bytes 1179656 | tf_op jit(solution)/shard_map/ppermute | solution.py:133
  13.4 9.0 %collective-permute-start.2 = (bf16[256,256]{1,0:T(8,128)(2,1)S(1)}, bf16[256,256]{1,0:T(8,128)(2,1)S(1)}, u32[]{:S(2)}, u32[]{:S(2)}) collective-permute-start(bf16[256,256]{1,0:T(8,128)(2,1)S(1)} %get-tuple-element.24.refs_0_.refs_2_), channel_id=1, source_target_pairs={{0,4},{1,5},{2,6},{3,7},{4,0},{5,1},{6,2},{7,3},{8,12},{9,13},{10,... | collective-permute-start | bytes 393224 | tf_op jit(solution)/shard_map/ppermute | solution.py:133
  16.2 8.3 %collective-permute-start.6 = (bf16[256,512]{1,0:T(8,128)(2,1)S(1)}, bf16[256,512]{1,0:T(8,128)(2,1)S(1)}, u32[]{:S(2)}, u32[]{:S(2)}) collective-permute-start(bf16[256,512]{1,0:T(8,128)(2,1)S(1)} %collective-permute-done.5.refs_5_), channel_id=1, source_target_pairs={{0,16},{1,17},{2,18},{3,19},{4,20},{5,21},{6,22},{7,23},{8,24},{9,... | collective-permute-start | bytes 786440 | tf_op jit(solution)/shard_map/ppermute | solution.py:133
  17.8 5.8 %collective-permute-start.3 = (bf16[256,256]{1,0:T(8,128)(2,1)S(1)}, bf16[256,256]{1,0:T(8,128)(2,1)S(1)}, u32[]{:S(2)}, u32[]{:S(2)}) collective-permute-start(bf16[256,256]{1,0:T(8,128)(2,1)S(1)} %collective-permute-done.refs_1_.refs_0_), channel_id=1, source_target_pairs={{0,2},{1,3},{2,0},{3,1},{4,6},{5,7},{6,4},{7,5},{8,10},{9,11},{10,... | collective-permute-start | bytes 393224 | tf_op jit(solution)/shard_map/ppermute | solution.py:133
  18.6 7.2 %collective-permute-start.11 = (bf16[256,512]{1,0:T(8,128)(2,1)S(1)}, bf16[256,512]{1,0:T(8,128)(2,1)S(1)}, u32[]{:S(2)}, u32[]{:S(2)}) collective-permute-start(bf16[256,512]{1,0:T(8,128)(2,1)S(1)} %collective-permute-done.7.refs_7_), channel_id=1, source_target_pairs={{0,1},{1,0},{2,3},{3,2},{4,5},{5,4},{6,7},{7,6},{8,9},{9,8},{10,11... | collective-permute-start | bytes 786440 | tf_op jit(solution)/shard_map/ppermute | solution.py:133
  22.4 2.1 %collective-permute-start.10 = (bf16[256,256]{1,0:T(8,128)(2,1)S(1)}, bf16[256,256]{1,0:T(8,128)(2,1)S(1)}, u32[]{:S(2)}, u32[]{:S(2)}) collective-permute-start(bf16[256,256]{1,0:T(8,128)(2,1)S(1)} %collective-permute-done.9.refs_6_), channel_id=1, source_target_pairs={{0,1},{1,0},{2,3},{3,2},{4,5},{5,4},{6,7},{7,6},{8,9},{9,8},{10,11... | collective-permute-start | bytes 393224 | tf_op jit(solution)/shard_map/ppermute | solution.py:133
  23.5 5.4 %collective-permute-start.4 = (bf16[256,256]{1,0:T(8,128)(2,1)S(1)}, bf16[256,256]{1,0:T(8,128)(2,1)S(1)}, u32[]{:S(2)}, u32[]{:S(2)}) collective-permute-start(bf16[256,256]{1,0:T(8,128)(2,1)S(1)} %collective-permute-done.2.refs_4_), channel_id=1, source_target_pairs={{0,16},{1,17},{2,18},{3,19},{4,20},{5,21},{6,22},{7,23},{8,24},{9,... | collective-permute-start | bytes 393224 | tf_op jit(solution)/shard_map/ppermute | solution.py:133
  24.5 5.0 %collective-permute-start.15 = (bf16[256,512]{1,0:T(8,128)(2,1)S(1)}, bf16[256,512]{1,0:T(8,128)(2,1)S(1)}, u32[]{:S(2)}, u32[]{:S(2)}) collective-permute-start(bf16[256,512]{1,0:T(8,128)(2,1)S(1)} %collective-permute-done.5.refs_5_), channel_id=1, source_target_pairs={{0,1},{1,0},{2,3},{3,2},{4,5},{5,4},{6,7},{7,6},{8,9},{9,8},{10,11... | collective-permute-start | bytes 786440 | tf_op jit(solution)/shard_map/ppermute | solution.py:133
  24.5 7.0 %collective-permute-start.13 = (bf16[256,512]{1,0:T(8,128)(2,1)S(1)}, bf16[256,512]{1,0:T(8,128)(2,1)S(1)}, u32[]{:S(2)}, u32[]{:S(2)}) collective-permute-start(bf16[256,512]{1,0:T(8,128)(2,1)S(1)} %collective-permute-done.6.refs_4_.refs_2_), channel_id=1, source_target_pairs={{0,1},{1,0},{2,3},{3,2},{4,5},{5,4},{6,7},{7,6},{8,9},{9,8},{10,11... | collective-permute-start | bytes 786440 | tf_op jit(solution)/shard_map/ppermute | solution.py:133
  25.7 3.8 %collective-permute-start.14 = (bf16[256,256]{1,0:T(8,128)(2,1)S(1)}, bf16[256,256]{1,0:T(8,128)(2,1)S(1)}, u32[]{:S(2)}, u32[]{:S(2)}) collective-permute-start(bf16[256,256]{1,0:T(8,128)(2,1)S(1)} %collective-permute-done.2.refs_4_), channel_id=1, source_target_pairs={{0,1},{1,0},{2,3},{3,2},{4,5},{5,4},{6,7},{7,6},{8,9},{9,8},{10,11... | collective-permute-start | bytes 393224 | tf_op jit(solution)/shard_map/ppermute | solution.py:133
  28.9 2.6 %collective-permute-start.12 = (bf16[256,256]{1,0:T(8,128)(2,1)S(1)}, bf16[256,256]{1,0:T(8,128)(2,1)S(1)}, u32[]{:S(2)}, u32[]{:S(2)}) collective-permute-start(bf16[256,256]{1,0:T(8,128)(2,1)S(1)} %collective-permute-done.4.refs_3_.refs_1_), channel_id=1, source_target_pairs={{0,1},{1,0},{2,3},{3,2},{4,5},{5,4},{6,7},{7,6},{8,9},{9,8},{10,11... | collective-permute-start | bytes 393224 | tf_op jit(solution)/shard_map/ppermute | solution.py:133
  32.2 10.2 %collective-permute-start.16 = (bf16[256,512]{1,0:T(8,128)(2,1)S(1)}, bf16[256,512]{1,0:T(8,128)(2,1)S(1)}, u32[]{:S(2)}, u32[]{:S(2)}) collective-permute-start(bf16[256,512]{1,0:T(8,128)(2,1)S(1)} %shard_map.50), channel_id=1, source_target_pairs={{0,10},{1,11},{2,8},{3,9},{4,14},{5,15},{6,12},{7,13},{8,2},{9,3},... | collective-permute-start | bytes 786440 | tf_op jit(solution)/shard_map/ppermute | solution.py:133
  35.5 11.6 %collective-permute-start.17 = (bf16[256,512]{1,0:T(8,128)(2,1)S(1)}, bf16[256,512]{1,0:T(8,128)(2,1)S(1)}, u32[]{:S(2)}, u32[]{:S(2)}) collective-permute-start(bf16[256,512]{1,0:T(8,128)(2,1)S(1)} %get-tuple-element.39), channel_id=1, source_target_pairs={{0,8},{1,9},{2,10},{3,11},{4,12},{5,13},{6,14},{7,15},{8,0},{9,1},... | collective-permute-start | bytes 786440 | tf_op jit(solution)/shard_map/ppermute | solution.py:133
  36.1 11.1 %collective-permute-start.18 = (bf16[256,512]{1,0:T(8,128)(2,1)S(1)}, bf16[256,512]{1,0:T(8,128)(2,1)S(1)}, u32[]{:S(2)}, u32[]{:S(2)}) collective-permute-start(bf16[256,512]{1,0:T(8,128)(2,1)S(1)} %get-tuple-element.40), channel_id=1, source_target_pairs={{0,2},{1,3},{2,0},{3,1},{4,6},{5,7},{6,4},{7,5},{8,10},{9,11},{10,... | collective-permute-start | bytes 786440 | tf_op jit(solution)/shard_map/ppermute | solution.py:133

commit v7 on v6

--- a/solution.py
+++ b/solution.py
@@ -94,19 +94,29 @@
 
 
 def final_kernel(sigma_ref, *refs):
-    out_ref = refs[-1]
-    total = refs[0][...]
-    for r in refs[1:-1]:
-        total = total + r[...].astype(jnp.float32)
-    out_ref[...] = sigma_ref[:, :1] * total
-
-
-def call(kernel, args, outs, specs=None, scratch=(), aliases=None):
+    out_hbm, out_ref, sems = refs[-3:]
+    rows = out_ref.shape[0]
+    parts = sems.shape[0]
+    step = rows // parts
+    stores = []
+    for k in range(parts):
+        at = slice(k * step, (k + 1) * step)
+        total = refs[0][at]
+        for r in refs[1:-3]:
+            total = total + r[at].astype(jnp.float32)
+        out_ref[at] = sigma_ref[at, :1] * total
+        stores.append(pltpu.make_async_copy(out_ref.at[at], out_hbm.at[at], sems.at[k]))
+        stores[-1].start()
+    for store in stores:
+        store.wait()
+
+
+def call(kernel, args, outs, specs=None, scratch=(), aliases=None, out_spec=None):
     return pl.pallas_call(
         kernel,
         out_shape=outs,
         in_specs=specs or [vspec() for _ in args],
-        out_specs=jax.tree.map(lambda _: vspec(), outs),
+        out_specs=out_spec or jax.tree.map(lambda _: vspec(), outs),
         scratch_shapes=scratch,
         input_output_aliases=aliases or {},
         compiler_params=pltpu.CompilerParams(vmem_limit_bytes=48 * 1024 * 1024),
@@ -202,7 +212,13 @@
     arrived = [total[0]]
     for i, x, zl in ((3, 1, 1), (1, 1, 0), (2, 0, 1)):
         arrived.append(send(total[i], x=x, zl=zl))
-    return call(final_kernel, (sigma, *arrived), shape((own, ports), jnp.float32))
+    return call(
+        final_kernel,
+        (sigma, *arrived),
+        shape((own, ports), jnp.float32),
+        scratch=[VMEM((own, ports), jnp.float32), pltpu.SemaphoreType.DMA((4,))],
+        out_spec=pl.BlockSpec(memory_space=pltpu.HBM),
+    )
 
 
 def solution(mesh):

time: 48.2 us -> 48.2 us (level)
  no operation moved by 1% of the time
where the time goes in v7:
time: 48.2 us; the launch traced here: 48.1 us
  starting transfers between devices  19 us (39%)
  waiting for transfers between devices  19 us (39%)
  Pallas kernels  9.4 us (20%)
  between operations  0.74 us (2%)
    ppermute x19, starting transfers between devices, send(): return lax.ppermute(value, ('row', 'col'), pairs)  19 us
    ppermute x19, waiting for transfers between devices, send(): return lax.ppermute(value, ('row', 'col'), pairs)  19 us
    pallas_call x6, Pallas kernels, call(): pl.pallas_call(kernel, out_shape=outs, in_specs=specs or [vspec() for _ i...  9.4 us
  transfers between devices with their start and end apart: 19, of which 8 were waited for; matrix products, arithmetic and copies ran while one was open for 0% of the time, Pallas kernels for 16%

profile of v7, /device:TPU:0, one launch (start us, length us, event | category | flops | bytes accessed | tf_op | source)
XLA Modules:
  0.0 48.1 jit_solution(715397710779674755)
XLA Ops:
  0.0 0.0 copy-start
  0.0 4.0 %collective-permute-start.5 = (bf16[256,512]{1,0:T(8,128)(2,1)}, bf16[256,512]{1,0:T(8,128)(2,1)S(1)}, u32[]{:S(2)}, u32[]{:S(2)}) collective-permute-start(bf16[256,512]{1,0:T(8,128)(2,1)} %w_hbm.1), channel_id=1, source_target_pairs={{0,4},{1,5},{2,6},{3,7},{4,0},{5,1},{6,2},{7,3},{8,12},{9,13},{10,... | collective-permute-start | bytes 786440 | tf_op jit(solution)/shard_map/ppermute | solution.py:143
  4.0 1.2 %shard_map.46 = (bf16[256,256]{1,0:T(8,128)(2,1)S(1)}, bf16[256,768]{1,0:T(8,128)(2,1)S(1)}, f32[256,128]{1,0:T(8,128)S(1)}) custom-call(s32[1,256]{1,0:T(1,128)} %bitcast.1, bf16[256,256]{1,0:T(8,128)(2,1)} %ret_hbm.1, bf16[256,512]{1,0:T(8,128)(2,1)} %w_hbm.1), custom_call_target="tpu_custom_call" | custom-call | tf_op jit(solution)/shard_map/pallas_call | solution.py:115
  5.3 1.6 %collective-permute-start.1 = (bf16[256,256]{1,0:T(8,128)(2,1)S(1)}, bf16[256,256]{1,0:T(8,128)(2,1)S(1)}, u32[]{:S(2)}, u32[]{:S(2)}) collective-permute-start(bf16[256,256]{1,0:T(8,128)(2,1)S(1)} %get-tuple-element.24.refs_0_.refs_2_), channel_id=1, source_target_pairs={{0,2},{1,3},{2,0},{3,1},{4,6},{5,7},{6,4},{7,5},{8,10},{9,11},{10,... | collective-permute-start | bytes 393224 | tf_op jit(solution)/shard_map/ppermute | solution.py:143
  6.9 0.0 copy-done
  6.9 1.5 %collective-permute-start.7 = (bf16[256,512]{1,0:T(8,128)(2,1)S(1)}, bf16[256,512]{1,0:T(8,128)(2,1)S(1)}, u32[]{:S(2)}, u32[]{:S(2)}) collective-permute-start(bf16[256,512]{1,0:T(8,128)(2,1)S(1)} %copy-done), channel_id=1, source_target_pairs={{0,16},{1,17},{2,18},{3,19},{4,20},{5,21},{6,22},{7,23},{8,24},{9,... | collective-permute-start | bytes 786440 | tf_op jit(solution)/shard_map/ppermute | solution.py:143
  8.4 1.5 %collective-permute-start = (bf16[256,256]{1,0:T(8,128)(2,1)S(1)}, bf16[256,256]{1,0:T(8,128)(2,1)S(1)}, u32[]{:S(2)}, u32[]{:S(2)}) collective-permute-start(bf16[256,256]{1,0:T(8,128)(2,1)S(1)} %get-tuple-element.24.refs_0_.refs_2_), channel_id=1, source_target_pairs={{0,8},{1,9},{2,10},{3,11},{4,12},{5,13},{6,14},{7,15},{8,0},{9,1},... | collective-permute-start | bytes 393224 | tf_op jit(solution)/shard_map/ppermute | solution.py:143
  9.9 0.5 %collective-permute-start.9 = (bf16[256,256]{1,0:T(8,128)(2,1)S(1)}, bf16[256,256]{1,0:T(8,128)(2,1)S(1)}, u32[]{:S(2)}, u32[]{:S(2)}) collective-permute-start(bf16[256,256]{1,0:T(8,128)(2,1)S(1)} %get-tuple-element.24.refs_0_.refs_2_), channel_id=1, source_target_pairs={{0,16},{1,17},{2,18},{3,19},{4,20},{5,21},{6,22},{7,23},{8,24},{9,... | collective-permute-start | bytes 393224 | tf_op jit(solution)/shard_map/ppermute | solution.py:143
  10.4 2.2 %collective-permute-done.1.refs_2_.refs_1_ = bf16[256,256]{1,0:T(8,128)(2,1)S(1)} collective-permute-done((bf16[256,256]{1,0:T(8,128)(2,1)S(1)}, bf16[256,256]{1,0:T(8,128)(2,1)S(1)}, u32[]{:S(2)}, u32[]{:S(2)}) %collective-permute-start.1) | collective-permute-done | bytes 131104 | tf_op jit(solution)/shard_map/ppermute | solution.py:143
  12.7 0.0 collective-permute-start.8
  12.7 0.7 %collective-permute-done.refs_1_.refs_0_ = bf16[256,256]{1,0:T(8,128)(2,1)S(1)} collective-permute-done((bf16[256,256]{1,0:T(8,128)(2,1)S(1)}, bf16[256,256]{1,0:T(8,128)(2,1)S(1)}, u32[]{:S(2)}, u32[]{:S(2)}) %collective-permute-start) | collective-permute-done | bytes 131104 | tf_op jit(solution)/shard_map/ppermute | solution.py:143
  13.4 1.7 %collective-permute-start.2 = (bf16[256,256]{1,0:T(8,128)(2,1)S(1)}, bf16[256,256]{1,0:T(8,128)(2,1)S(1)}, u32[]{:S(2)}, u32[]{:S(2)}) collective-permute-start(bf16[256,256]{1,0:T(8,128)(2,1)S(1)} %get-tuple-element.24.refs_0_.refs_2_), channel_id=1, source_target_pairs={{0,4},{1,5},{2,6},{3,7},{4,0},{5,1},{6,2},{7,3},{8,12},{9,13},{10,... | collective-permute-start | bytes 393224 | tf_op jit(solution)/shard_map/ppermute | solution.py:143
  15.1 1.2 %collective-permute-done.5.refs_5_ = bf16[256,512]{1,0:T(8,128)(2,1)S(1)} collective-permute-done((bf16[256,512]{1,0:T(8,128)(2,1)}, bf16[256,512]{1,0:T(8,128)(2,1)S(1)}, u32[]{:S(2)}, u32[]{:S(2)}) %collective-permute-start.5) | collective-permute-done | bytes 262176 | tf_op jit(solution)/shard_map/ppermute | solution.py:143
  16.2 1.5 %collective-permute-start.6 = (bf16[256,512]{1,0:T(8,128)(2,1)S(1)}, bf16[256,512]{1,0:T(8,128)(2,1)S(1)}, u32[]{:S(2)}, u32[]{:S(2)}) collective-permute-start(bf16[256,512]{1,0:T(8,128)(2,1)S(1)} %collective-permute-done.5.refs_5_), channel_id=1, source_target_pairs={{0,16},{1,17},{2,18},{3,19},{4,20},{5,21},{6,22},{7,23},{8,24},{9,... | collective-permute-start | bytes 786440 | tf_op jit(solution)/shard_map/ppermute | solution.py:143
  17.8 0.0 collective-permute-done.9.refs_6_
  17.8 0.9 %collective-permute-start.3 = (bf16[256,256]{1,0:T(8,128)(2,1)S(1)}, bf16[256,256]{1,0:T(8,128)(2,1)S(1)}, u32[]{:S(2)}, u32[]{:S(2)}) collective-permute-start(bf16[256,256]{1,0:T(8,128)(2,1)S(1)} %collective-permute-done.refs_1_.refs_0_), channel_id=1, source_target_pairs={{0,2},{1,3},{2,0},{3,1},{4,6},{5,7},{6,4},{7,5},{8,10},{9,11},{10,... | collective-permute-start | bytes 393224 | tf_op jit(solution)/shard_map/ppermute | solution.py:143
  18.6 0.0 collective-permute-done.7.refs_7_
  18.6 0.0 collective-permute-start.11
  18.6 3.8 %collective-permute-done.2.refs_4_ = bf16[256,256]{1,0:T(8,128)(2,1)S(1)} collective-permute-done((bf16[256,256]{1,0:T(8,128)(2,1)S(1)}, bf16[256,256]{1,0:T(8,128)(2,1)S(1)}, u32[]{:S(2)}, u32[]{:S(2)}) %collective-permute-start.2) | collective-permute-done | bytes 131104 | tf_op jit(solution)/shard_map/ppermute | solution.py:143
  22.4 0.0 collective-permute-start.10
  22.4 1.1 %collective-permute-done.3.refs_3_.refs_0_ = bf16[256,256]{1,0:T(8,128)(2,1)S(1)} collective-permute-done((bf16[256,256]{1,0:T(8,128)(2,1)S(1)}, bf16[256,256]{1,0:T(8,128)(2,1)S(1)}, u32[]{:S(2)}, u32[]{:S(2)}) %collective-permute-start.3) | collective-permute-done | bytes 131104 | tf_op jit(solution)/shard_map/ppermute | solution.py:143
  23.5 1.0 %collective-permute-start.4 = (bf16[256,256]{1,0:T(8,128)(2,1)S(1)}, bf16[256,256]{1,0:T(8,128)(2,1)S(1)}, u32[]{:S(2)}, u32[]{:S(2)}) collective-permute-start(bf16[256,256]{1,0:T(8,128)(2,1)S(1)} %collective-permute-done.2.refs_4_), channel_id=1, source_target_pairs={{0,16},{1,17},{2,18},{3,19},{4,20},{5,21},{6,22},{7,23},{8,24},{9,... | collective-permute-start | bytes 393224 | tf_op jit(solution)/shard_map/ppermute | solution.py:143
  24.5 0.0 collective-permute-done.10.refs_8_
  24.5 0.0 collective-permute-start.15
  24.5 0.0 collective-permute-done.6.refs_4_.refs_2_
  24.5 0.5 %collective-permute-start.13 = (bf16[256,512]{1,0:T(8,128)(2,1)S(1)}, bf16[256,512]{1,0:T(8,128)(2,1)S(1)}, u32[]{:S(2)}, u32[]{:S(2)}) collective-permute-start(bf16[256,512]{1,0:T(8,128)(2,1)S(1)} %collective-permute-done.6.refs_4_.refs_2_), channel_id=1, source_target_pairs={{0,1},{1,0},{2,3},{3,2},{4,5},{5,4},{6,7},{7,6},{8,9},{9,8},{10,11... | collective-permute-start | bytes 786440 | tf_op jit(solution)/shard_map/ppermute | solution.py:143
  25.7 0.0 collective-permute-done.8.refs_5_
  25.7 0.1 collective-permute-start.14
  25.8 0.0 collective-permute-done.11.refs_9_
  25.8 3.1 %shard_map.47 = (f32[256,512]{1,0:T(8,128)S(1)}, f32[256,512]{1,0:T(8,128)S(1)}, f32[256,512]{1,0:T(8,128)S(1)}, f32[256,512]{1,0:T(8,128)S(1)}) custom-call(s32[1]{0:T(128)S(6)} %copy.13.code_ref, bf16[256,256]{1,0:T(8,128)(2,1)S(1)} %get-tuple-element.24.refs_0_.refs_2_, bf16[256,256]{1,0:T(8,128)(2,1)S(1)} %collective-permute-done.refs_1_.refs_0_, ...), custom_call_target="tpu_custom_call" | custom-call | tf_op jit(solution)/shard_map/pallas_call | solution.py:115
  28.9 0.0 collective-permute-done.4.refs_3_.refs_1_
  28.9 0.5 %collective-permute-start.12 = (bf16[256,256]{1,0:T(8,128)(2,1)S(1)}, bf16[256,256]{1,0:T(8,128)(2,1)S(1)}, u32[]{:S(2)}, u32[]{:S(2)}) collective-permute-start(bf16[256,256]{1,0:T(8,128)(2,1)S(1)} %collective-permute-done.4.refs_3_.refs_1_), channel_id=1, source_target_pairs={{0,1},{1,0},{2,3},{3,2},{4,5},{5,4},{6,7},{7,6},{8,9},{9,8},{10,11... | collective-permute-start | bytes 393224 | tf_op jit(solution)/shard_map/ppermute | solution.py:143
  29.5 0.0 collective-permute-done.14.refs_6_
  29.5 0.0 collective-permute-done.15.refs_7_
  29.5 2.0 %shard_map.48 = (f32[256,512]{1,0:T(8,128)S(1)}, f32[256,512]{1,0:T(8,128)S(1)}, f32[256,512]{1,0:T(8,128)S(1)}, f32[256,512]{1,0:T(8,128)S(1)}) custom-call(s32[1]{0:T(128)S(6)} %copy.13.code_ref, bf16[256,256]{1,0:T(8,128)(2,1)S(1)} %get-tuple-element.24.refs_0_.refs_2_, ...), custom_call_target="tpu_custom_call", output_to_operand_aliasing={{0}: (9, {}), {1}: (10, {}), {2}: (11, {}), {3}: (12, {})} | custom-call | tf_op jit(solution)/shard_map/pallas_call | solution.py:115
  31.5 0.0 collective-permute-done.12.refs_5_.refs_3_
  31.5 0.0 collective-permute-done.13.refs_6_.refs_4_
  31.5 0.7 %shard_map.50 = bf16[256,512]{1,0:T(8,128)(2,1)S(1)} custom-call(s32[1]{0:T(128)S(6)} %copy.13.code_ref, bf16[256,256]{1,0:T(8,128)(2,1)S(1)} %collective-permute-done.3.refs_3_.refs_0_, bf16[256,256]{1,0:T(8,128)(2,1)S(1)} %collective-permute-done.4.refs_3_.refs_1_, bf16[256,512]{1,0:T(8,128)(2,1)S(1)} %collective-permute-done.6.refs_4_.refs_2_, ...), custom_call_target="tpu_custom_call" | custom-call | tf_op jit(solution)/shard_map/pallas_call | solution.py:115
  32.2 1.8 %collective-permute-start.16 = (bf16[256,512]{1,0:T(8,128)(2,1)S(1)}, bf16[256,512]{1,0:T(8,128)(2,1)S(1)}, u32[]{:S(2)}, u32[]{:S(2)}) collective-permute-start(bf16[256,512]{1,0:T(8,128)(2,1)S(1)} %shard_map.50), channel_id=1, source_target_pairs={{0,10},{1,11},{2,8},{3,9},{4,14},{5,15},{6,12},{7,13},{8,2},{9,3},... | collective-permute-start | bytes 786440 | tf_op jit(solution)/shard_map/ppermute | solution.py:143
  34.1 1.4 %shard_map.49 = (bf16[256,512]{1,0:T(8,128)(2,1)S(1)}, bf16[256,512]{1,0:T(8,128)(2,1)S(1)}, f32[256,512]{1,0:T(8,128)S(1)}) custom-call(s32[1]{0:T(128)S(6)} %copy.13.code_ref, bf16[256,256]{1,0:T(8,128)(2,1)S(1)} %collective-permute-done.refs_1_.refs_0_, bf16[256,256]{1,0:T(8,128)(2,1)S(1)} %collective-permute-done.1.refs_2_.refs_1_, ...), custom_call_target="tpu_custom_call" | custom-call | tf_op jit(solution)/shard_map/pallas_call | solution.py:115
  35.5 0.6 %collective-permute-start.17 = (bf16[256,512]{1,0:T(8,128)(2,1)S(1)}, bf16[256,512]{1,0:T(8,128)(2,1)S(1)}, u32[]{:S(2)}, u32[]{:S(2)}) collective-permute-start(bf16[256,512]{1,0:T(8,128)(2,1)S(1)} %get-tuple-element.39), channel_id=1, source_target_pairs={{0,8},{1,9},{2,10},{3,11},{4,12},{5,13},{6,14},{7,15},{8,0},{9,1},... | collective-permute-start | bytes 786440 | tf_op jit(solution)/shard_map/ppermute | solution.py:143
  36.1 1.2 %collective-permute-start.18 = (bf16[256,512]{1,0:T(8,128)(2,1)S(1)}, bf16[256,512]{1,0:T(8,128)(2,1)S(1)}, u32[]{:S(2)}, u32[]{:S(2)}) collective-permute-start(bf16[256,512]{1,0:T(8,128)(2,1)S(1)} %get-tuple-element.40), channel_id=1, source_target_pairs={{0,2},{1,3},{2,0},{3,1},{4,6},{5,7},{6,4},{7,5},{8,10},{9,11},{10,... | collective-permute-start | bytes 786440 | tf_op jit(solution)/shard_map/ppermute | solution.py:143
  37.3 5.1 %collective-permute-done.16.refs_1_ = bf16[256,512]{1,0:T(8,128)(2,1)S(1)} collective-permute-done((bf16[256,512]{1,0:T(8,128)(2,1)S(1)}, bf16[256,512]{1,0:T(8,128)(2,1)S(1)}, u32[]{:S(2)}, u32[]{:S(2)}) %collective-permute-start.16) | collective-permute-done | bytes 262176 | tf_op jit(solution)/shard_map/ppermute | solution.py:143
  42.4 4.7 %collective-permute-done.17.refs_2_ = bf16[256,512]{1,0:T(8,128)(2,1)S(1)} collective-permute-done((bf16[256,512]{1,0:T(8,128)(2,1)S(1)}, bf16[256,512]{1,0:T(8,128)(2,1)S(1)}, u32[]{:S(2)}, u32[]{:S(2)}) %collective-permute-start.17) | collective-permute-done | bytes 262176 | tf_op jit(solution)/shard_map/ppermute | solution.py:143
  47.1 0.1 collective-permute-done.18.refs_3_
  47.2 0.9 %shard_map.51 = f32[256,512]{1,0:T(8,128)} custom-call(f32[256,128]{1,0:T(8,128)S(1)} %get-tuple-element.23.sigma_ref, f32[256,512]{1,0:T(8,128)S(1)} %get-tuple-element.37.refs_0_, bf16[256,512]{1,0:T(8,128)(2,1)S(1)} %collective-permute-done.16.refs_1_, bf16[256,512]{1,0:T(8,128)(2,1)S(1)} %collective-permute-done.17.refs_2_, ...), custom_call_target="tpu_custom_call" | custom-call | tf_op jit(solution)/shard_map/pallas_call | solution.py:115
Async XLA Ops:
  0.0 6.9 %copy-start = (bf16[256,512]{1,0:T(8,128)(2,1)S(1)}, bf16[256,512]{1,0:T(8,128)(2,1)}, u32[]{:S(2)}) copy-start(bf16[256,512]{1,0:T(8,128)(2,1)} %w_hbm.1) | copy-start | bytes 786436
  0.0 16.2 %collective-permute-start.5 = (bf16[256,512]{1,0:T(8,128)(2,1)}, bf16[256,512]{1,0:T(8,128)(2,1)S(1)}, u32[]{:S(2)}, u32[]{:S(2)}) collective-permute-start(bf16[256,512]{1,0:T(8,128)(2,1)} %w_hbm.1), channel_id=1, source_target_pairs={{0,4},{1,5},{2,6},{3,7},{4,0},{5,1},{6,2},{7,3},{8,12},{9,13},{10,... | collective-permute-start | bytes 786440 | tf_op jit(solution)/shard_map/ppermute | solution.py:143
  5.3 7.4 %collective-permute-start.1 = (bf16[256,256]{1,0:T(8,128)(2,1)S(1)}, bf16[256,256]{1,0:T(8,128)(2,1)S(1)}, u32[]{:S(2)}, u32[]{:S(2)}) collective-permute-start(bf16[256,256]{1,0:T(8,128)(2,1)S(1)} %get-tuple-element.24.refs_0_.refs_2_), channel_id=1, source_target_pairs={{0,2},{1,3},{2,0},{3,1},{4,6},{5,7},{6,4},{7,5},{8,10},{9,11},{10,... | collective-permute-start | bytes 393224 | tf_op jit(solution)/shard_map/ppermute | solution.py:143
  6.9 11.7 %collective-permute-start.7 = (bf16[256,512]{1,0:T(8,128)(2,1)S(1)}, bf16[256,512]{1,0:T(8,128)(2,1)S(1)}, u32[]{:S(2)}, u32[]{:S(2)}) collective-permute-start(bf16[256,512]{1,0:T(8,128)(2,1)S(1)} %copy-done), channel_id=1, source_target_pairs={{0,16},{1,17},{2,18},{3,19},{4,20},{5,21},{6,22},{7,23},{8,24},{9,... | collective-permute-start | bytes 786440 | tf_op jit(solution)/shard_map/ppermute | solution.py:143
  8.4 5.0 %collective-permute-start = (bf16[256,256]{1,0:T(8,128)(2,1)S(1)}, bf16[256,256]{1,0:T(8,128)(2,1)S(1)}, u32[]{:S(2)}, u32[]{:S(2)}) collective-permute-start(bf16[256,256]{1,0:T(8,128)(2,1)S(1)} %get-tuple-element.24.refs_0_.refs_2_), channel_id=1, source_target_pairs={{0,8},{1,9},{2,10},{3,11},{4,12},{5,13},{6,14},{7,15},{8,0},{9,1},... | collective-permute-start | bytes 393224 | tf_op jit(solution)/shard_map/ppermute | solution.py:143
  9.9 7.8 %collective-permute-start.9 = (bf16[256,256]{1,0:T(8,128)(2,1)S(1)}, bf16[256,256]{1,0:T(8,128)(2,1)S(1)}, u32[]{:S(2)}, u32[]{:S(2)}) collective-permute-start(bf16[256,256]{1,0:T(8,128)(2,1)S(1)} %get-tuple-element.24.refs_0_.refs_2_), channel_id=1, source_target_pairs={{0,16},{1,17},{2,18},{3,19},{4,20},{5,21},{6,22},{7,23},{8,24},{9,... | collective-permute-start | bytes 393224 | tf_op jit(solution)/shard_map/ppermute | solution.py:143
  12.7 13.0 %collective-permute-start.8 = (bf16[256,768]{1,0:T(8,128)(2,1)S(1)}, bf16[256,768]{1,0:T(8,128)(2,1)S(1)}, u32[]{:S(2)}, u32[]{:S(2)}) collective-permute-start(bf16[256,768]{1,0:T(8,128)(2,1)S(1)} %get-tuple-element.28.refs_4_), channel_id=1, source_target_pairs={{0,1},{1,0},{2,3},{3,2},{4,5},{5,4},{6,7},{7,6},{8,9},{9,8},{10,11... | collective-permute-start | bytes 1179656 | tf_op jit(solution)/shard_map/ppermute | solution.py:143
  13.4 9.0 %collective-permute-start.2 = (bf16[256,256]{1,0:T(8,128)(2,1)S(1)}, bf16[256,256]{1,0:T(8,128)(2,1)S(1)}, u32[]{:S(2)}, u32[]{:S(2)}) collective-permute-start(bf16[256,256]{1,0:T(8,128)(2,1)S(1)} %get-tuple-element.24.refs_0_.refs_2_), channel_id=1, source_target_pairs={{0,4},{1,5},{2,6},{3,7},{4,0},{5,1},{6,2},{7,3},{8,12},{9,13},{10,... | collective-permute-start | bytes 393224 | tf_op jit(solution)/shard_map/ppermute | solution.py:143
  16.2 8.3 %collective-permute-start.6 = (bf16[256,512]{1,0:T(8,128)(2,1)S(1)}, bf16[256,512]{1,0:T(8,128)(2,1)S(1)}, u32[]{:S(2)}, u32[]{:S(2)}) collective-permute-start(bf16[256,512]{1,0:T(8,128)(2,1)S(1)} %collective-permute-done.5.refs_5_), channel_id=1, source_target_pairs={{0,16},{1,17},{2,18},{3,19},{4,20},{5,21},{6,22},{7,23},{8,24},{9,... | collective-permute-start | bytes 786440 | tf_op jit(solution)/shard_map/ppermute | solution.py:143
  17.8 5.8 %collective-permute-start.3 = (bf16[256,256]{1,0:T(8,128)(2,1)S(1)}, bf16[256,256]{1,0:T(8,128)(2,1)S(1)}, u32[]{:S(2)}, u32[]{:S(2)}) collective-permute-start(bf16[256,256]{1,0:T(8,128)(2,1)S(1)} %collective-permute-done.refs_1_.refs_0_), channel_id=1, source_target_pairs={{0,2},{1,3},{2,0},{3,1},{4,6},{5,7},{6,4},{7,5},{8,10},{9,11},{10,... | collective-permute-start | bytes 393224 | tf_op jit(solution)/shard_map/ppermute | solution.py:143
  18.6 7.2 %collective-permute-start.11 = (bf16[256,512]{1,0:T(8,128)(2,1)S(1)}, bf16[256,512]{1,0:T(8,128)(2,1)S(1)}, u32[]{:S(2)}, u32[]{:S(2)}) collective-permute-start(bf16[256,512]{1,0:T(8,128)(2,1)S(1)} %collective-permute-done.7.refs_7_), channel_id=1, source_target_pairs={{0,1},{1,0},{2,3},{3,2},{4,5},{5,4},{6,7},{7,6},{8,9},{9,8},{10,11... | collective-permute-start | bytes 786440 | tf_op jit(solution)/shard_map/ppermute | solution.py:143
  22.4 2.1 %collective-permute-start.10 = (bf16[256,256]{1,0:T(8,128)(2,1)S(1)}, bf16[256,256]{1,0:T(8,128)(2,1)S(1)}, u32[]{:S(2)}, u32[]{:S(2)}) collective-permute-start(bf16[256,256]{1,0:T(8,128)(2,1)S(1)} %collective-permute-done.9.refs_6_), channel_id=1, source_target_pairs={{0,1},{1,0},{2,3},{3,2},{4,5},{5,4},{6,7},{7,6},{8,9},{9,8},{10,11... | collective-permute-start | bytes 393224 | tf_op jit(solution)/shard_map/ppermute | solution.py:143
  23.5 5.4 %collective-permute-start.4 = (bf16[256,256]{1,0:T(8,128)(2,1)S(1)}, bf16[256,256]{1,0:T(8,128)(2,1)S(1)}, u32[]{:S(2)}, u32[]{:S(2)}) collective-permute-start(bf16[256,256]{1,0:T(8,128)(2,1)S(1)} %collective-permute-done.2.refs_4_), channel_id=1, source_target_pairs={{0,16},{1,17},{2,18},{3,19},{4,20},{5,21},{6,22},{7,23},{8,24},{9,... | collective-permute-start | bytes 393224 | tf_op jit(solution)/shard_map/ppermute | solution.py:143
  24.5 5.0 %collective-permute-start.15 = (bf16[256,512]{1,0:T(8,128)(2,1)S(1)}, bf16[256,512]{1,0:T(8,128)(2,1)S(1)}, u32[]{:S(2)}, u32[]{:S(2)}) collective-permute-start(bf16[256,512]{1,0:T(8,128)(2,1)S(1)} %collective-permute-done.5.refs_5_), channel_id=1, source_target_pairs={{0,1},{1,0},{2,3},{3,2},{4,5},{5,4},{6,7},{7,6},{8,9},{9,8},{10,11... | collective-permute-start | bytes 786440 | tf_op jit(solution)/shard_map/ppermute | solution.py:143
  24.5 7.0 %collective-permute-start.13 = (bf16[256,512]{1,0:T(8,128)(2,1)S(1)}, bf16[256,512]{1,0:T(8,128)(2,1)S(1)}, u32[]{:S(2)}, u32[]{:S(2)}) collective-permute-start(bf16[256,512]{1,0:T(8,128)(2,1)S(1)} %collective-permute-done.6.refs_4_.refs_2_), channel_id=1, source_target_pairs={{0,1},{1,0},{2,3},{3,2},{4,5},{5,4},{6,7},{7,6},{8,9},{9,8},{10,11... | collective-permute-start | bytes 786440 | tf_op jit(solution)/shard_map/ppermute | solution.py:143
  25.7 3.8 %collective-permute-start.14 = (bf16[256,256]{1,0:T(8,128)(2,1)S(1)}, bf16[256,256]{1,0:T(8,128)(2,1)S(1)}, u32[]{:S(2)}, u32[]{:S(2)}) collective-permute-start(bf16[256,256]{1,0:T(8,128)(2,1)S(1)} %collective-permute-done.2.refs_4_), channel_id=1, source_target_pairs={{0,1},{1,0},{2,3},{3,2},{4,5},{5,4},{6,7},{7,6},{8,9},{9,8},{10,11... | collective-permute-start | bytes 393224 | tf_op jit(solution)/shard_map/ppermute | solution.py:143
  28.9 2.6 %collective-permute-start.12 = (bf16[256,256]{1,0:T(8,128)(2,1)S(1)}, bf16[256,256]{1,0:T(8,128)(2,1)S(1)}, u32[]{:S(2)}, u32[]{:S(2)}) collective-permute-start(bf16[256,256]{1,0:T(8,128)(2,1)S(1)} %collective-permute-done.4.refs_3_.refs_1_), channel_id=1, source_target_pairs={{0,1},{1,0},{2,3},{3,2},{4,5},{5,4},{6,7},{7,6},{8,9},{9,8},{10,11... | collective-permute-start | bytes 393224 | tf_op jit(solution)/shard_map/ppermute | solution.py:143
  32.2 10.2 %collective-permute-start.16 = (bf16[256,512]{1,0:T(8,128)(2,1)S(1)}, bf16[256,512]{1,0:T(8,128)(2,1)S(1)}, u32[]{:S(2)}, u32[]{:S(2)}) collective-permute-start(bf16[256,512]{1,0:T(8,128)(2,1)S(1)} %shard_map.50), channel_id=1, source_target_pairs={{0,10},{1,11},{2,8},{3,9},{4,14},{5,15},{6,12},{7,13},{8,2},{9,3},... | collective-permute-start | bytes 786440 | tf_op jit(solution)/shard_map/ppermute | solution.py:143
  35.5 11.6 %collective-permute-start.17 = (bf16[256,512]{1,0:T(8,128)(2,1)S(1)}, bf16[256,512]{1,0:T(8,128)(2,1)S(1)}, u32[]{:S(2)}, u32[]{:S(2)}) collective-permute-start(bf16[256,512]{1,0:T(8,128)(2,1)S(1)} %get-tuple-element.39), channel_id=1, source_target_pairs={{0,8},{1,9},{2,10},{3,11},{4,12},{5,13},{6,14},{7,15},{8,0},{9,1},... | collective-permute-start | bytes 786440 | tf_op jit(solution)/shard_map/ppermute | solution.py:143
  36.1 11.1 %collective-permute-start.18 = (bf16[256,512]{1,0:T(8,128)(2,1)S(1)}, bf16[256,512]{1,0:T(8,128)(2,1)S(1)}, u32[]{:S(2)}, u32[]{:S(2)}) collective-permute-start(bf16[256,512]{1,0:T(8,128)(2,1)S(1)} %get-tuple-element.40), channel_id=1, source_target_pairs={{0,2},{1,3},{2,0},{3,1},{4,6},{5,7},{6,4},{7,5},{8,10},{9,11},{10,... | collective-permute-start | bytes 786440 | tf_op jit(solution)/shard_map/ppermute | solution.py:143
